TPU v7x, 32 devices: a whole 2x2x4 slice. The times are simulated.
32 devices in a mesh: grp: 2 (over x), ex: 4 (over y, core), qry: 4 (over z).
Axes of the slice: x: 2, y: 2, z: 4, core: 2. Of those that a mesh axis runs over, the one named last changes fastest.
Arguments:
- hidden: bfloat16 [8192, 14336], P(('grp', 'ex', 'qry')), parts along dimension 0, may hold values from -6 to 6
- out_grad: bfloat16 [8192, 4096], P(('grp', 'ex', 'qry')), parts along dimension 0, may hold values from -6 to 6
- proj_in: bfloat16 [32, 14336], replicated, may hold values from -0.046875 to 0.046875
- proj_out: bfloat16 [32, 4096], replicated, may hold values from -0.09375 to 0.09375
- lengths: int32 [32, 9], P(('grp', 'ex', 'qry')), parts along dimension 0, may hold values from 1 to 64, 256 in all within a row
- queries: bfloat16 [4096, 1024], P(('grp', 'qry'), 'ex'), parts along dimension 0, may hold values from -6 to 6
Outputs:
- scores: float32 [256, 2048], P(('grp', 'ex'), 'qry'), parts along dimension 0
There are 2 independent parts, one for each index of `grp`. A program takes and returns all parts, laid end to end along the dimension named above; an argument that names none is the same for every part. Nothing has to cross between parts.
Inputs may be any that keep to these rules, and one draw needn't show every extreme that they name: `lengths`: in every row the first 8 entries are example token counts and the last the padding count; each row sums to 256 and its largest entry is 64.
All inputs are finite; a program needn't handle non-finite values.
Results may differ from a plain program's by a relative error of at most 0.0003.
Values may be sent and summed in bfloat16 or wider, within the bound.
No kernel may reach another device: no remote copies, remote signals or barrier semaphores. Data moves between devices by JAX's collectives and lax.ppermute only.
A program may use at most 128 MiB of HBM per device.

v0:
```python
import jax
import jax.numpy as jnp
from jax import lax
from jax.sharding import PartitionSpec as P


def inverse_apply(factor, right):
    middle = lax.linalg.triangular_solve(factor, right, left_side=True, lower=True)
    return lax.linalg.triangular_solve(factor, middle, left_side=True, lower=True, transpose_a=True)


def body(hidden, out_grad, proj_in, proj_out, lengths, queries):
    rank = proj_in.shape[0]
    width = rank * rank
    tok_rows = hidden.shape[0]
    examples_here = lengths.shape[1] - 1
    side_in = lax.dot_general(
        hidden, proj_in, (((1,), (1,)), ((), ())), preferred_element_type=jnp.float32
    )
    side_out = lax.dot_general(
        out_grad, proj_out, (((1,), (1,)), ((), ())), preferred_element_type=jnp.float32
    )
    outer = (side_out[:, :, None] * side_in[:, None, :]).reshape(tok_rows, width)
    counts = lengths[0, :examples_here]
    ends = jnp.cumsum(counts)
    starts = ends - counts
    places = jnp.arange(tok_rows, dtype=jnp.int32)
    member = ((places[None, :] >= starts[:, None]) & (places[None, :] < ends[:, None])).astype(
        jnp.float32
    )
    vectors = jnp.dot(member, outer, precision=lax.Precision.HIGHEST)
    total_examples = examples_here * lax.axis_size("ex") * lax.axis_size("qry")
    partial_fisher = jnp.dot(vectors.T, vectors, precision=lax.Precision.HIGHEST)
    fisher = lax.psum(partial_fisher, ("ex", "qry")) / total_examples
    row_block = lax.all_gather(vectors, "qry", axis=0, tiled=True)
    damp = 0.1 * jnp.trace(fisher) / width + 1e-05
    fisher = fisher + damp * jnp.eye(width, dtype=jnp.float32)
    factor = jnp.linalg.cholesky(fisher)
    weighted = inverse_apply(factor, row_block.T).T
    empty = jnp.zeros((row_block.shape[0], queries.shape[0]), jnp.float32)
    return empty + lax.dot_general(
        weighted,
        lax.all_gather(queries, "ex", axis=1, tiled=True).astype(jnp.float32),
        (((1,), (1,)), ((), ())),
        precision=lax.Precision.HIGHEST,
    )


def solution(mesh):
    placed = (
        P(("grp", "ex", "qry"), None),
        P(("grp", "ex", "qry"), None),
        P(),
        P(),
        P(("grp", "ex", "qry"), None),
        P(("grp", "qry"), "ex"),
    )
    return jax.shard_map(
        body, mesh=mesh, in_specs=placed, out_specs=P(("grp", "ex"), "qry"), check_vma=False
    )
```

profile of v0, /device:TPU:0, one launch (start us, length us, event | category | flops | bytes accessed | tf_op | source)
XLA Modules:
  0.0 509.2 jit_solution(5745467749486583503)
XLA Ops:
  9.0 5.6 %fusion.101 = f32[256,32]{0,1:T(8,128)S(1)} fusion(bf16[256,14336]{1,0:T(8,128)(2,1)} %param.6, bf16[32,14336]{1,0:T(8,128)(2,1)} %param.8), kind=kOutput, calls=%fused_computation.226 | convolution fusion | flops 234881024 | bytes 8290304 | tf_op jit(solution)/shard_map/dot_general | solution.py:17
  16.1 5.0 fusion.102
  21.7 16.4 %all_gather.6 = f32[32,1024]{1,0:T(8,128)} all-gather(f32[8,1024]{1,0:T(8,128)S(1)} %fusion.89), channel_id=1, replica_groups=mesh['grp'=2,'ex'=4,'qry'=4] {'qry'}, dimensions={0}, use_global_device_ids=true | all-gather | bytes 163840 | tf_op jit(solution)/shard_map/all_gather | solution.py:35
  38.2 98.8 %all-reduce.3.cloned.1.call-done = f32[1024,1024]{0,1:T(8,128)} async-done(((f32[1024,1024]{0,1:T(8,128)}), f32[1024,1024]{0,1:T(8,128)}) %all-reduce.3.cloned.1.call-update) | async-done | bytes 4194320 | tf_op jit(solution)/shard_map/psum | solution.py:34
  137.0 2.9 select_reduce_fusion
  140.5 5.0 select_add_fusion
  145.6 5.5 %copy.28 = f32[1024,1024]{1,0:T(8,128)} copy(f32[1024,1024]{0,1:T(8,128)} %select_add_fusion) | data formatting | bytes 8388608 | tf_op jit(solution)/shard_map/add | solution.py:37
  151.1 4.5 fusion
  155.5 1.9 copy-done.2
  157.5 11.7 %cholesky.222 = f32[128,128]{1,0:T(8,128)S(1)} custom-call(f32[128,128]{1,0:T(8,128)S(1)} %cholesky.577), custom_call_target="Cholesky" | custom-call | tf_op jit(solution)/shard_map/jit(cholesky)/cholesky | solution.py:38
  169.3 9.8 %custom-call.64 = f32[1,128,128]{1,2,0:T(8,128)S(1)} custom-call(f32[1,128,128]{2,1,0:T(8,128)S(1)} %get-tuple-element.44), custom_call_target="InvertDiagBlocksLowerTriangular" | custom-call | tf_op jit(solution)/shard_map/jit(cholesky)/cholesky | solution.py:38
  179.1 1.5 fusion.9
  180.9 1.6 convolution_subtract_fusion
  182.4 11.7 %cholesky.243 = f32[128,128]{1,0:T(8,128)S(1)} custom-call(f32[128,128]{1,0:T(8,128)S(1)} %cholesky.581), custom_call_target="Cholesky" | custom-call | tf_op jit(solution)/shard_map/jit(cholesky)/cholesky | solution.py:38
  194.5 9.8 %custom-call.65 = f32[1,128,128]{1,2,0:T(8,128)S(1)} custom-call(f32[1,128,128]{2,1,0:T(8,128)S(1)} %get-tuple-element.42), custom_call_target="InvertDiagBlocksLowerTriangular" | custom-call | tf_op jit(solution)/shard_map/jit(cholesky)/cholesky | solution.py:38
  205.4 2.0 copy-done.1
  207.4 2.4 convolution_subtract_fusion.1
  209.8 11.7 %cholesky.466 = f32[128,128]{1,0:T(8,128)S(1)} custom-call(f32[128,128]{1,0:T(8,128)S(1)} %cholesky.586), custom_call_target="Cholesky" | custom-call | tf_op jit(solution)/shard_map/jit(cholesky)/cholesky | solution.py:38
  222.3 9.8 %custom-call.66 = f32[1,128,128]{1,2,0:T(8,128)S(1)} custom-call(f32[1,128,128]{2,1,0:T(8,128)S(1)} %get-tuple-element.40), custom_call_target="InvertDiagBlocksLowerTriangular" | custom-call | tf_op jit(solution)/shard_map/jit(cholesky)/cholesky | solution.py:38
  232.1 1.3 convolution_dynamic-update-slice_fusion.1
  233.4 3.5 convolution_subtract_fusion.2
  236.9 11.7 %cholesky.485 = f32[128,128]{1,0:T(8,128)S(1)} custom-call(f32[128,128]{1,0:T(8,128)S(1)} %cholesky.591), custom_call_target="Cholesky" | custom-call | tf_op jit(solution)/shard_map/jit(cholesky)/cholesky | solution.py:38
  249.4 9.8 %custom-call.67 = f32[1,128,128]{1,2,0:T(8,128)S(1)} custom-call(f32[1,128,128]{2,1,0:T(8,128)S(1)} %get-tuple-element.38), custom_call_target="InvertDiagBlocksLowerTriangular" | custom-call | tf_op jit(solution)/shard_map/jit(cholesky)/cholesky | solution.py:38
  259.2 1.1 convolution_dynamic-update-slice_fusion.2
  260.4 3.2 convolution_subtract_fusion.3
  263.5 11.9 %cholesky.504 = f32[128,128]{1,0:T(8,128)S(1)} custom-call(f32[128,128]{1,0:T(8,128)S(1)} %cholesky.596), custom_call_target="Cholesky" | custom-call | tf_op jit(solution)/shard_map/jit(cholesky)/cholesky | solution.py:38
  276.2 9.8 %custom-call.68 = f32[1,128,128]{1,2,0:T(8,128)S(1)} custom-call(f32[1,128,128]{2,1,0:T(8,128)S(1)} %get-tuple-element.36), custom_call_target="InvertDiagBlocksLowerTriangular" | custom-call | tf_op jit(solution)/shard_map/jit(cholesky)/cholesky | solution.py:38
  286.0 1.1 convolution_dynamic-update-slice_fusion.3
  287.1 3.1 convolution_subtract_fusion.4
  290.2 11.7 %cholesky.524 = f32[128,128]{1,0:T(8,128)S(1)} custom-call(f32[128,128]{1,0:T(8,128)S(1)} %cholesky.601), custom_call_target="Cholesky" | custom-call | tf_op jit(solution)/shard_map/jit(cholesky)/cholesky | solution.py:38
  302.7 9.8 %custom-call.69 = f32[1,128,128]{1,2,0:T(8,128)S(1)} custom-call(f32[1,128,128]{2,1,0:T(8,128)S(1)} %get-tuple-element.34), custom_call_target="InvertDiagBlocksLowerTriangular" | custom-call | tf_op jit(solution)/shard_map/jit(cholesky)/cholesky | solution.py:38
  312.5 1.0 convolution_dynamic-update-slice_fusion.4
  313.5 2.9 convolution_subtract_fusion.5
  316.4 11.7 %cholesky.544 = f32[128,128]{1,0:T(8,128)S(1)} custom-call(f32[128,128]{1,0:T(8,128)S(1)} %cholesky.606), custom_call_target="Cholesky" | custom-call | tf_op jit(solution)/shard_map/jit(cholesky)/cholesky | solution.py:38
  328.9 9.8 %custom-call.70 = f32[1,128,128]{1,2,0:T(8,128)S(1)} custom-call(f32[1,128,128]{2,1,0:T(8,128)S(1)} %get-tuple-element.32), custom_call_target="InvertDiagBlocksLowerTriangular" | custom-call | tf_op jit(solution)/shard_map/jit(cholesky)/cholesky | solution.py:38
  338.7 0.9 convolution_dynamic-update-slice_fusion.5
  339.6 2.1 convolution_subtract_fusion.6
  341.7 11.7 %cholesky.562 = f32[128,128]{1,0:T(8,128)S(1)} custom-call(f32[128,128]{1,0:T(8,128)S(1)} %convolution_subtract_fusion.6), custom_call_target="Cholesky" | custom-call | tf_op jit(solution)/shard_map/jit(cholesky)/cholesky | solution.py:38
  363.9 4.9 select_select_fusion
  368.8 28.5 %while.1 = (s32[]{:T(128)}, f32[1024,1024]{0,1:T(8,128)}, s32[8,2]{0,1:T(2,128)S(1)}, f32[8,128,128]{2,1,0:T(8,128)}, s32[]{:T(128)}) while((s32[]{:T(128)}, f32[1024,1024]{0,1:T(8,128)}, s32[8,2]{0,1:T(2,128)S(1)}, f32[8,128,128]{2,1,0:T(8,128)}, s32[]{:T(128)}) %tuple.50), condition=%wide.while_cond, body=%wide.while_body.sunk | while | flops 2 | bytes 393329 | solution.py:9
  369.4 2.2 dynamic-slice.7
  373.0 2.2 dynamic-slice.7
  376.5 2.2 dynamic-slice.7
  380.1 2.2 dynamic-slice.7
  383.7 2.2 dynamic-slice.7
  387.3 2.2 dynamic-slice.7
  390.8 2.2 dynamic-slice.7
  394.4 2.2 dynamic-slice.7
  397.3 79.6 %custom-call.71 = f32[8,128,128]{1,2,0:T(8,128)S(1)} custom-call(f32[8,128,128]{2,1,0:T(8,128)} %get-tuple-element.12), custom_call_target="InvertDiagBlocksLowerTriangular" | custom-call | tf_op jit(solution)/shard_map/triangular_solve | solution.py:9
  477.1 1.0 convolution_subtract_fusion.14
  478.3 1.1 convolution_subtract_fusion.13
  479.6 1.2 convolution_subtract_fusion.12
  480.9 1.2 convolution_subtract_fusion.11
  482.3 1.3 convolution_subtract_fusion.20
  483.8 1.3 convolution_subtract_fusion.19
  485.3 1.4 convolution_subtract_fusion.18
  487.2 1.1 convolution_subtract_fusion.10
  488.5 1.2 convolution_subtract_fusion.9
  489.9 1.3 convolution_subtract_fusion.8
  491.4 1.3 convolution_subtract_fusion.7
  493.0 1.4 convolution_subtract_fusion.17
  494.7 1.5 convolution_subtract_fusion.16
  496.5 1.6 convolution_subtract_fusion.15
  498.4 2.9 fusion.103
  (133 shorter events, 28.7 us)
Async XLA Ops:
  7.4 7.3 %copy-start = (bf16[256,4096]{1,0:T(8,128)(2,1)S(1)}, bf16[256,4096]{1,0:T(8,128)(2,1)}, u32[]{:S(2)}) copy-start(bf16[256,4096]{1,0:T(8,128)(2,1)} %param.7) | copy-start | bytes 6291460
  7.4 7.3 %copy-start.4 = (bf16[32,4096]{1,0:T(8,128)(2,1)S(1)}, bf16[32,4096]{1,0:T(8,128)(2,1)}, u32[]{:S(2)}) copy-start(bf16[32,4096]{1,0:T(8,128)(2,1)} %param.9) | copy-start | bytes 786436
  7.4 129.6 %all-reduce.3.cloned.1.call-start = ((), (), s32[]{:S(2)}) async-start(), calls=%async_computation | async-start | bytes 8388608 | tf_op jit(solution)/shard_map/psum | solution.py:34
  21.2 477.2 %all-gather.2.cloned.1.call-start = ((), (), s32[]{:S(2)}) async-start(), calls=%async_computation.1 | async-start | bytes 1310720 | tf_op jit(solution)/shard_map/all_gather | solution.py:43
  155.5 1.9 copy-start.2
  205.4 2.0 copy-start.1
  363.9 113.0 %copy-start.3 = (f32[32,1024]{1,0:T(8,128)S(1)}, f32[32,1024]{1,0:T(8,128)}, u32[]{:S(2)}) copy-start(f32[32,1024]{1,0:T(8,128)} %all_gather.6) | copy-start | bytes 393220
Sparse Core Ops, SparseCore 0:
  21.3 115.6 all-reduce.2
Sparse Core Ops, SparseCore 1:
  23.3 19.7 all-gather.1
where the time goes:
time: 515 us; the launch traced here: 509 us
  other arithmetic  265 us (51%)
  waiting for transfers between devices  99.3 us (19%)
  matrix products  61.8 us (12%)
  local copies, waits for them, and re-layouts  44.3 us (9%)
  between operations  21.7 us (4%)
  blocking collectives  16.4 us (3%)
    another operation x30, other arithmetic, body(): factor = jnp.linalg.cholesky(fisher)  167 us
    psum x1, waiting for transfers between devices, body(): fisher = lax.psum(partial_fisher, ('ex', 'qry')) / total_examples  98.8 us
    another operation x3, other arithmetic, inverse_apply(): lax.linalg.triangular_solve(factor, middle, left_side=True, lower=True, t...  84.5 us
    another operation x41, local copies, waits for them, and re-layouts  29.2 us
    another operation x14, matrix products, body(): factor = jnp.linalg.cholesky(fisher)  26.1 us
    all_gather x1, blocking collectives, body(): row_block = lax.all_gather(vectors, 'qry', axis=0, tiled=True)  16.4 us
    another operation x15, matrix products, inverse_apply(): lax.linalg.triangular_solve(factor, middle, left_side=True, lower=True, t...  10.9 us
  transfers between devices with their start and end apart: 2, of which 1 were waited for; matrix products, arithmetic and copies ran while one was open for 69% of the time, Pallas kernels for 0%

commit v1 on v0

v1 whole, which is shorter than its diff:
```python
import jax
import jax.numpy as jnp
from jax import lax
from jax.experimental import pallas as pl
from jax.experimental.pallas import tpu as pltpu
from jax.sharding import PartitionSpec as P

HIGHEST = lax.Precision.HIGHEST
F32 = jnp.float32
BF16 = jnp.bfloat16
NT = (((1,), (1,)), ((), ()))
NN = (((1,), (0,)), ((), ()))


def dot(a, b, dims=NN, precision=None):
    return lax.dot_general(a, b, dims, precision=precision, preferred_element_type=F32)


def split2(x):
    hi = x.astype(BF16)
    return hi, (x - hi.astype(F32)).astype(BF16)


def split3(x):
    hi = x.astype(BF16)
    rest = x - hi.astype(F32)
    mid = rest.astype(BF16)
    return hi, mid, (rest - mid.astype(F32)).astype(BF16)


def vectors_kernel(lengths, hidden, out_grad, proj_in, proj_out, vectors, side_in, side_out, stacked):
    step = pl.program_id(0)
    part_in = dot(proj_in[...], hidden[...], NT)
    part_out = dot(proj_out[...], out_grad[...], NT)

    @pl.when(step == 0)
    def _():
        side_in[...] = part_in
        side_out[...] = part_out

    @pl.when(step > 0)
    def _():
        side_in[...] += part_in
        side_out[...] += part_out

    @pl.when(step == pl.num_programs(0) - 1)
    def _():
        rank, tokens = side_in.shape
        examples = lengths.shape[1] - 1
        place = lax.broadcasted_iota(jnp.int32, (1, tokens), 1)
        outs = side_out[...]
        rows = []
        start = jnp.int32(0)
        for e in range(examples):
            end = start + lengths[0, e]
            inside = (place >= start) & (place < end)
            rows.append(jnp.where(inside, outs, 0.0))
            start = end
        masked = jnp.concatenate(rows, axis=0)
        stacked[:, :rank] = dot(masked, side_in[...], NT, HIGHEST)
        per = 128 // rank
        lane = lax.broadcasted_iota(jnp.int32, (examples, 128), 1) // rank
        for block in range(rank // per):
            total = None
            for k in range(per):
                piece = stacked[pl.ds(block * per + k, examples, stride=rank), :]
                if k:
                    piece = jnp.where(lane == k, pltpu.roll(piece, k * rank, axis=1), total)
                total = piece
            vectors[:, block * 128:(block + 1) * 128] = total


def example_vectors(hidden, out_grad, proj_in, proj_out, lengths):
    rank, features = proj_in.shape
    width_out = proj_out.shape[1]
    tokens = hidden.shape[0]
    examples = lengths.shape[1] - 1
    steps = 8
    kin, kout = features // steps, width_out // steps
    return pl.pallas_call(
        vectors_kernel,
        grid=(steps,),
        in_specs=[
            pl.BlockSpec(memory_space=pltpu.SMEM),
            pl.BlockSpec((tokens, kin), lambda i: (0, i)),
            pl.BlockSpec((tokens, kout), lambda i: (0, i)),
            pl.BlockSpec((rank, kin), lambda i: (0, i)),
            pl.BlockSpec((rank, kout), lambda i: (0, i)),
        ],
        out_specs=pl.BlockSpec((examples, rank * rank), lambda i: (0, 0)),
        out_shape=jax.ShapeDtypeStruct((examples, rank * rank), F32),
        scratch_shapes=[
            pltpu.VMEM((rank, tokens), F32),
            pltpu.VMEM((rank, tokens), F32),
            pltpu.VMEM((rank * examples, 128), F32),
        ],
        compiler_params=pltpu.CompilerParams(vmem_limit_bytes=24 * 2**20),
        cost_estimate=pl.CostEstimate(
            flops=2 * tokens * rank * (features + width_out),
            bytes_accessed=2 * (tokens + rank) * (features + width_out),
            transcendentals=0,
        ),
    )(lengths, hidden, out_grad, proj_in, proj_out)


def times(a, b):
    ah, am = split2(a)
    bh, bm = split2(b)
    left = jnp.concatenate([ah, am], axis=1)
    right = jnp.concatenate(
        [jnp.concatenate([bh, bm], axis=1), jnp.concatenate([bh, jnp.zeros_like(bm)], axis=1)], axis=0
    )
    both = dot(left, right)
    n = b.shape[1]
    return both[:, :n] + both[:, n:]


def scores_kernel(near, far, q0, q1, q2, q3, out, total, width):
    ex, qry = lax.axis_index("ex"), lax.axis_index("qry")
    block = q0.shape[1]
    n = total
    halves = (near, far)
    vec = jnp.concatenate([near[...], far[...]], axis=0)
    vh, vm, vl = split3(vec)
    gram = dot(vh, vh, NT) + ((dot(vh, vm, NT) + dot(vm, vh, NT)) + (dot(vm, vm, NT) + dot(vh, vl, NT) + dot(vl, vh, NT)))
    gram = gram / n
    row = lax.broadcasted_iota(jnp.int32, (n, n), 0)
    col = lax.broadcasted_iota(jnp.int32, (n, n), 1)
    eye = jnp.where(row == col, 1.0, 0.0).astype(F32)
    diag = gram * eye
    diag_row = jnp.sum(diag, axis=0, keepdims=True)
    diag_col = jnp.sum(diag, axis=1, keepdims=True)
    damp = 0.1 * jnp.sum(diag_row, axis=1, keepdims=True) / width + 1e-05
    root_row = lax.rsqrt(diag_row + damp)
    root_col = lax.rsqrt(diag_col + damp)
    system = (gram + damp * eye) * root_row * root_col
    size = jnp.max(jnp.sum(jnp.abs(system), axis=0, keepdims=True), axis=1, keepdims=True)
    inv_size = 1.0 / (0.51 * size)
    power = eye - system * inv_size
    series = eye + power
    power = times(power, power)
    for k in range(4):
        both = times(jnp.concatenate([series, power], axis=0), power)
        series = series + both[:n]
        power = both[n:]
    series = series + times(series, power)
    inverse = series * inv_size

    def refine(x):
        error = eye - dot(system, x, NN, HIGHEST)
        return x + times(x, error), jnp.max(jnp.abs(error))

    inverse, miss = refine(inverse)

    def again(state):
        x, _, turns = state
        x, left = refine(x)
        return x, left, turns + 1

    inverse, _, _ = lax.while_loop(
        lambda s: (s[1] > 1e-4) & (s[2] < 16), again, (inverse, miss, jnp.int32(0))
    )

    cross = None
    for k, q in enumerate((q0, q1, q2, q3)):
        start = pl.multiple_of((ex ^ k) * block, block)
        here = jnp.concatenate([h[:, pl.ds(start, block)] for h in halves], axis=0)
        hh, hm, hl = split3(here)
        qb = q[...]
        term = dot(hh, qb, NT) + dot(hm, qb, NT) + dot(hl, qb, NT)
        cross = term if cross is None else cross + term
    groups = lax.axis_size("qry")
    mine = out.shape[0]
    each = mine // groups
    weights = inverse[:mine] * root_row * root_col[:mine]
    result = dot(weights, cross, NN, HIGHEST)
    for g in range(groups):
        to = pl.multiple_of((qry ^ g) * each, each)
        out[pl.ds(to, each), :] = result[g * each:(g + 1) * each]


def swap(x, axis, bit):
    size = lax.axis_size(axis)
    return lax.ppermute(x, axis, [(i, i ^ bit) for i in range(size)])


def doubled(x, axis, bit):
    return jnp.concatenate([x, swap(x, axis, bit)], axis=0)


def body_small(hidden, out_grad, proj_in, proj_out, lengths, queries):
    width = proj_in.shape[0] * proj_in.shape[0]
    q1 = swap(queries, "ex", 1)
    q2 = swap(queries, "ex", 2)
    vectors = example_vectors(hidden, out_grad, proj_in, proj_out, lengths)
    vectors = doubled(vectors, "qry", 1)
    vectors = doubled(vectors, "qry", 2)
    q3 = swap(q2, "ex", 1)
    vectors = doubled(vectors, "ex", 2)
    far = swap(vectors, "ex", 1)
    total = 2 * vectors.shape[0]
    mine = total // lax.axis_size("ex")
    count = queries.shape[0]
    return pl.pallas_call(
        lambda *refs: scores_kernel(*refs, total=total, width=width),
        out_shape=jax.ShapeDtypeStruct((mine, count), F32),
        in_specs=[pl.BlockSpec(memory_space=pltpu.VMEM)] * 6,
        out_specs=pl.BlockSpec(memory_space=pltpu.VMEM),
        compiler_params=pltpu.CompilerParams(vmem_limit_bytes=24 * 2**20),
    )(vectors, far, queries, q1, q2, q3)


def body_large(hidden, out_grad, proj_in, proj_out, lengths, queries):
    width = proj_in.shape[0] * proj_in.shape[0]
    vectors = example_vectors(hidden, out_grad, proj_in, proj_out, lengths)
    every = lax.all_gather(vectors, ("ex", "qry"), axis=0, tiled=True)
    total = every.shape[0]
    gram = lax.dot_general(every, every, NT, precision=HIGHEST) / total
    damp = 0.1 * jnp.trace(gram) / width + 1e-05
    factor = jnp.linalg.cholesky(gram + damp * jnp.eye(total, dtype=F32))
    mine = total // lax.axis_size("ex")
    pick = jnp.eye(total, dtype=F32)
    own = lax.dynamic_slice_in_dim(pick, lax.axis_index("ex") * mine, mine, axis=1)
    middle = lax.linalg.triangular_solve(factor, own, left_side=True, lower=True)
    solved = lax.linalg.triangular_solve(factor, middle, left_side=True, lower=True, transpose_a=True)
    weighted = lax.dot_general(solved, every, (((0,), (0,)), ((), ())), precision=HIGHEST)
    features = lax.all_gather(queries, "ex", axis=1, tiled=True).astype(F32)
    return lax.dot_general(weighted, features, NT, precision=HIGHEST)


def solution(mesh):
    placed = (
        P(("grp", "ex", "qry"), None),
        P(("grp", "ex", "qry"), None),
        P(),
        P(),
        P(("grp", "ex", "qry"), None),
        P(("grp", "qry"), "ex"),
    )
    small = mesh.shape["ex"] == 4 and mesh.shape["qry"] == 4
    return jax.shard_map(
        body_small if small else body_large,
        mesh=mesh,
        in_specs=placed,
        out_specs=P(("grp", "ex"), "qry"),
        check_vma=False,
    )
```

time: 515 us -> 37.5 us (0.07); the launches traced: 509 us -> 37.2 us
  other arithmetic: 265 us -> 0.03 us
  waiting for transfers between devices: 99.3 us -> 9.27 us
  matrix products: 61.8 us -> 0 us
  local copies, waits for them, and re-layouts: 44.3 us -> 7.46 us
  between operations: 21.7 us -> 0.05 us
  blocking collectives: 16.4 us -> 0 us
  Pallas kernels: 0 us -> 10.3 us
  starting transfers between devices: 0.05 us -> 10.1 us
    another operation x34 -> x0, other arithmetic: 252 us -> none  [the longest x30 167 us: body(): factor = jnp.linalg.cholesky(fisher)]
    psum x1 -> x0, waiting for transfers between devices: 98.8 us -> none  [body(): fisher = lax.psum(partial_fisher, ('ex', 'qry')) / total_examples]
    another operation x44 -> x0, matrix products: 47 us -> none  [the longest x14 26.1 us: body(): factor = jnp.linalg.cholesky(fisher)]
    another operation x71 -> x0, local copies, waits for them, and re-layouts: 34.8 us -> none
    all_gather x1 -> x0, blocking collectives: 16.4 us -> none  [body(): row_block = lax.all_gather(vectors, 'qry', axis=0, tiled=True)]
    dot_general x5 -> x0, matrix products: 14.8 us -> none  [the longest x1 5.6 us: body(): lax.dot_general(hidden, proj_in, (((1,), (1,)), ((), ())), preferred_elem...]
    pallas_call x0 -> x2, Pallas kernels: none -> 10.3 us  [the longest x1 5.76 us: example_vectors(): pl.pallas_call(vectors_kernel, grid=(steps,), in_specs=[pl.BlockSpec(memo...]
    ppermute x0 -> x7, starting transfers between devices: none -> 10.1 us  [swap(): return lax.ppermute(x, axis, [(i, i ^ bit) for i in range(size)])]
  transfers between devices with their start and end apart: 2 -> 7, of which waited for: 1 -> 5; matrix products, arithmetic and copies ran while one was open for 69% -> 0% of each run, Pallas kernels for 0% -> 0%
where the time goes in v1:
time: 37.5 us; the launch traced here: 37.2 us
  Pallas kernels  10.3 us (27%)
  starting transfers between devices  10.1 us (27%)
  waiting for transfers between devices  9.27 us (25%)
  local copies, waits for them, and re-layouts  7.46 us (20%)
    ppermute x7, starting transfers between devices, swap(): return lax.ppermute(x, axis, [(i, i ^ bit) for i in range(size)])  10.1 us
    ppermute x7, waiting for transfers between devices, swap(): return lax.ppermute(x, axis, [(i, i ^ bit) for i in range(size)])  9.27 us
    unnamed x12, local copies, waits for them, and re-layouts  7.46 us
    pallas_call x1, Pallas kernels, example_vectors(): pl.pallas_call(vectors_kernel, grid=(steps,), in_specs=[pl.BlockSpec(memo...  5.76 us
    pallas_call x1, Pallas kernels, body_small(): pl.pallas_call(lambda *refs: scores_kernel(*refs, total=total, width=widt...  4.56 us
  transfers between devices with their start and end apart: 7, of which 5 were waited for; matrix products, arithmetic and copies ran while one was open for 0% of the time, Pallas kernels for 0%

profile of v1, /device:TPU:0, one launch (start us, length us, event | category | flops | bytes accessed | tf_op | source)
XLA Modules:
  0.0 37.2 jit_solution(4512993443592753787)
XLA Ops:
  0.0 0.0 copy-start
  0.0 3.1 %copy-done = bf16[256,14336]{1,0:T(8,128)(2,1)S(1)} copy-done((bf16[256,14336]{1,0:T(8,128)(2,1)S(1)}, bf16[256,14336]{1,0:T(8,128)(2,1)}, u32[]{:S(2)}) %copy-start) | copy-done | bytes 7340056
  3.1 0.0 copy-start.1
  3.1 1.6 %copy-done.1 = bf16[256,4096]{1,0:T(8,128)(2,1)S(1)} copy-done((bf16[256,4096]{1,0:T(8,128)(2,1)S(1)}, bf16[256,4096]{1,0:T(8,128)(2,1)}, u32[]{:S(2)}) %copy-start.1) | copy-done | bytes 2097176
  4.7 0.0 copy-start.2
  4.7 1.2 %copy-done.2 = bf16[32,14336]{1,0:T(8,128)(2,1)S(1)} copy-done((bf16[32,14336]{1,0:T(8,128)(2,1)S(1)}, bf16[32,14336]{1,0:T(8,128)(2,1)}, u32[]{:S(2)}) %copy-start.2) | copy-done | bytes 917528
  5.9 0.0 copy-start.3
  5.9 0.9 %copy-done.3 = bf16[32,4096]{1,0:T(8,128)(2,1)S(1)} copy-done((bf16[32,4096]{1,0:T(8,128)(2,1)S(1)}, bf16[32,4096]{1,0:T(8,128)(2,1)}, u32[]{:S(2)}) %copy-start.3) | copy-done | bytes 262168
  6.8 0.0 copy-start.5
  6.8 0.7 %copy-done.5 = s32[1,9]{1,0:T(1,128)S(1)} copy-done((s32[1,9]{1,0:T(1,128)S(1)}, s32[1,9]{1,0:T(1,128)}, u32[]{:S(2)}) %copy-start.5) | copy-done | bytes 60
  7.5 0.0 copy-start.4
  7.5 5.8 %shard_map.64 = f32[8,1024]{1,0:T(8,128)S(1)} custom-call(s32[1,9]{1,0:T(1,128)S(1)} %copy-done.5, bf16[256,14336]{1,0:T(8,128)(2,1)S(1)} %copy-done, bf16[256,4096]{1,0:T(8,128)(2,1)S(1)} %copy-done.1, bf16[32,14336]{1,0:T(8,128)(2,1)S(1)} %copy-done.2, bf16[32,4096]{1,0:T(8,128)(2,1)S(1)} %copy-done.3), custom_call_target="tpu_custom_call" | custom-call | flops 301989888 | bytes 10616832 | tf_op jit(solution)/shard_map/pallas_call | solution.py:80
  13.2 3.1 %collective-permute-start = (f32[8,1024]{1,0:T(8,128)S(1)}, f32[8,1024]{1,0:T(8,128)S(1)}, u32[]{:S(2)}, u32[]{:S(2)}) collective-permute-start(f32[8,1024]{1,0:T(8,128)S(1)} %shard_map.64), channel_id=1, source_target_pairs={{0,1},{1,0},{2,3},{3,2},{4,5},{5,4},{6,7},{7,6},{8,9},{9,8},{10,11... | collective-permute-start | bytes 98312 | tf_op jit(solution)/shard_map/ppermute | solution.py:184
  16.3 1.9 %collective-permute-done = f32[8,1024]{1,0:T(8,128)S(1)} collective-permute-done((f32[8,1024]{1,0:T(8,128)S(1)}, f32[8,1024]{1,0:T(8,128)S(1)}, u32[]{:S(2)}, u32[]{:S(2)}) %collective-permute-start) | collective-permute-done | bytes 32800 | tf_op jit(solution)/shard_map/ppermute | solution.py:184
  18.2 3.0 %collective-permute-start.1 = (f32[16,1024]{1,0:T(8,128)S(1)}, f32[16,1024]{1,0:T(8,128)S(1)}, u32[]{:S(2)}, u32[]{:S(2)}) collective-permute-start(f32[16,1024]{1,0:T(8,128)S(1)} %pad_maximum_fusion.2), channel_id=1, source_target_pairs={{0,2},{1,3},{2,0},{3,1},{4,6},{5,7},{6,4},{7,5},{8,10},{9,11},{10,... | collective-permute-start | bytes 196616 | tf_op jit(solution)/shard_map/ppermute | solution.py:184
  21.3 0.0 copy-done.4
  21.3 1.5 %collective-permute-start.5 = (bf16[512,256]{1,0:T(8,128)(2,1)S(1)}, bf16[512,256]{1,0:T(8,128)(2,1)S(1)}, u32[]{:S(2)}, u32[]{:S(2)}) collective-permute-start(bf16[512,256]{1,0:T(8,128)(2,1)S(1)} %copy-done.4), channel_id=1, source_target_pairs={{0,8},{4,12},{8,0},{12,4},{1,9},{5,13},{9,1},{13,5},{2,10},{6,14},... | collective-permute-start | bytes 786440 | tf_op jit(solution)/shard_map/ppermute | solution.py:184
  22.8 0.7 %collective-permute-done.1 = f32[16,1024]{1,0:T(8,128)S(1)} collective-permute-done((f32[16,1024]{1,0:T(8,128)S(1)}, f32[16,1024]{1,0:T(8,128)S(1)}, u32[]{:S(2)}, u32[]{:S(2)}) %collective-permute-start.1) | collective-permute-done | bytes 65568 | tf_op jit(solution)/shard_map/ppermute | solution.py:184
  23.5 1.9 %collective-permute-start.2 = (f32[32,1024]{1,0:T(8,128)S(1)}, f32[32,1024]{1,0:T(8,128)S(1)}, u32[]{:S(2)}, u32[]{:S(2)}) collective-permute-start(f32[32,1024]{1,0:T(8,128)S(1)} %pad_maximum_fusion.1), channel_id=1, source_target_pairs={{0,8},{4,12},{8,0},{12,4},{1,9},{5,13},{9,1},{13,5},{2,10},{6,14},... | collective-permute-start | bytes 393224 | tf_op jit(solution)/shard_map/ppermute | solution.py:184
  25.4 0.0 collective-permute-start.4
  25.4 5.3 %collective-permute-done.2 = f32[32,1024]{1,0:T(8,128)S(1)} collective-permute-done((f32[32,1024]{1,0:T(8,128)S(1)}, f32[32,1024]{1,0:T(8,128)S(1)}, u32[]{:S(2)}, u32[]{:S(2)}) %collective-permute-start.2) | collective-permute-done | bytes 131104 | tf_op jit(solution)/shard_map/ppermute | solution.py:184
  30.7 0.1 collective-permute-start.3
  30.8 0.0 collective-permute-done.5.refs_4_
  30.8 0.5 %collective-permute-start.6 = (bf16[512,256]{1,0:T(8,128)(2,1)S(1)}, bf16[512,256]{1,0:T(8,128)(2,1)S(1)}, u32[]{:S(2)}, u32[]{:S(2)}) collective-permute-start(bf16[512,256]{1,0:T(8,128)(2,1)S(1)} %collective-permute-done.5.refs_4_), channel_id=1, source_target_pairs={{0,4},{4,0},{8,12},{12,8},{1,5},{5,1},{9,13},{13,9},{2,6},{6,2},{1... | collective-permute-start | bytes 786440 | tf_op jit(solution)/shard_map/ppermute | solution.py:184
  31.3 0.0 collective-permute-done.4.refs_3_
  31.3 1.0 %collective-permute-done.3.refs_1_ = f32[64,1024]{1,0:T(8,128)S(1)} collective-permute-done((f32[64,1024]{1,0:T(8,128)S(1)}, f32[64,1024]{1,0:T(8,128)S(1)}, u32[]{:S(2)}, u32[]{:S(2)}) %collective-permute-start.3) | collective-permute-done | bytes 262176 | tf_op jit(solution)/shard_map/ppermute | solution.py:184
  32.3 0.4 %collective-permute-done.6.refs_5_ = bf16[512,256]{1,0:T(8,128)(2,1)S(1)} collective-permute-done((bf16[512,256]{1,0:T(8,128)(2,1)S(1)}, bf16[512,256]{1,0:T(8,128)(2,1)S(1)}, u32[]{:S(2)}, u32[]{:S(2)}) %collective-permute-start.6) | collective-permute-done | bytes 262176 | tf_op jit(solution)/shard_map/ppermute | solution.py:184
  32.7 4.6 %shard_map.65 = f32[32,512]{1,0:T(8,128)} custom-call(f32[64,1024]{1,0:T(8,128)S(1)} %pad_maximum_fusion.refs_0_, f32[64,1024]{1,0:T(8,128)S(1)} %collective-permute-done.3.refs_1_, bf16[512,256]{1,0:T(8,128)(2,1)S(1)} %copy-done.4, bf16[512,256]{1,0:T(8,128)(2,1)S(1)} %collective-permute-done.4.refs_3_, ...), custom_call_target="tpu_custom_call" | custom-call | tf_op jit(solution)/shard_map/pallas_call | solution.py:204
  (3 shorter events, 0.0 us)
Async XLA Ops:
  0.0 3.1 %copy-start = (bf16[256,14336]{1,0:T(8,128)(2,1)S(1)}, bf16[256,14336]{1,0:T(8,128)(2,1)}, u32[]{:S(2)}) copy-start(bf16[256,14336]{1,0:T(8,128)(2,1)} %hidden.1) | copy-start | bytes 22020100
  3.1 1.6 %copy-start.1 = (bf16[256,4096]{1,0:T(8,128)(2,1)S(1)}, bf16[256,4096]{1,0:T(8,128)(2,1)}, u32[]{:S(2)}) copy-start(bf16[256,4096]{1,0:T(8,128)(2,1)} %out_grad.1) | copy-start | bytes 6291460
  4.7 1.2 %copy-start.2 = (bf16[32,14336]{1,0:T(8,128)(2,1)S(1)}, bf16[32,14336]{1,0:T(8,128)(2,1)}, u32[]{:S(2)}) copy-start(bf16[32,14336]{1,0:T(8,128)(2,1)} %proj_in.1) | copy-start | bytes 2752516
  5.9 0.9 %copy-start.3 = (bf16[32,4096]{1,0:T(8,128)(2,1)S(1)}, bf16[32,4096]{1,0:T(8,128)(2,1)}, u32[]{:S(2)}) copy-start(bf16[32,4096]{1,0:T(8,128)(2,1)} %proj_out.1) | copy-start | bytes 786436
  6.8 0.7 %copy-start.5 = (s32[1,9]{1,0:T(1,128)S(1)}, s32[1,9]{1,0:T(1,128)}, u32[]{:S(2)}) copy-start(s32[1,9]{1,0:T(1,128)} %lengths.1) | copy-start | bytes 112
  7.5 13.8 %copy-start.4 = (bf16[512,256]{1,0:T(8,128)(2,1)S(1)}, bf16[512,256]{1,0:T(8,128)(2,1)}, u32[]{:S(2)}) copy-start(bf16[512,256]{1,0:T(8,128)(2,1)} %refs_2_.1) | copy-start | bytes 786436
  13.2 5.0 %collective-permute-start = (f32[8,1024]{1,0:T(8,128)S(1)}, f32[8,1024]{1,0:T(8,128)S(1)}, u32[]{:S(2)}, u32[]{:S(2)}) collective-permute-start(f32[8,1024]{1,0:T(8,128)S(1)} %shard_map.64), channel_id=1, source_target_pairs={{0,1},{1,0},{2,3},{3,2},{4,5},{5,4},{6,7},{7,6},{8,9},{9,8},{10,11... | collective-permute-start | bytes 98312 | tf_op jit(solution)/shard_map/ppermute | solution.py:184
  18.2 5.3 %collective-permute-start.1 = (f32[16,1024]{1,0:T(8,128)S(1)}, f32[16,1024]{1,0:T(8,128)S(1)}, u32[]{:S(2)}, u32[]{:S(2)}) collective-permute-start(f32[16,1024]{1,0:T(8,128)S(1)} %pad_maximum_fusion.2), channel_id=1, source_target_pairs={{0,2},{1,3},{2,0},{3,1},{4,6},{5,7},{6,4},{7,5},{8,10},{9,11},{10,... | collective-permute-start | bytes 196616 | tf_op jit(solution)/shard_map/ppermute | solution.py:184
  21.3 9.5 %collective-permute-start.5 = (bf16[512,256]{1,0:T(8,128)(2,1)S(1)}, bf16[512,256]{1,0:T(8,128)(2,1)S(1)}, u32[]{:S(2)}, u32[]{:S(2)}) collective-permute-start(bf16[512,256]{1,0:T(8,128)(2,1)S(1)} %copy-done.4), channel_id=1, source_target_pairs={{0,8},{4,12},{8,0},{12,4},{1,9},{5,13},{9,1},{13,5},{2,10},{6,14},... | collective-permute-start | bytes 786440 | tf_op jit(solution)/shard_map/ppermute | solution.py:184
  23.5 7.2 %collective-permute-start.2 = (f32[32,1024]{1,0:T(8,128)S(1)}, f32[32,1024]{1,0:T(8,128)S(1)}, u32[]{:S(2)}, u32[]{:S(2)}) collective-permute-start(f32[32,1024]{1,0:T(8,128)S(1)} %pad_maximum_fusion.1), channel_id=1, source_target_pairs={{0,8},{4,12},{8,0},{12,4},{1,9},{5,13},{9,1},{13,5},{2,10},{6,14},... | collective-permute-start | bytes 393224 | tf_op jit(solution)/shard_map/ppermute | solution.py:184
  25.4 5.9 %collective-permute-start.4 = (bf16[512,256]{1,0:T(8,128)(2,1)S(1)}, bf16[512,256]{1,0:T(8,128)(2,1)S(1)}, u32[]{:S(2)}, u32[]{:S(2)}) collective-permute-start(bf16[512,256]{1,0:T(8,128)(2,1)S(1)} %copy-done.4), channel_id=1, source_target_pairs={{0,4},{4,0},{8,12},{12,8},{1,5},{5,1},{9,13},{13,9},{2,6},{6,2},{1... | collective-permute-start | bytes 786440 | tf_op jit(solution)/shard_map/ppermute | solution.py:184
  30.7 1.6 %collective-permute-start.3 = (f32[64,1024]{1,0:T(8,128)S(1)}, f32[64,1024]{1,0:T(8,128)S(1)}, u32[]{:S(2)}, u32[]{:S(2)}) collective-permute-start(f32[64,1024]{1,0:T(8,128)S(1)} %pad_maximum_fusion.refs_0_), channel_id=1, source_target_pairs={{0,4},{4,0},{8,12},{12,8},{1,5},{5,1},{9,13},{13,9},{2,6},{6,2},{1... | collective-permute-start | bytes 786440 | tf_op jit(solution)/shard_map/ppermute | solution.py:184
  30.8 1.9 %collective-permute-start.6 = (bf16[512,256]{1,0:T(8,128)(2,1)S(1)}, bf16[512,256]{1,0:T(8,128)(2,1)S(1)}, u32[]{:S(2)}, u32[]{:S(2)}) collective-permute-start(bf16[512,256]{1,0:T(8,128)(2,1)S(1)} %collective-permute-done.5.refs_4_), channel_id=1, source_target_pairs={{0,4},{4,0},{8,12},{12,8},{1,5},{5,1},{9,13},{13,9},{2,6},{6,2},{1... | collective-permute-start | bytes 786440 | tf_op jit(solution)/shard_map/ppermute | solution.py:184

commit v2 on v1

--- a/solution.py
+++ b/solution.py
@@ -28,46 +28,61 @@
     return hi, mid, (rest - mid.astype(F32)).astype(BF16)
 
 
-def vectors_kernel(lengths, hidden, out_grad, proj_in, proj_out, vectors, side_in, side_out, stacked):
-    step = pl.program_id(0)
-    part_in = dot(proj_in[...], hidden[...], NT)
-    part_out = dot(proj_out[...], out_grad[...], NT)
-
-    @pl.when(step == 0)
-    def _():
-        side_in[...] = part_in
-        side_out[...] = part_out
-
-    @pl.when(step > 0)
-    def _():
-        side_in[...] += part_in
-        side_out[...] += part_out
-
-    @pl.when(step == pl.num_programs(0) - 1)
-    def _():
-        rank, tokens = side_in.shape
-        examples = lengths.shape[1] - 1
-        place = lax.broadcasted_iota(jnp.int32, (1, tokens), 1)
-        outs = side_out[...]
-        rows = []
-        start = jnp.int32(0)
-        for e in range(examples):
-            end = start + lengths[0, e]
-            inside = (place >= start) & (place < end)
-            rows.append(jnp.where(inside, outs, 0.0))
-            start = end
-        masked = jnp.concatenate(rows, axis=0)
-        stacked[:, :rank] = dot(masked, side_in[...], NT, HIGHEST)
-        per = 128 // rank
-        lane = lax.broadcasted_iota(jnp.int32, (examples, 128), 1) // rank
-        for block in range(rank // per):
-            total = None
-            for k in range(per):
-                piece = stacked[pl.ds(block * per + k, examples, stride=rank), :]
-                if k:
-                    piece = jnp.where(lane == k, pltpu.roll(piece, k * rank, axis=1), total)
-                total = piece
-            vectors[:, block * 128:(block + 1) * 128] = total
+STEPS = 4
+
+
+def vectors_kernel(
+    lengths, hidden, out_grad, proj_in, proj_out, vectors, tokens_in, tokens_out, rows_in, rows_out, counts, stacked, sems
+):
+    rank, examples = proj_in.shape[0], vectors.shape[0]
+    tokens = hidden.shape[0]
+    count_copy = pltpu.make_async_copy(lengths, counts, sems.at[STEPS, 0])
+
+    def copies(step):
+        pairs = ((proj_out, rows_out), (out_grad, tokens_out), (proj_in, rows_in), (hidden, tokens_in))
+        made = []
+        for k, (source, target) in enumerate(pairs):
+            size = source.shape[1] // STEPS
+            part = pl.ds(pl.multiple_of(step * size, 128), size)
+            made.append(pltpu.make_async_copy(source.at[:, part], target.at[:, part], sems.at[step, k]))
+        return made
+
+    for step in range(STEPS):
+        for copy in copies(step):
+            copy.start()
+    count_copy.start()
+
+    def project(step, sums):
+        for copy in copies(step):
+            copy.wait()
+        new = []
+        for total, weights, x in ((sums[0], rows_out, tokens_out), (sums[1], rows_in, tokens_in)):
+            size = x.shape[1] // STEPS
+            part = pl.ds(pl.multiple_of(step * size, 128), size)
+            new.append(total + dot(weights[:, part], x[:, part], NT))
+        return tuple(new)
+
+    nothing = jnp.zeros((rank, tokens), F32)
+    side_out, side_in = lax.fori_loop(0, STEPS, project, (nothing, nothing))
+    count_copy.wait()
+    place = lax.broadcasted_iota(jnp.int32, (1, tokens), 1)
+    rows = []
+    start = jnp.int32(0)
+    for e in range(examples):
+        end = start + counts[0, e]
+        rows.append(jnp.where((place >= start) & (place < end), side_out, 0.0))
+        start = end
+    stacked[:, :rank] = dot(jnp.concatenate(rows, axis=0), side_in, NT, HIGHEST)
+    per = 128 // rank
+    lane = lax.broadcasted_iota(jnp.int32, (examples, 128), 1) // rank
+    for block in range(rank // per):
+        total = None
+        for k in range(per):
+            piece = stacked[pl.ds(block * per + k, examples, stride=rank), :]
+            if k:
+                piece = jnp.where(lane == k, pltpu.roll(piece, k * rank, axis=1), total)
+            total = piece
+        vectors[:, block * 128:(block + 1) * 128] = total
 
 
 def example_vectors(hidden, out_grad, proj_in, proj_out, lengths):
@@ -75,26 +90,21 @@
     width_out = proj_out.shape[1]
     tokens = hidden.shape[0]
     examples = lengths.shape[1] - 1
-    steps = 8
-    kin, kout = features // steps, width_out // steps
     return pl.pallas_call(
         vectors_kernel,
-        grid=(steps,),
-        in_specs=[
-            pl.BlockSpec(memory_space=pltpu.SMEM),
-            pl.BlockSpec((tokens, kin), lambda i: (0, i)),
-            pl.BlockSpec((tokens, kout), lambda i: (0, i)),
-            pl.BlockSpec((rank, kin), lambda i: (0, i)),
-            pl.BlockSpec((rank, kout), lambda i: (0, i)),
-        ],
-        out_specs=pl.BlockSpec((examples, rank * rank), lambda i: (0, 0)),
+        in_specs=[pl.BlockSpec(memory_space=pl.ANY)] * 5,
+        out_specs=pl.BlockSpec(memory_space=pltpu.VMEM),
         out_shape=jax.ShapeDtypeStruct((examples, rank * rank), F32),
         scratch_shapes=[
-            pltpu.VMEM((rank, tokens), F32),
-            pltpu.VMEM((rank, tokens), F32),
+            pltpu.VMEM((tokens, features), BF16),
+            pltpu.VMEM((tokens, width_out), BF16),
+            pltpu.VMEM((rank, features), BF16),
+            pltpu.VMEM((rank, width_out), BF16),
+            pltpu.SMEM(lengths.shape, jnp.int32),
             pltpu.VMEM((rank * examples, 128), F32),
+            pltpu.SemaphoreType.DMA((STEPS + 1, 4)),
         ],
-        compiler_params=pltpu.CompilerParams(vmem_limit_bytes=24 * 2**20),
+        compiler_params=pltpu.CompilerParams(vmem_limit_bytes=60 * 2**20),
         cost_estimate=pl.CostEstimate(
             flops=2 * tokens * rank * (features + width_out),
             bytes_accessed=2 * (tokens + rank) * (features + width_out),
@@ -115,12 +125,12 @@
     return both[:, :n] + both[:, n:]
 
 
-def scores_kernel(near, far, q0, q1, q2, q3, out, total, width):
+def scores_kernel(*refs, width):
+    *pieces, q0, q1, q2, q3, out = refs
     ex, qry = lax.axis_index("ex"), lax.axis_index("qry")
     block = q0.shape[1]
-    n = total
-    halves = (near, far)
-    vec = jnp.concatenate([near[...], far[...]], axis=0)
+    vec = jnp.concatenate([piece[...] for piece in pieces], axis=0)
+    n = vec.shape[0]
     vh, vm, vl = split3(vec)
     gram = dot(vh, vh, NT) + ((dot(vh, vm, NT) + dot(vm, vh, NT)) + (dot(vm, vm, NT) + dot(vh, vl, NT) + dot(vl, vh, NT)))
     gram = gram / n
@@ -164,7 +174,7 @@
     cross = None
     for k, q in enumerate((q0, q1, q2, q3)):
         start = pl.multiple_of((ex ^ k) * block, block)
-        here = jnp.concatenate([h[:, pl.ds(start, block)] for h in halves], axis=0)
+        here = jnp.concatenate([piece[:, pl.ds(start, block)] for piece in pieces], axis=0)
         hh, hm, hl = split3(here)
         qb = q[...]
         term = dot(hh, qb, NT) + dot(hm, qb, NT) + dot(hl, qb, NT)
@@ -174,8 +184,8 @@
     each = mine // groups
     weights = inverse[:mine] * root_row * root_col[:mine]
     result = dot(weights, cross, NN, HIGHEST)
-    for g in range(groups):
-        to = pl.multiple_of((qry ^ g) * each, each)
+    for g, away in enumerate((0, 2, 1, 3)):
+        to = pl.multiple_of((qry ^ away) * each, each)
         out[pl.ds(to, each), :] = result[g * each:(g + 1) * each]
 
 
@@ -184,30 +194,29 @@
     return lax.ppermute(x, axis, [(i, i ^ bit) for i in range(size)])
 
 
-def doubled(x, axis, bit):
-    return jnp.concatenate([x, swap(x, axis, bit)], axis=0)
-
-
 def body_small(hidden, out_grad, proj_in, proj_out, lengths, queries):
     width = proj_in.shape[0] * proj_in.shape[0]
+    both = ("ex", "qry")
+    per = lax.axis_size("qry")
     q1 = swap(queries, "ex", 1)
     q2 = swap(queries, "ex", 2)
     vectors = example_vectors(hidden, out_grad, proj_in, proj_out, lengths)
-    vectors = doubled(vectors, "qry", 1)
-    vectors = doubled(vectors, "qry", 2)
+    vectors, q1, q2 = lax.optimization_barrier((vectors, q1, q2))
+    own = jnp.concatenate([vectors, swap(vectors, "qry", 2)], axis=0)
+    here = (own, swap(own, "qry", 1), swap(own, "ex", 2), swap(own, both, 2 * per + 1))
+    there = tuple(swap(piece, "ex", 1) for piece in here)
     q3 = swap(q2, "ex", 1)
-    vectors = doubled(vectors, "ex", 2)
-    far = swap(vectors, "ex", 1)
-    total = 2 * vectors.shape[0]
+    pieces = here + there
+    total = sum(piece.shape[0] for piece in pieces)
     mine = total // lax.axis_size("ex")
     count = queries.shape[0]
     return pl.pallas_call(
-        lambda *refs: scores_kernel(*refs, total=total, width=width),
+        lambda *refs: scores_kernel(*refs, width=width),
         out_shape=jax.ShapeDtypeStruct((mine, count), F32),
-        in_specs=[pl.BlockSpec(memory_space=pltpu.VMEM)] * 6,
+        in_specs=[pl.BlockSpec(memory_space=pltpu.VMEM)] * (len(pieces) + 4),
         out_specs=pl.BlockSpec(memory_space=pltpu.VMEM),
         compiler_params=pltpu.CompilerParams(vmem_limit_bytes=24 * 2**20),
-    )(vectors, far, queries, q1, q2, q3)
+    )(*pieces, queries, q1, q2, q3)
 
 
 def body_large(hidden, out_grad, proj_in, proj_out, lengths, queries):

time: 37.5 us -> 28.7 us (0.77)
  local copies, waits for them, and re-layouts: 7.46 us -> 0.8 us
  waiting for transfers between devices: 9.27 us -> 7.59 us
  starting transfers between devices: 10.1 us -> 9.35 us
  Pallas kernels: 10.3 us -> 10.8 us
    unnamed x12 -> x3, local copies, waits for them, and re-layouts: 7.46 us -> 0.79 us
    ppermute x7 -> x11, waiting for transfers between devices: 9.27 us -> 7.59 us  [swap(): return lax.ppermute(x, axis, [(i, i ^ bit) for i in range(size)])]
    ppermute x7 -> x11, starting transfers between devices: 10.1 us -> 9.35 us  [swap(): return lax.ppermute(x, axis, [(i, i ^ bit) for i in range(size)])]
    pallas_call x2, Pallas kernels: 10.3 us -> 10.8 us  [the longest x1 6.21 us: example_vectors(): pl.pallas_call(vectors_kernel, in_specs=[pl.BlockSpec(memory_space=pl.ANY...]
  transfers between devices with their start and end apart: 7 -> 11, of which waited for: 5 -> 7; matrix products, arithmetic and copies ran while one was open for 0% -> 3% of each run, Pallas kernels for 0% -> 22%
where the time goes in v2:
time: 28.7 us; the launch traced here: 28.5 us
  Pallas kernels  10.8 us (38%)
  starting transfers between devices  9.35 us (33%)
  waiting for transfers between devices  7.59 us (26%)
  local copies, waits for them, and re-layouts  0.8 us (3%)
    ppermute x11, starting transfers between devices, swap(): return lax.ppermute(x, axis, [(i, i ^ bit) for i in range(size)])  9.35 us
    ppermute x11, waiting for transfers between devices, swap(): return lax.ppermute(x, axis, [(i, i ^ bit) for i in range(size)])  7.59 us
    pallas_call x1, Pallas kernels, example_vectors(): pl.pallas_call(vectors_kernel, in_specs=[pl.BlockSpec(memory_space=pl.ANY...  6.21 us
    pallas_call x1, Pallas kernels, body_small(): pl.pallas_call(lambda *refs: scores_kernel(*refs, width=width), out_shape...  4.57 us
    unnamed x3, local copies, waits for them, and re-layouts  0.79 us
  transfers between devices with their start and end apart: 11, of which 7 were waited for; matrix products, arithmetic and copies ran while one was open for 3% of the time, Pallas kernels for 22%

profile of v2, /device:TPU:0, one launch (start us, length us, event | category | flops | bytes accessed | tf_op | source)
XLA Modules:
  0.0 28.5 jit_solution(11336241560661793827)
XLA Ops:
  0.0 0.0 copy-start
  0.0 0.5 %collective-permute-start = (bf16[512,256]{1,0:T(8,128)(2,1)}, bf16[512,256]{1,0:T(8,128)(2,1)S(1)}, u32[]{:S(2)}, u32[]{:S(2)}) collective-permute-start(bf16[512,256]{1,0:T(8,128)(2,1)} %refs_8_.1), channel_id=1, source_target_pairs={{0,4},{4,0},{8,12},{12,8},{1,5},{5,1},{9,13},{13,9},{2,6},{6,2},{1... | collective-permute-start | bytes 786440 | tf_op jit(solution)/shard_map/ppermute | solution.py:194
  0.5 2.6 %collective-permute-start.1 = (bf16[512,256]{1,0:T(8,128)(2,1)}, bf16[512,256]{1,0:T(8,128)(2,1)S(1)}, u32[]{:S(2)}, u32[]{:S(2)}) collective-permute-start(bf16[512,256]{1,0:T(8,128)(2,1)} %refs_8_.1), channel_id=1, source_target_pairs={{0,8},{4,12},{8,0},{12,4},{1,9},{5,13},{9,1},{13,5},{2,10},{6,14},... | collective-permute-start | bytes 786440 | tf_op jit(solution)/shard_map/ppermute | solution.py:194
  3.0 6.2 %shard_map.64 = f32[8,1024]{1,0:T(8,128)} custom-call(s32[1,9]{1,0:T(1,128)} %lengths.1, bf16[256,14336]{1,0:T(8,128)(2,1)} %hidden.1, bf16[256,4096]{1,0:T(8,128)(2,1)} %out_grad.1, bf16[32,14336]{1,0:T(8,128)(2,1)} %proj_in.1, bf16[32,4096]{1,0:T(8,128)(2,1)} %proj_out.1), custom_call_target="tpu_custom_call" | custom-call | flops 301989888 | bytes 10616832 | tf_op jit(solution)/shard_map/pallas_call | solution.py:93
  9.3 0.0 collective-permute-done.refs_9_
  9.3 0.9 %collective-permute-done.1.refs_10_ = bf16[512,256]{1,0:T(8,128)(2,1)S(1)} collective-permute-done((bf16[512,256]{1,0:T(8,128)(2,1)}, bf16[512,256]{1,0:T(8,128)(2,1)S(1)}, u32[]{:S(2)}, u32[]{:S(2)}) %collective-permute-start.1) | collective-permute-done | bytes 262176 | tf_op jit(solution)/shard_map/ppermute | solution.py:194
  10.2 2.8 %collective-permute-start.2 = (f32[8,1024]{1,0:T(8,128)}, f32[8,1024]{1,0:T(8,128)S(1)}, u32[]{:S(2)}, u32[]{:S(2)}) collective-permute-start(f32[8,1024]{1,0:T(8,128)} %shard_map.64), channel_id=1, source_target_pairs={{0,2},{1,3},{2,0},{3,1},{4,6},{5,7},{6,4},{7,5},{8,10},{9,11},{10,... | collective-permute-start | bytes 98312 | tf_op jit(solution)/shard_map/ppermute | solution.py:194
  13.0 0.0 collective-permute-start.10
  13.0 0.8 %constant_dynamic-update-slice_fusion.1 = f32[16,1024]{1,0:T(8,128)S(1)} fusion(f32[8,1024]{1,0:T(8,128)} %shard_map.64), kind=kLoop, calls=%fused_computation.1 | loop fusion | bytes 65536
  13.8 1.7 %collective-permute-done.2 = f32[8,1024]{1,0:T(8,128)S(1)} collective-permute-done((f32[8,1024]{1,0:T(8,128)}, f32[8,1024]{1,0:T(8,128)S(1)}, u32[]{:S(2)}, u32[]{:S(2)}) %collective-permute-start.2) | collective-permute-done | bytes 32800 | tf_op jit(solution)/shard_map/ppermute | solution.py:194
  15.5 2.5 %collective-permute-start.5 = (f32[16,1024]{1,0:T(8,128)S(1)}, f32[16,1024]{1,0:T(8,128)S(1)}, u32[]{:S(2)}, u32[]{:S(2)}) collective-permute-start(f32[16,1024]{1,0:T(8,128)S(1)} %constant_dynamic-update-slice_fusion.refs_0_), channel_id=1, source_target_pairs={{0,9},{1,8},{2,11},{3,10},{4,13},{5,12},{6,15},{7,14},{8,1},{9,0},... | collective-permute-start | bytes 196616 | tf_op jit(solution)/shard_map/ppermute | solution.py:194
  17.9 0.5 %collective-permute-start.4 = (f32[16,1024]{1,0:T(8,128)S(1)}, f32[16,1024]{1,0:T(8,128)S(1)}, u32[]{:S(2)}, u32[]{:S(2)}) collective-permute-start(f32[16,1024]{1,0:T(8,128)S(1)} %constant_dynamic-update-slice_fusion.refs_0_), channel_id=1, source_target_pairs={{0,8},{4,12},{8,0},{12,4},{1,9},{5,13},{9,1},{13,5},{2,10},{6,14},... | collective-permute-start | bytes 196616 | tf_op jit(solution)/shard_map/ppermute | solution.py:194
  18.5 0.5 %collective-permute-start.3 = (f32[16,1024]{1,0:T(8,128)S(1)}, f32[16,1024]{1,0:T(8,128)S(1)}, u32[]{:S(2)}, u32[]{:S(2)}) collective-permute-start(f32[16,1024]{1,0:T(8,128)S(1)} %constant_dynamic-update-slice_fusion.refs_0_), channel_id=1, source_target_pairs={{0,1},{1,0},{2,3},{3,2},{4,5},{5,4},{6,7},{7,6},{8,9},{9,8},{10,11... | collective-permute-start | bytes 196616 | tf_op jit(solution)/shard_map/ppermute | solution.py:194
  19.0 0.0 collective-permute-start.6
  19.0 2.0 %collective-permute-done.5.refs_3_ = f32[16,1024]{1,0:T(8,128)S(1)} collective-permute-done((f32[16,1024]{1,0:T(8,128)S(1)}, f32[16,1024]{1,0:T(8,128)S(1)}, u32[]{:S(2)}, u32[]{:S(2)}) %collective-permute-start.5) | collective-permute-done | bytes 65568 | tf_op jit(solution)/shard_map/ppermute | solution.py:194
  21.0 0.0 collective-permute-start.9
  21.0 1.2 %collective-permute-done.4.refs_2_ = f32[16,1024]{1,0:T(8,128)S(1)} collective-permute-done((f32[16,1024]{1,0:T(8,128)S(1)}, f32[16,1024]{1,0:T(8,128)S(1)}, u32[]{:S(2)}, u32[]{:S(2)}) %collective-permute-start.4) | collective-permute-done | bytes 65568 | tf_op jit(solution)/shard_map/ppermute | solution.py:194
  22.2 0.0 collective-permute-start.8
  22.2 0.5 %collective-permute-done.3.refs_1_ = f32[16,1024]{1,0:T(8,128)S(1)} collective-permute-done((f32[16,1024]{1,0:T(8,128)S(1)}, f32[16,1024]{1,0:T(8,128)S(1)}, u32[]{:S(2)}, u32[]{:S(2)}) %collective-permute-start.3) | collective-permute-done | bytes 65568 | tf_op jit(solution)/shard_map/ppermute | solution.py:194
  22.7 0.0 collective-permute-start.7
  22.7 0.0 collective-permute-done.6.refs_4_
  22.7 0.0 collective-permute-done.9.refs_7_
  22.7 0.7 %collective-permute-done.8.refs_6_ = f32[16,1024]{1,0:T(8,128)S(1)} collective-permute-done((f32[16,1024]{1,0:T(8,128)S(1)}, f32[16,1024]{1,0:T(8,128)S(1)}, u32[]{:S(2)}, u32[]{:S(2)}) %collective-permute-start.8) | collective-permute-done | bytes 65568 | tf_op jit(solution)/shard_map/ppermute | solution.py:194
  23.5 0.5 %collective-permute-done.7.refs_5_ = f32[16,1024]{1,0:T(8,128)S(1)} collective-permute-done((f32[16,1024]{1,0:T(8,128)S(1)}, f32[16,1024]{1,0:T(8,128)S(1)}, u32[]{:S(2)}, u32[]{:S(2)}) %collective-permute-start.7) | collective-permute-done | bytes 65568 | tf_op jit(solution)/shard_map/ppermute | solution.py:194
  24.0 0.0 collective-permute-done.10.refs_11_
  24.0 0.0 copy-done
  24.0 4.6 %shard_map.65 = f32[32,512]{1,0:T(8,128)} custom-call(f32[16,1024]{1,0:T(8,128)S(1)} %constant_dynamic-update-slice_fusion.refs_0_, f32[16,1024]{1,0:T(8,128)S(1)} %collective-permute-done.3.refs_1_, f32[16,1024]{1,0:T(8,128)S(1)} %collective-permute-done.4.refs_2_, f32[16,1024]{1,0:T(8,128)S(1)} %collective-permute-done.5.refs_3_, ...), custom_call_target="tpu_custom_call" | custom-call | tf_op jit(solution)/shard_map/pallas_call | solution.py:213
  (1 shorter events, 0.0 us)
Async XLA Ops:
  0.0 24.0 %copy-start = (bf16[512,256]{1,0:T(8,128)(2,1)S(1)}, bf16[512,256]{1,0:T(8,128)(2,1)}, u32[]{:S(2)}) copy-start(bf16[512,256]{1,0:T(8,128)(2,1)} %refs_8_.1) | copy-start | bytes 786436
  0.0 9.3 %collective-permute-start = (bf16[512,256]{1,0:T(8,128)(2,1)}, bf16[512,256]{1,0:T(8,128)(2,1)S(1)}, u32[]{:S(2)}, u32[]{:S(2)}) collective-permute-start(bf16[512,256]{1,0:T(8,128)(2,1)} %refs_8_.1), channel_id=1, source_target_pairs={{0,4},{4,0},{8,12},{12,8},{1,5},{5,1},{9,13},{13,9},{2,6},{6,2},{1... | collective-permute-start | bytes 786440 | tf_op jit(solution)/shard_map/ppermute | solution.py:194
  0.5 9.7 %collective-permute-start.1 = (bf16[512,256]{1,0:T(8,128)(2,1)}, bf16[512,256]{1,0:T(8,128)(2,1)S(1)}, u32[]{:S(2)}, u32[]{:S(2)}) collective-permute-start(bf16[512,256]{1,0:T(8,128)(2,1)} %refs_8_.1), channel_id=1, source_target_pairs={{0,8},{4,12},{8,0},{12,4},{1,9},{5,13},{9,1},{13,5},{2,10},{6,14},... | collective-permute-start | bytes 786440 | tf_op jit(solution)/shard_map/ppermute | solution.py:194
  10.2 5.3 %collective-permute-start.2 = (f32[8,1024]{1,0:T(8,128)}, f32[8,1024]{1,0:T(8,128)S(1)}, u32[]{:S(2)}, u32[]{:S(2)}) collective-permute-start(f32[8,1024]{1,0:T(8,128)} %shard_map.64), channel_id=1, source_target_pairs={{0,2},{1,3},{2,0},{3,1},{4,6},{5,7},{6,4},{7,5},{8,10},{9,11},{10,... | collective-permute-start | bytes 98312 | tf_op jit(solution)/shard_map/ppermute | solution.py:194
  13.0 11.0 %collective-permute-start.10 = (bf16[512,256]{1,0:T(8,128)(2,1)S(1)}, bf16[512,256]{1,0:T(8,128)(2,1)S(1)}, u32[]{:S(2)}, u32[]{:S(2)}) collective-permute-start(bf16[512,256]{1,0:T(8,128)(2,1)S(1)} %collective-permute-done.1.refs_10_), channel_id=1, source_target_pairs={{0,4},{4,0},{8,12},{12,8},{1,5},{5,1},{9,13},{13,9},{2,6},{6,2},{1... | collective-permute-start | bytes 786440 | tf_op jit(solution)/shard_map/ppermute | solution.py:194
  15.5 5.5 %collective-permute-start.5 = (f32[16,1024]{1,0:T(8,128)S(1)}, f32[16,1024]{1,0:T(8,128)S(1)}, u32[]{:S(2)}, u32[]{:S(2)}) collective-permute-start(f32[16,1024]{1,0:T(8,128)S(1)} %constant_dynamic-update-slice_fusion.refs_0_), channel_id=1, source_target_pairs={{0,9},{1,8},{2,11},{3,10},{4,13},{5,12},{6,15},{7,14},{8,1},{9,0},... | collective-permute-start | bytes 196616 | tf_op jit(solution)/shard_map/ppermute | solution.py:194
  17.9 4.3 %collective-permute-start.4 = (f32[16,1024]{1,0:T(8,128)S(1)}, f32[16,1024]{1,0:T(8,128)S(1)}, u32[]{:S(2)}, u32[]{:S(2)}) collective-permute-start(f32[16,1024]{1,0:T(8,128)S(1)} %constant_dynamic-update-slice_fusion.refs_0_), channel_id=1, source_target_pairs={{0,8},{4,12},{8,0},{12,4},{1,9},{5,13},{9,1},{13,5},{2,10},{6,14},... | collective-permute-start | bytes 196616 | tf_op jit(solution)/shard_map/ppermute | solution.py:194
  18.5 4.3 %collective-permute-start.3 = (f32[16,1024]{1,0:T(8,128)S(1)}, f32[16,1024]{1,0:T(8,128)S(1)}, u32[]{:S(2)}, u32[]{:S(2)}) collective-permute-start(f32[16,1024]{1,0:T(8,128)S(1)} %constant_dynamic-update-slice_fusion.refs_0_), channel_id=1, source_target_pairs={{0,1},{1,0},{2,3},{3,2},{4,5},{5,4},{6,7},{7,6},{8,9},{9,8},{10,11... | collective-permute-start | bytes 196616 | tf_op jit(solution)/shard_map/ppermute | solution.py:194
  19.0 3.8 %collective-permute-start.6 = (f32[16,1024]{1,0:T(8,128)S(1)}, f32[16,1024]{1,0:T(8,128)S(1)}, u32[]{:S(2)}, u32[]{:S(2)}) collective-permute-start(f32[16,1024]{1,0:T(8,128)S(1)} %constant_dynamic-update-slice_fusion.refs_0_), channel_id=1, source_target_pairs={{0,4},{4,0},{8,12},{12,8},{1,5},{5,1},{9,13},{13,9},{2,6},{6,2},{1... | collective-permute-start | bytes 196616 | tf_op jit(solution)/shard_map/ppermute | solution.py:194
  21.0 1.7 %collective-permute-start.9 = (f32[16,1024]{1,0:T(8,128)S(1)}, f32[16,1024]{1,0:T(8,128)S(1)}, u32[]{:S(2)}, u32[]{:S(2)}) collective-permute-start(f32[16,1024]{1,0:T(8,128)S(1)} %collective-permute-done.5.refs_3_), channel_id=1, source_target_pairs={{0,4},{4,0},{8,12},{12,8},{1,5},{5,1},{9,13},{13,9},{2,6},{6,2},{1... | collective-permute-start | bytes 196616 | tf_op jit(solution)/shard_map/ppermute | solution.py:194
  22.2 1.3 %collective-permute-start.8 = (f32[16,1024]{1,0:T(8,128)S(1)}, f32[16,1024]{1,0:T(8,128)S(1)}, u32[]{:S(2)}, u32[]{:S(2)}) collective-permute-start(f32[16,1024]{1,0:T(8,128)S(1)} %collective-permute-done.4.refs_2_), channel_id=1, source_target_pairs={{0,4},{4,0},{8,12},{12,8},{1,5},{5,1},{9,13},{13,9},{2,6},{6,2},{1... | collective-permute-start | bytes 196616 | tf_op jit(solution)/shard_map/ppermute | solution.py:194
  22.7 1.3 %collective-permute-start.7 = (f32[16,1024]{1,0:T(8,128)S(1)}, f32[16,1024]{1,0:T(8,128)S(1)}, u32[]{:S(2)}, u32[]{:S(2)}) collective-permute-start(f32[16,1024]{1,0:T(8,128)S(1)} %collective-permute-done.3.refs_1_), channel_id=1, source_target_pairs={{0,4},{4,0},{8,12},{12,8},{1,5},{5,1},{9,13},{13,9},{2,6},{6,2},{1... | collective-permute-start | bytes 196616 | tf_op jit(solution)/shard_map/ppermute | solution.py:194

commit v3 on v2

--- a/solution.py
+++ b/solution.py
@@ -104,7 +104,7 @@
             pltpu.VMEM((rank * examples, 128), F32),
             pltpu.SemaphoreType.DMA((STEPS + 1, 4)),
         ],
-        compiler_params=pltpu.CompilerParams(vmem_limit_bytes=60 * 2**20),
+        compiler_params=pltpu.CompilerParams(vmem_limit_bytes=55104 * 1024),
         cost_estimate=pl.CostEstimate(
             flops=2 * tokens * rank * (features + width_out),
             bytes_accessed=2 * (tokens + rank) * (features + width_out),
@@ -196,17 +196,22 @@
 
 def body_small(hidden, out_grad, proj_in, proj_out, lengths, queries):
     width = proj_in.shape[0] * proj_in.shape[0]
-    both = ("ex", "qry")
     per = lax.axis_size("qry")
+    core, y = per, 2 * per
+
+    def cross(x, bits):
+        return swap(x, ("ex", "qry"), bits)
+
     q1 = swap(queries, "ex", 1)
     q2 = swap(queries, "ex", 2)
+    hidden, q1 = lax.optimization_barrier((hidden, q1))
     vectors = example_vectors(hidden, out_grad, proj_in, proj_out, lengths)
-    vectors, q1, q2 = lax.optimization_barrier((vectors, q1, q2))
-    own = jnp.concatenate([vectors, swap(vectors, "qry", 2)], axis=0)
-    here = (own, swap(own, "qry", 1), swap(own, "ex", 2), swap(own, both, 2 * per + 1))
-    there = tuple(swap(piece, "ex", 1) for piece in here)
+    own = jnp.concatenate([vectors, cross(vectors, 2)], axis=0)
+    own, q1, q2 = lax.optimization_barrier((own, q1, q2))
+    here = (own, cross(own, core + 1), cross(own, core + y), cross(own, core + y + 1))
+    there = tuple(cross(piece, core) for piece in here)
     q3 = swap(q2, "ex", 1)
-    pieces = here + there
+    pieces = (here[0], there[1], here[1], there[0], *here[2:], *there[2:])
     total = sum(piece.shape[0] for piece in pieces)
     mine = total // lax.axis_size("ex")
     count = queries.shape[0]

time: 28.7 us -> 27.4 us (0.955)
  waiting for transfers between devices: 7.59 us -> 6.17 us
  starting transfers between devices: 9.35 us -> 10.2 us
  Pallas kernels: 10.8 us -> 10.2 us
    ppermute x11, waiting for transfers between devices: 7.59 us -> 6.17 us  [swap(): return lax.ppermute(x, axis, [(i, i ^ bit) for i in range(size)])]
    ppermute x11, starting transfers between devices: 9.35 us -> 10.2 us  [swap(): return lax.ppermute(x, axis, [(i, i ^ bit) for i in range(size)])]
    pallas_call x1, Pallas kernels: 6.21 us -> 5.6 us  [example_vectors(): pl.pallas_call(vectors_kernel, in_specs=[pl.BlockSpec(memory_space=pl.ANY...]
    unnamed x3 -> x4, local copies, waits for them, and re-layouts: 0.79 us -> 0.66 us
  transfers between devices with their start and end apart: 11 -> 11, of which waited for: 7 -> 5; matrix products, arithmetic and copies ran while one was open for 3% -> 0% of each run, Pallas kernels for 22% -> 21%
where the time goes in v3:
time: 27.4 us; the launch traced here: 27.2 us
  starting transfers between devices  10.2 us (37%)
  Pallas kernels  10.2 us (37%)
  waiting for transfers between devices  6.17 us (23%)
  local copies, waits for them, and re-layouts  0.66 us (2%)
    ppermute x11, starting transfers between devices, swap(): return lax.ppermute(x, axis, [(i, i ^ bit) for i in range(size)])  10.2 us
    ppermute x11, waiting for transfers between devices, swap(): return lax.ppermute(x, axis, [(i, i ^ bit) for i in range(size)])  6.17 us
    pallas_call x1, Pallas kernels, example_vectors(): pl.pallas_call(vectors_kernel, in_specs=[pl.BlockSpec(memory_space=pl.ANY...  5.6 us
    pallas_call x1, Pallas kernels, body_small(): pl.pallas_call(lambda *refs: scores_kernel(*refs, width=width), out_shape...  4.57 us
    unnamed x4, local copies, waits for them, and re-layouts  0.66 us
  transfers between devices with their start and end apart: 11, of which 5 were waited for; matrix products, arithmetic and copies ran while one was open for 0% of the time, Pallas kernels for 21%

profile of v3, /device:TPU:0, one launch (start us, length us, event | category | flops | bytes accessed | tf_op | source)
XLA Modules:
  0.0 27.2 jit_solution(10328710528164219446)
XLA Ops:
  0.0 0.0 copy-start
  0.0 0.5 %collective-permute-start = (bf16[512,256]{1,0:T(8,128)(2,1)}, bf16[512,256]{1,0:T(8,128)(2,1)S(1)}, u32[]{:S(2)}, u32[]{:S(2)}) collective-permute-start(bf16[512,256]{1,0:T(8,128)(2,1)} %refs_8_.1), channel_id=1, source_target_pairs={{0,4},{4,0},{8,12},{12,8},{1,5},{5,1},{9,13},{13,9},{2,6},{6,2},{1... | collective-permute-start | bytes 786440 | tf_op jit(solution)/shard_map/ppermute | solution.py:194
  0.5 2.6 %collective-permute-start.2 = (bf16[512,256]{1,0:T(8,128)(2,1)}, bf16[512,256]{1,0:T(8,128)(2,1)S(1)}, u32[]{:S(2)}, u32[]{:S(2)}) collective-permute-start(bf16[512,256]{1,0:T(8,128)(2,1)} %refs_8_.1), channel_id=1, source_target_pairs={{0,8},{4,12},{8,0},{12,4},{1,9},{5,13},{9,1},{13,5},{2,10},{6,14},... | collective-permute-start | bytes 786440 | tf_op jit(solution)/shard_map/ppermute | solution.py:194
  3.0 0.0 collective-permute-done.refs_9_
  3.0 0.0 copy-start.1
  3.0 0.7 %copy-done.1 = s32[1,9]{1,0:T(1,128)S(1)} copy-done((s32[1,9]{1,0:T(1,128)S(1)}, s32[1,9]{1,0:T(1,128)}, u32[]{:S(2)}) %copy-start.1) | copy-done | bytes 60
  3.7 5.6 %shard_map.64 = f32[8,1024]{1,0:T(8,128)S(1)} custom-call(s32[1,9]{1,0:T(1,128)S(1)} %copy-done.1, bf16[256,14336]{1,0:T(8,128)(2,1)} %hidden, bf16[256,4096]{1,0:T(8,128)(2,1)} %out_grad.1, bf16[32,14336]{1,0:T(8,128)(2,1)} %proj_in.1, bf16[32,4096]{1,0:T(8,128)(2,1)} %proj_out.1), custom_call_target="tpu_custom_call" | custom-call | flops 301989888 | bytes 10616832 | tf_op jit(solution)/shard_map/pallas_call | solution.py:93
  9.3 2.8 %collective-permute-start.1 = (f32[8,1024]{1,0:T(8,128)S(1)}, f32[8,1024]{1,0:T(8,128)S(1)}, u32[]{:S(2)}, u32[]{:S(2)}) collective-permute-start(f32[8,1024]{1,0:T(8,128)S(1)} %shard_map.64), channel_id=1, source_target_pairs={{0,2},{1,3},{2,0},{3,1},{4,6},{5,7},{6,4},{7,5},{8,10},{9,11},{10,... | collective-permute-start | bytes 98312 | tf_op jit(solution)/shard_map/ppermute | solution.py:194
  12.1 2.1 %collective-permute-done.1 = f32[8,1024]{1,0:T(8,128)S(1)} collective-permute-done((f32[8,1024]{1,0:T(8,128)S(1)}, f32[8,1024]{1,0:T(8,128)S(1)}, u32[]{:S(2)}, u32[]{:S(2)}) %collective-permute-start.1) | collective-permute-done | bytes 32800 | tf_op jit(solution)/shard_map/ppermute | solution.py:194
  14.2 0.0 collective-permute-done.2.refs_10_
  14.2 0.1 collective-permute-start.10
  14.3 2.8 %collective-permute-start.7 = (f32[16,1024]{1,0:T(8,128)S(1)}, f32[16,1024]{1,0:T(8,128)S(1)}, u32[]{:S(2)}, u32[]{:S(2)}) collective-permute-start(f32[16,1024]{1,0:T(8,128)S(1)} %pad_maximum_fusion.refs_0_), channel_id=1, source_target_pairs={{0,13},{1,12},{2,15},{3,14},{4,9},{5,8},{6,11},{7,10},{8,5},{9,4},... | collective-permute-start | bytes 196616 | tf_op jit(solution)/shard_map/ppermute | solution.py:194
  17.1 0.2 collective-permute-start.6
  17.3 0.4 %collective-permute-start.3 = (f32[16,1024]{1,0:T(8,128)S(1)}, f32[16,1024]{1,0:T(8,128)S(1)}, u32[]{:S(2)}, u32[]{:S(2)}) collective-permute-start(f32[16,1024]{1,0:T(8,128)S(1)} %pad_maximum_fusion.refs_0_), channel_id=1, source_target_pairs={{0,5},{1,4},{2,7},{3,6},{4,1},{5,0},{6,3},{7,2},{8,13},{9,12},{10,... | collective-permute-start | bytes 196616 | tf_op jit(solution)/shard_map/ppermute | solution.py:194
  17.6 0.4 %collective-permute-start.5 = (f32[16,1024]{1,0:T(8,128)S(1)}, f32[16,1024]{1,0:T(8,128)S(1)}, u32[]{:S(2)}, u32[]{:S(2)}) collective-permute-start(f32[16,1024]{1,0:T(8,128)S(1)} %pad_maximum_fusion.refs_0_), channel_id=1, source_target_pairs={{0,4},{1,5},{2,6},{3,7},{4,0},{5,1},{6,2},{7,3},{8,12},{9,13},{10,... | collective-permute-start | bytes 196616 | tf_op jit(solution)/shard_map/ppermute | solution.py:194
  18.0 1.5 %collective-permute-done.7.refs_5_ = f32[16,1024]{1,0:T(8,128)S(1)} collective-permute-done((f32[16,1024]{1,0:T(8,128)S(1)}, f32[16,1024]{1,0:T(8,128)S(1)}, u32[]{:S(2)}, u32[]{:S(2)}) %collective-permute-start.7) | collective-permute-done | bytes 65568 | tf_op jit(solution)/shard_map/ppermute | solution.py:194
  19.5 0.0 collective-permute-start.9
  19.5 1.7 %collective-permute-done.6.refs_4_ = f32[16,1024]{1,0:T(8,128)S(1)} collective-permute-done((f32[16,1024]{1,0:T(8,128)S(1)}, f32[16,1024]{1,0:T(8,128)S(1)}, u32[]{:S(2)}, u32[]{:S(2)}) %collective-permute-start.6) | collective-permute-done | bytes 65568 | tf_op jit(solution)/shard_map/ppermute | solution.py:194
  21.2 0.1 collective-permute-start.8
  21.3 0.0 collective-permute-done.3.refs_2_
  21.3 0.4 %collective-permute-start.4 = (f32[16,1024]{1,0:T(8,128)S(1)}, f32[16,1024]{1,0:T(8,128)S(1)}, u32[]{:S(2)}, u32[]{:S(2)}) collective-permute-start(f32[16,1024]{1,0:T(8,128)S(1)} %collective-permute-done.3.refs_2_), channel_id=1, source_target_pairs={{0,4},{1,5},{2,6},{3,7},{4,0},{5,1},{6,2},{7,3},{8,12},{9,13},{10,... | collective-permute-start | bytes 196616 | tf_op jit(solution)/shard_map/ppermute | solution.py:194
  21.7 0.0 collective-permute-done.5.refs_3_
  21.7 0.0 collective-permute-done.9.refs_7_
  21.7 0.7 %collective-permute-done.8.refs_6_ = f32[16,1024]{1,0:T(8,128)S(1)} collective-permute-done((f32[16,1024]{1,0:T(8,128)S(1)}, f32[16,1024]{1,0:T(8,128)S(1)}, u32[]{:S(2)}, u32[]{:S(2)}) %collective-permute-start.8) | collective-permute-done | bytes 65568 | tf_op jit(solution)/shard_map/ppermute | solution.py:194
  22.5 0.2 collective-permute-done.4.refs_1_
  22.6 0.0 collective-permute-done.10.refs_11_
  22.6 0.0 copy-done
  22.6 4.6 %shard_map.65 = f32[32,512]{1,0:T(8,128)} custom-call(f32[16,1024]{1,0:T(8,128)S(1)} %pad_maximum_fusion.refs_0_, f32[16,1024]{1,0:T(8,128)S(1)} %collective-permute-done.4.refs_1_, f32[16,1024]{1,0:T(8,128)S(1)} %collective-permute-done.3.refs_2_, f32[16,1024]{1,0:T(8,128)S(1)} %collective-permute-done.5.refs_3_, ...), custom_call_target="tpu_custom_call" | custom-call | tf_op jit(solution)/shard_map/pallas_call | solution.py:218
  (1 shorter events, 0.0 us)
Async XLA Ops:
  0.0 22.6 %copy-start = (bf16[512,256]{1,0:T(8,128)(2,1)S(1)}, bf16[512,256]{1,0:T(8,128)(2,1)}, u32[]{:S(2)}) copy-start(bf16[512,256]{1,0:T(8,128)(2,1)} %refs_8_.1) | copy-start | bytes 786436
  0.0 3.0 %collective-permute-start = (bf16[512,256]{1,0:T(8,128)(2,1)}, bf16[512,256]{1,0:T(8,128)(2,1)S(1)}, u32[]{:S(2)}, u32[]{:S(2)}) collective-permute-start(bf16[512,256]{1,0:T(8,128)(2,1)} %refs_8_.1), channel_id=1, source_target_pairs={{0,4},{4,0},{8,12},{12,8},{1,5},{5,1},{9,13},{13,9},{2,6},{6,2},{1... | collective-permute-start | bytes 786440 | tf_op jit(solution)/shard_map/ppermute | solution.py:194
  0.5 13.7 %collective-permute-start.2 = (bf16[512,256]{1,0:T(8,128)(2,1)}, bf16[512,256]{1,0:T(8,128)(2,1)S(1)}, u32[]{:S(2)}, u32[]{:S(2)}) collective-permute-start(bf16[512,256]{1,0:T(8,128)(2,1)} %refs_8_.1), channel_id=1, source_target_pairs={{0,8},{4,12},{8,0},{12,4},{1,9},{5,13},{9,1},{13,5},{2,10},{6,14},... | collective-permute-start | bytes 786440 | tf_op jit(solution)/shard_map/ppermute | solution.py:194
  3.0 0.7 %copy-start.1 = (s32[1,9]{1,0:T(1,128)S(1)}, s32[1,9]{1,0:T(1,128)}, u32[]{:S(2)}) copy-start(s32[1,9]{1,0:T(1,128)} %lengths.1) | copy-start | bytes 112
  9.3 4.9 %collective-permute-start.1 = (f32[8,1024]{1,0:T(8,128)S(1)}, f32[8,1024]{1,0:T(8,128)S(1)}, u32[]{:S(2)}, u32[]{:S(2)}) collective-permute-start(f32[8,1024]{1,0:T(8,128)S(1)} %shard_map.64), channel_id=1, source_target_pairs={{0,2},{1,3},{2,0},{3,1},{4,6},{5,7},{6,4},{7,5},{8,10},{9,11},{10,... | collective-permute-start | bytes 98312 | tf_op jit(solution)/shard_map/ppermute | solution.py:194
  14.2 8.4 %collective-permute-start.10 = (bf16[512,256]{1,0:T(8,128)(2,1)S(1)}, bf16[512,256]{1,0:T(8,128)(2,1)S(1)}, u32[]{:S(2)}, u32[]{:S(2)}) collective-permute-start(bf16[512,256]{1,0:T(8,128)(2,1)S(1)} %collective-permute-done.2.refs_10_), channel_id=1, source_target_pairs={{0,4},{4,0},{8,12},{12,8},{1,5},{5,1},{9,13},{13,9},{2,6},{6,2},{1... | collective-permute-start | bytes 786440 | tf_op jit(solution)/shard_map/ppermute | solution.py:194
  14.3 5.2 %collective-permute-start.7 = (f32[16,1024]{1,0:T(8,128)S(1)}, f32[16,1024]{1,0:T(8,128)S(1)}, u32[]{:S(2)}, u32[]{:S(2)}) collective-permute-start(f32[16,1024]{1,0:T(8,128)S(1)} %pad_maximum_fusion.refs_0_), channel_id=1, source_target_pairs={{0,13},{1,12},{2,15},{3,14},{4,9},{5,8},{6,11},{7,10},{8,5},{9,4},... | collective-permute-start | bytes 196616 | tf_op jit(solution)/shard_map/ppermute | solution.py:194
  17.1 4.1 %collective-permute-start.6 = (f32[16,1024]{1,0:T(8,128)S(1)}, f32[16,1024]{1,0:T(8,128)S(1)}, u32[]{:S(2)}, u32[]{:S(2)}) collective-permute-start(f32[16,1024]{1,0:T(8,128)S(1)} %pad_maximum_fusion.refs_0_), channel_id=1, source_target_pairs={{0,12},{1,13},{2,14},{3,15},{4,8},{5,9},{6,10},{7,11},{8,4},{9,5},... | collective-permute-start | bytes 196616 | tf_op jit(solution)/shard_map/ppermute | solution.py:194
  17.3 4.1 %collective-permute-start.3 = (f32[16,1024]{1,0:T(8,128)S(1)}, f32[16,1024]{1,0:T(8,128)S(1)}, u32[]{:S(2)}, u32[]{:S(2)}) collective-permute-start(f32[16,1024]{1,0:T(8,128)S(1)} %pad_maximum_fusion.refs_0_), channel_id=1, source_target_pairs={{0,5},{1,4},{2,7},{3,6},{4,1},{5,0},{6,3},{7,2},{8,13},{9,12},{10,... | collective-permute-start | bytes 196616 | tf_op jit(solution)/shard_map/ppermute | solution.py:194
  17.6 4.1 %collective-permute-start.5 = (f32[16,1024]{1,0:T(8,128)S(1)}, f32[16,1024]{1,0:T(8,128)S(1)}, u32[]{:S(2)}, u32[]{:S(2)}) collective-permute-start(f32[16,1024]{1,0:T(8,128)S(1)} %pad_maximum_fusion.refs_0_), channel_id=1, source_target_pairs={{0,4},{1,5},{2,6},{3,7},{4,0},{5,1},{6,2},{7,3},{8,12},{9,13},{10,... | collective-permute-start | bytes 196616 | tf_op jit(solution)/shard_map/ppermute | solution.py:194
  19.5 2.3 %collective-permute-start.9 = (f32[16,1024]{1,0:T(8,128)S(1)}, f32[16,1024]{1,0:T(8,128)S(1)}, u32[]{:S(2)}, u32[]{:S(2)}) collective-permute-start(f32[16,1024]{1,0:T(8,128)S(1)} %collective-permute-done.7.refs_5_), channel_id=1, source_target_pairs={{0,4},{1,5},{2,6},{3,7},{4,0},{5,1},{6,2},{7,3},{8,12},{9,13},{10,... | collective-permute-start | bytes 196616 | tf_op jit(solution)/shard_map/ppermute | solution.py:194
  21.2 1.3 %collective-permute-start.8 = (f32[16,1024]{1,0:T(8,128)S(1)}, f32[16,1024]{1,0:T(8,128)S(1)}, u32[]{:S(2)}, u32[]{:S(2)}) collective-permute-start(f32[16,1024]{1,0:T(8,128)S(1)} %collective-permute-done.6.refs_4_), channel_id=1, source_target_pairs={{0,4},{1,5},{2,6},{3,7},{4,0},{5,1},{6,2},{7,3},{8,12},{9,13},{10,... | collective-permute-start | bytes 196616 | tf_op jit(solution)/shard_map/ppermute | solution.py:194
  21.3 1.3 %collective-permute-start.4 = (f32[16,1024]{1,0:T(8,128)S(1)}, f32[16,1024]{1,0:T(8,128)S(1)}, u32[]{:S(2)}, u32[]{:S(2)}) collective-permute-start(f32[16,1024]{1,0:T(8,128)S(1)} %collective-permute-done.3.refs_2_), channel_id=1, source_target_pairs={{0,4},{1,5},{2,6},{3,7},{4,0},{5,1},{6,2},{7,3},{8,12},{9,13},{10,... | collective-permute-start | bytes 196616 | tf_op jit(solution)/shard_map/ppermute | solution.py:194

commit v4 on v3

--- a/solution.py
+++ b/solution.py
@@ -113,26 +113,42 @@
     )(lengths, hidden, out_grad, proj_in, proj_out)
 
 
-def times(a, b):
+def product(a, b):
     ah, am = split2(a)
     bh, bm = split2(b)
-    left = jnp.concatenate([ah, am], axis=1)
     right = jnp.concatenate(
         [jnp.concatenate([bh, bm], axis=1), jnp.concatenate([bh, jnp.zeros_like(bm)], axis=1)], axis=0
     )
-    both = dot(left, right)
+    both = dot(jnp.concatenate([ah, am], axis=1), right)
     n = b.shape[1]
     return both[:, :n] + both[:, n:]
+
+
+def product6(a, b):
+    ah, am, al = split3(a)
+    bh, bm, bl = split3(b)
+    top = jnp.concatenate([bh, bm], axis=1)
+    both = dot(jnp.concatenate([ah, am], axis=1), jnp.concatenate([top, top], axis=0))
+    small = dot(jnp.concatenate([al, ah], axis=1), jnp.concatenate([bh, bl], axis=0))
+    n = b.shape[1]
+    return both[:, :n] + (both[:, n:] + small)
 
 
 def scores_kernel(*refs, width):
     *pieces, q0, q1, q2, q3, out = refs
     ex, qry = lax.axis_index("ex"), lax.axis_index("qry")
     block = q0.shape[1]
-    vec = jnp.concatenate([piece[...] for piece in pieces], axis=0)
+    columns = []
+    for k in range(4):
+        part = pl.ds(pl.multiple_of((ex ^ k) * block, block), block)
+        columns.append(jnp.concatenate([piece[:, part] for piece in pieces], axis=0))
+    vec = jnp.concatenate(columns, axis=1)
     n = vec.shape[0]
     vh, vm, vl = split3(vec)
-    gram = dot(vh, vh, NT) + ((dot(vh, vm, NT) + dot(vm, vh, NT)) + (dot(vm, vm, NT) + dot(vh, vl, NT) + dot(vl, vh, NT)))
+    large = jnp.concatenate([vh, vm], axis=0)
+    quads = dot(large, large, NT)
+    tail = dot(vh, vl, NT)
+    gram = quads[:n, :n] + ((quads[:n, n:] + quads[n:, :n]) + (quads[n:, n:] + (tail + tail.T)))
     gram = gram / n
     row = lax.broadcasted_iota(jnp.int32, (n, n), 0)
     col = lax.broadcasted_iota(jnp.int32, (n, n), 1)
@@ -144,49 +160,47 @@
     root_row = lax.rsqrt(diag_row + damp)
     root_col = lax.rsqrt(diag_col + damp)
     system = (gram + damp * eye) * root_row * root_col
-    size = jnp.max(jnp.sum(jnp.abs(system), axis=0, keepdims=True), axis=1, keepdims=True)
-    inv_size = 1.0 / (0.51 * size)
-    power = eye - system * inv_size
-    series = eye + power
-    power = times(power, power)
-    for k in range(4):
-        both = times(jnp.concatenate([series, power], axis=0), power)
+    square = product(system, system)
+    size = jnp.max(jnp.sum(jnp.abs(square), axis=0, keepdims=True), axis=1, keepdims=True)
+    scale = (1.0 / 0.51) * lax.rsqrt(size)
+    scaled = system * scale
+    power = (eye - 2.0 * scaled) + square * (scale * scale)
+    series = 2.0 * eye - scaled
+    for _ in range(3):
+        both = product(jnp.concatenate([series, power], axis=0), power)
         series = series + both[:n]
         power = both[n:]
-    series = series + times(series, power)
-    inverse = series * inv_size
+    series = (series + product(series, power)) * scale
+
+    wanted = jnp.concatenate([q[...] for q in (q0, q1, q2, q3)], axis=1)
+    crossed = dot(jnp.concatenate([vh, vm, vl], axis=0), wanted, NT)
+    cross = crossed[:n] + (crossed[n:2 * n] + crossed[2 * n:])
+    mine = out.shape[0]
+    groups = lax.axis_size("qry")
+    each = mine // groups
 
     def refine(x):
-        error = eye - dot(system, x, NN, HIGHEST)
-        return x + times(x, error), jnp.max(jnp.abs(error))
-
-    inverse, miss = refine(inverse)
-
-    def again(state):
-        x, _, turns = state
-        x, left = refine(x)
-        return x, left, turns + 1
-
-    inverse, _, _ = lax.while_loop(
-        lambda s: (s[1] > 1e-4) & (s[2] < 16), again, (inverse, miss, jnp.int32(0))
-    )
-
-    cross = None
-    for k, q in enumerate((q0, q1, q2, q3)):
-        start = pl.multiple_of((ex ^ k) * block, block)
-        here = jnp.concatenate([piece[:, pl.ds(start, block)] for piece in pieces], axis=0)
-        hh, hm, hl = split3(here)
-        qb = q[...]
-        term = dot(hh, qb, NT) + dot(hm, qb, NT) + dot(hl, qb, NT)
-        cross = term if cross is None else cross + term
-    groups = lax.axis_size("qry")
-    mine = out.shape[0]
-    each = mine // groups
-    weights = inverse[:mine] * root_row * root_col[:mine]
-    result = dot(weights, cross, NN, HIGHEST)
-    for g, away in enumerate((0, 2, 1, 3)):
-        to = pl.multiple_of((qry ^ away) * each, each)
-        out[pl.ds(to, each), :] = result[g * each:(g + 1) * each]
+        error = eye - product6(system, x)
+        return x + product(x, error), jnp.sum(error * error)
+
+    def store(x):
+        weights = x[:mine] * root_row * root_col[:mine]
+        result = dot(weights, cross, NN, HIGHEST)
+        for g, away in enumerate((0, 2, 1, 3)):
+            to = pl.multiple_of((qry ^ away) * each, each)
+            out[pl.ds(to, each), :] = result[g * each:(g + 1) * each]
+
+    inverse, miss = refine(series)
+    store(inverse)
+
+    @pl.when(miss > 1e-6)
+    def _():
+        def again(state):
+            x, _, turns = state
+            x, left = refine(x)
+            return x, left, turns + 1
+
+        store(lax.while_loop(lambda s: (s[1] > 1e-6) & (s[2] < 16), again, (inverse, miss, jnp.int32(0)))[0])
 
 
 def swap(x, axis, bit):

time: 27.4 us -> 26.2 us (0.956); the launches traced: 27.2 us -> 26.4 us
  Pallas kernels: 10.2 us -> 9.32 us
    pallas_call x1, Pallas kernels: 4.57 us -> 3.72 us  [body_small(): pl.pallas_call(lambda *refs: scores_kernel(*refs, width=width), out_shape...]
where the time goes in v4:
time: 26.2 us; the launch traced here: 26.4 us
  starting transfers between devices  10.2 us (39%)
  Pallas kernels  9.32 us (36%)
  waiting for transfers between devices  6.17 us (24%)
  local copies, waits for them, and re-layouts  0.66 us (3%)
    ppermute x11, starting transfers between devices, swap(): return lax.ppermute(x, axis, [(i, i ^ bit) for i in range(size)])  10.2 us
    ppermute x11, waiting for transfers between devices, swap(): return lax.ppermute(x, axis, [(i, i ^ bit) for i in range(size)])  6.17 us
    pallas_call x1, Pallas kernels, example_vectors(): pl.pallas_call(vectors_kernel, in_specs=[pl.BlockSpec(memory_space=pl.ANY...  5.6 us
    pallas_call x1, Pallas kernels, body_small(): pl.pallas_call(lambda *refs: scores_kernel(*refs, width=width), out_shape...  3.72 us
    unnamed x4, local copies, waits for them, and re-layouts  0.66 us
  transfers between devices with their start and end apart: 11, of which 5 were waited for; matrix products, arithmetic and copies ran while one was open for 0% of the time, Pallas kernels for 21%

profile of v4, /device:TPU:0, one launch (start us, length us, event | category | flops | bytes accessed | tf_op | source)
XLA Modules:
  0.0 26.4 jit_solution(1923806919528405125)
XLA Ops:
  0.0 0.0 copy-start
  0.0 0.5 %collective-permute-start = (bf16[512,256]{1,0:T(8,128)(2,1)}, bf16[512,256]{1,0:T(8,128)(2,1)S(1)}, u32[]{:S(2)}, u32[]{:S(2)}) collective-permute-start(bf16[512,256]{1,0:T(8,128)(2,1)} %refs_8_.1), channel_id=1, source_target_pairs={{0,4},{4,0},{8,12},{12,8},{1,5},{5,1},{9,13},{13,9},{2,6},{6,2},{1... | collective-permute-start | bytes 786440 | tf_op jit(solution)/shard_map/ppermute | solution.py:208
  0.5 2.6 %collective-permute-start.2 = (bf16[512,256]{1,0:T(8,128)(2,1)}, bf16[512,256]{1,0:T(8,128)(2,1)S(1)}, u32[]{:S(2)}, u32[]{:S(2)}) collective-permute-start(bf16[512,256]{1,0:T(8,128)(2,1)} %refs_8_.1), channel_id=1, source_target_pairs={{0,8},{4,12},{8,0},{12,4},{1,9},{5,13},{9,1},{13,5},{2,10},{6,14},... | collective-permute-start | bytes 786440 | tf_op jit(solution)/shard_map/ppermute | solution.py:208
  3.0 0.0 collective-permute-done.refs_9_
  3.0 0.0 copy-start.1
  3.0 0.7 %copy-done.1 = s32[1,9]{1,0:T(1,128)S(1)} copy-done((s32[1,9]{1,0:T(1,128)S(1)}, s32[1,9]{1,0:T(1,128)}, u32[]{:S(2)}) %copy-start.1) | copy-done | bytes 60
  3.7 5.6 %shard_map.64 = f32[8,1024]{1,0:T(8,128)S(1)} custom-call(s32[1,9]{1,0:T(1,128)S(1)} %copy-done.1, bf16[256,14336]{1,0:T(8,128)(2,1)} %hidden, bf16[256,4096]{1,0:T(8,128)(2,1)} %out_grad.1, bf16[32,14336]{1,0:T(8,128)(2,1)} %proj_in.1, bf16[32,4096]{1,0:T(8,128)(2,1)} %proj_out.1), custom_call_target="tpu_custom_call" | custom-call | flops 301989888 | bytes 10616832 | tf_op jit(solution)/shard_map/pallas_call | solution.py:93
  9.3 2.8 %collective-permute-start.1 = (f32[8,1024]{1,0:T(8,128)S(1)}, f32[8,1024]{1,0:T(8,128)S(1)}, u32[]{:S(2)}, u32[]{:S(2)}) collective-permute-start(f32[8,1024]{1,0:T(8,128)S(1)} %shard_map.64), channel_id=1, source_target_pairs={{0,2},{1,3},{2,0},{3,1},{4,6},{5,7},{6,4},{7,5},{8,10},{9,11},{10,... | collective-permute-start | bytes 98312 | tf_op jit(solution)/shard_map/ppermute | solution.py:208
  12.1 2.1 %collective-permute-done.1 = f32[8,1024]{1,0:T(8,128)S(1)} collective-permute-done((f32[8,1024]{1,0:T(8,128)S(1)}, f32[8,1024]{1,0:T(8,128)S(1)}, u32[]{:S(2)}, u32[]{:S(2)}) %collective-permute-start.1) | collective-permute-done | bytes 32800 | tf_op jit(solution)/shard_map/ppermute | solution.py:208
  14.2 0.0 collective-permute-done.2.refs_10_
  14.2 0.1 collective-permute-start.10
  14.3 2.8 %collective-permute-start.7 = (f32[16,1024]{1,0:T(8,128)S(1)}, f32[16,1024]{1,0:T(8,128)S(1)}, u32[]{:S(2)}, u32[]{:S(2)}) collective-permute-start(f32[16,1024]{1,0:T(8,128)S(1)} %pad_maximum_fusion.refs_0_), channel_id=1, source_target_pairs={{0,13},{1,12},{2,15},{3,14},{4,9},{5,8},{6,11},{7,10},{8,5},{9,4},... | collective-permute-start | bytes 196616 | tf_op jit(solution)/shard_map/ppermute | solution.py:208
  17.1 0.2 collective-permute-start.6
  17.3 0.4 %collective-permute-start.3 = (f32[16,1024]{1,0:T(8,128)S(1)}, f32[16,1024]{1,0:T(8,128)S(1)}, u32[]{:S(2)}, u32[]{:S(2)}) collective-permute-start(f32[16,1024]{1,0:T(8,128)S(1)} %pad_maximum_fusion.refs_0_), channel_id=1, source_target_pairs={{0,5},{1,4},{2,7},{3,6},{4,1},{5,0},{6,3},{7,2},{8,13},{9,12},{10,... | collective-permute-start | bytes 196616 | tf_op jit(solution)/shard_map/ppermute | solution.py:208
  17.6 0.4 %collective-permute-start.5 = (f32[16,1024]{1,0:T(8,128)S(1)}, f32[16,1024]{1,0:T(8,128)S(1)}, u32[]{:S(2)}, u32[]{:S(2)}) collective-permute-start(f32[16,1024]{1,0:T(8,128)S(1)} %pad_maximum_fusion.refs_0_), channel_id=1, source_target_pairs={{0,4},{1,5},{2,6},{3,7},{4,0},{5,1},{6,2},{7,3},{8,12},{9,13},{10,... | collective-permute-start | bytes 196616 | tf_op jit(solution)/shard_map/ppermute | solution.py:208
  18.0 1.5 %collective-permute-done.7.refs_5_ = f32[16,1024]{1,0:T(8,128)S(1)} collective-permute-done((f32[16,1024]{1,0:T(8,128)S(1)}, f32[16,1024]{1,0:T(8,128)S(1)}, u32[]{:S(2)}, u32[]{:S(2)}) %collective-permute-start.7) | collective-permute-done | bytes 65568 | tf_op jit(solution)/shard_map/ppermute | solution.py:208
  19.5 0.0 collective-permute-start.9
  19.5 1.7 %collective-permute-done.6.refs_4_ = f32[16,1024]{1,0:T(8,128)S(1)} collective-permute-done((f32[16,1024]{1,0:T(8,128)S(1)}, f32[16,1024]{1,0:T(8,128)S(1)}, u32[]{:S(2)}, u32[]{:S(2)}) %collective-permute-start.6) | collective-permute-done | bytes 65568 | tf_op jit(solution)/shard_map/ppermute | solution.py:208
  21.2 0.1 collective-permute-start.8
  21.3 0.0 collective-permute-done.3.refs_2_
  21.3 0.4 %collective-permute-start.4 = (f32[16,1024]{1,0:T(8,128)S(1)}, f32[16,1024]{1,0:T(8,128)S(1)}, u32[]{:S(2)}, u32[]{:S(2)}) collective-permute-start(f32[16,1024]{1,0:T(8,128)S(1)} %collective-permute-done.3.refs_2_), channel_id=1, source_target_pairs={{0,4},{1,5},{2,6},{3,7},{4,0},{5,1},{6,2},{7,3},{8,12},{9,13},{10,... | collective-permute-start | bytes 196616 | tf_op jit(solution)/shard_map/ppermute | solution.py:208
  21.7 0.0 collective-permute-done.5.refs_3_
  21.7 0.0 collective-permute-done.9.refs_7_
  21.7 0.7 %collective-permute-done.8.refs_6_ = f32[16,1024]{1,0:T(8,128)S(1)} collective-permute-done((f32[16,1024]{1,0:T(8,128)S(1)}, f32[16,1024]{1,0:T(8,128)S(1)}, u32[]{:S(2)}, u32[]{:S(2)}) %collective-permute-start.8) | collective-permute-done | bytes 65568 | tf_op jit(solution)/shard_map/ppermute | solution.py:208
  22.5 0.2 collective-permute-done.4.refs_1_
  22.6 0.0 collective-permute-done.10.refs_11_
  22.6 0.0 copy-done
  22.6 3.7 %shard_map.65 = f32[32,512]{1,0:T(8,128)} custom-call(f32[16,1024]{1,0:T(8,128)S(1)} %pad_maximum_fusion.refs_0_, f32[16,1024]{1,0:T(8,128)S(1)} %collective-permute-done.4.refs_1_, f32[16,1024]{1,0:T(8,128)S(1)} %collective-permute-done.3.refs_2_, f32[16,1024]{1,0:T(8,128)S(1)} %collective-permute-done.5.refs_3_, ...), custom_call_target="tpu_custom_call" | custom-call | tf_op jit(solution)/shard_map/pallas_call | solution.py:232
  (1 shorter events, 0.0 us)
Async XLA Ops:
  0.0 22.6 %copy-start = (bf16[512,256]{1,0:T(8,128)(2,1)S(1)}, bf16[512,256]{1,0:T(8,128)(2,1)}, u32[]{:S(2)}) copy-start(bf16[512,256]{1,0:T(8,128)(2,1)} %refs_8_.1) | copy-start | bytes 786436
  0.0 3.0 %collective-permute-start = (bf16[512,256]{1,0:T(8,128)(2,1)}, bf16[512,256]{1,0:T(8,128)(2,1)S(1)}, u32[]{:S(2)}, u32[]{:S(2)}) collective-permute-start(bf16[512,256]{1,0:T(8,128)(2,1)} %refs_8_.1), channel_id=1, source_target_pairs={{0,4},{4,0},{8,12},{12,8},{1,5},{5,1},{9,13},{13,9},{2,6},{6,2},{1... | collective-permute-start | bytes 786440 | tf_op jit(solution)/shard_map/ppermute | solution.py:208
  0.5 13.7 %collective-permute-start.2 = (bf16[512,256]{1,0:T(8,128)(2,1)}, bf16[512,256]{1,0:T(8,128)(2,1)S(1)}, u32[]{:S(2)}, u32[]{:S(2)}) collective-permute-start(bf16[512,256]{1,0:T(8,128)(2,1)} %refs_8_.1), channel_id=1, source_target_pairs={{0,8},{4,12},{8,0},{12,4},{1,9},{5,13},{9,1},{13,5},{2,10},{6,14},... | collective-permute-start | bytes 786440 | tf_op jit(solution)/shard_map/ppermute | solution.py:208
  3.0 0.7 %copy-start.1 = (s32[1,9]{1,0:T(1,128)S(1)}, s32[1,9]{1,0:T(1,128)}, u32[]{:S(2)}) copy-start(s32[1,9]{1,0:T(1,128)} %lengths.1) | copy-start | bytes 112
  9.3 4.9 %collective-permute-start.1 = (f32[8,1024]{1,0:T(8,128)S(1)}, f32[8,1024]{1,0:T(8,128)S(1)}, u32[]{:S(2)}, u32[]{:S(2)}) collective-permute-start(f32[8,1024]{1,0:T(8,128)S(1)} %shard_map.64), channel_id=1, source_target_pairs={{0,2},{1,3},{2,0},{3,1},{4,6},{5,7},{6,4},{7,5},{8,10},{9,11},{10,... | collective-permute-start | bytes 98312 | tf_op jit(solution)/shard_map/ppermute | solution.py:208
  14.2 8.4 %collective-permute-start.10 = (bf16[512,256]{1,0:T(8,128)(2,1)S(1)}, bf16[512,256]{1,0:T(8,128)(2,1)S(1)}, u32[]{:S(2)}, u32[]{:S(2)}) collective-permute-start(bf16[512,256]{1,0:T(8,128)(2,1)S(1)} %collective-permute-done.2.refs_10_), channel_id=1, source_target_pairs={{0,4},{4,0},{8,12},{12,8},{1,5},{5,1},{9,13},{13,9},{2,6},{6,2},{1... | collective-permute-start | bytes 786440 | tf_op jit(solution)/shard_map/ppermute | solution.py:208
  14.3 5.2 %collective-permute-start.7 = (f32[16,1024]{1,0:T(8,128)S(1)}, f32[16,1024]{1,0:T(8,128)S(1)}, u32[]{:S(2)}, u32[]{:S(2)}) collective-permute-start(f32[16,1024]{1,0:T(8,128)S(1)} %pad_maximum_fusion.refs_0_), channel_id=1, source_target_pairs={{0,13},{1,12},{2,15},{3,14},{4,9},{5,8},{6,11},{7,10},{8,5},{9,4},... | collective-permute-start | bytes 196616 | tf_op jit(solution)/shard_map/ppermute | solution.py:208
  17.1 4.1 %collective-permute-start.6 = (f32[16,1024]{1,0:T(8,128)S(1)}, f32[16,1024]{1,0:T(8,128)S(1)}, u32[]{:S(2)}, u32[]{:S(2)}) collective-permute-start(f32[16,1024]{1,0:T(8,128)S(1)} %pad_maximum_fusion.refs_0_), channel_id=1, source_target_pairs={{0,12},{1,13},{2,14},{3,15},{4,8},{5,9},{6,10},{7,11},{8,4},{9,5},... | collective-permute-start | bytes 196616 | tf_op jit(solution)/shard_map/ppermute | solution.py:208
  17.3 4.1 %collective-permute-start.3 = (f32[16,1024]{1,0:T(8,128)S(1)}, f32[16,1024]{1,0:T(8,128)S(1)}, u32[]{:S(2)}, u32[]{:S(2)}) collective-permute-start(f32[16,1024]{1,0:T(8,128)S(1)} %pad_maximum_fusion.refs_0_), channel_id=1, source_target_pairs={{0,5},{1,4},{2,7},{3,6},{4,1},{5,0},{6,3},{7,2},{8,13},{9,12},{10,... | collective-permute-start | bytes 196616 | tf_op jit(solution)/shard_map/ppermute | solution.py:208
  17.6 4.1 %collective-permute-start.5 = (f32[16,1024]{1,0:T(8,128)S(1)}, f32[16,1024]{1,0:T(8,128)S(1)}, u32[]{:S(2)}, u32[]{:S(2)}) collective-permute-start(f32[16,1024]{1,0:T(8,128)S(1)} %pad_maximum_fusion.refs_0_), channel_id=1, source_target_pairs={{0,4},{1,5},{2,6},{3,7},{4,0},{5,1},{6,2},{7,3},{8,12},{9,13},{10,... | collective-permute-start | bytes 196616 | tf_op jit(solution)/shard_map/ppermute | solution.py:208
  19.5 2.3 %collective-permute-start.9 = (f32[16,1024]{1,0:T(8,128)S(1)}, f32[16,1024]{1,0:T(8,128)S(1)}, u32[]{:S(2)}, u32[]{:S(2)}) collective-permute-start(f32[16,1024]{1,0:T(8,128)S(1)} %collective-permute-done.7.refs_5_), channel_id=1, source_target_pairs={{0,4},{1,5},{2,6},{3,7},{4,0},{5,1},{6,2},{7,3},{8,12},{9,13},{10,... | collective-permute-start | bytes 196616 | tf_op jit(solution)/shard_map/ppermute | solution.py:208
  21.2 1.3 %collective-permute-start.8 = (f32[16,1024]{1,0:T(8,128)S(1)}, f32[16,1024]{1,0:T(8,128)S(1)}, u32[]{:S(2)}, u32[]{:S(2)}) collective-permute-start(f32[16,1024]{1,0:T(8,128)S(1)} %collective-permute-done.6.refs_4_), channel_id=1, source_target_pairs={{0,4},{1,5},{2,6},{3,7},{4,0},{5,1},{6,2},{7,3},{8,12},{9,13},{10,... | collective-permute-start | bytes 196616 | tf_op jit(solution)/shard_map/ppermute | solution.py:208
  21.3 1.3 %collective-permute-start.4 = (f32[16,1024]{1,0:T(8,128)S(1)}, f32[16,1024]{1,0:T(8,128)S(1)}, u32[]{:S(2)}, u32[]{:S(2)}) collective-permute-start(f32[16,1024]{1,0:T(8,128)S(1)} %collective-permute-done.3.refs_2_), channel_id=1, source_target_pairs={{0,4},{1,5},{2,6},{3,7},{4,0},{5,1},{6,2},{7,3},{8,12},{9,13},{10,... | collective-permute-start | bytes 196616 | tf_op jit(solution)/shard_map/ppermute | solution.py:208

commit v5 on v4

--- a/solution.py
+++ b/solution.py
@@ -90,9 +90,10 @@
     width_out = proj_out.shape[1]
     tokens = hidden.shape[0]
     examples = lengths.shape[1] - 1
+    operands = (lengths, hidden, out_grad, proj_in, proj_out)
     return pl.pallas_call(
         vectors_kernel,
-        in_specs=[pl.BlockSpec(memory_space=pl.ANY)] * 5,
+        in_specs=[pl.BlockSpec(memory_space=pltpu.HBM)] * 5,
         out_specs=pl.BlockSpec(memory_space=pltpu.VMEM),
         out_shape=jax.ShapeDtypeStruct((examples, rank * rank), F32),
         scratch_shapes=[
@@ -104,13 +105,13 @@
             pltpu.VMEM((rank * examples, 128), F32),
             pltpu.SemaphoreType.DMA((STEPS + 1, 4)),
         ],
-        compiler_params=pltpu.CompilerParams(vmem_limit_bytes=55104 * 1024),
+        compiler_params=pltpu.CompilerParams(vmem_limit_bytes=24 * 2**20),
         cost_estimate=pl.CostEstimate(
             flops=2 * tokens * rank * (features + width_out),
             bytes_accessed=2 * (tokens + rank) * (features + width_out),
             transcendentals=0,
         ),
-    )(lengths, hidden, out_grad, proj_in, proj_out)
+    )(*(pltpu.with_memory_space_constraint(x, pltpu.HBM) for x in operands))
 
 
 def product(a, b):
@@ -134,14 +135,17 @@
     return both[:, :n] + (both[:, n:] + small)
 
 
-def scores_kernel(*refs, width):
+def scores_kernel(*refs, width, rows):
     *pieces, q0, q1, q2, q3, out = refs
     ex, qry = lax.axis_index("ex"), lax.axis_index("qry")
     block = q0.shape[1]
+    mine = out.shape[0]
+    groups = lax.axis_size("qry")
+    each = mine // groups
     columns = []
     for k in range(4):
         part = pl.ds(pl.multiple_of((ex ^ k) * block, block), block)
-        columns.append(jnp.concatenate([piece[:, part] for piece in pieces], axis=0))
+        columns.append(jnp.concatenate([pieces[p][half * each:(half + 1) * each, part] for _, p, half in rows], axis=0))
     vec = jnp.concatenate(columns, axis=1)
     n = vec.shape[0]
     vh, vm, vl = split3(vec)
@@ -175,9 +179,6 @@
     wanted = jnp.concatenate([q[...] for q in (q0, q1, q2, q3)], axis=1)
     crossed = dot(jnp.concatenate([vh, vm, vl], axis=0), wanted, NT)
     cross = crossed[:n] + (crossed[n:2 * n] + crossed[2 * n:])
-    mine = out.shape[0]
-    groups = lax.axis_size("qry")
-    each = mine // groups
 
     def refine(x):
         error = eye - product6(system, x)
@@ -186,9 +187,9 @@
     def store(x):
         weights = x[:mine] * root_row * root_col[:mine]
         result = dot(weights, cross, NN, HIGHEST)
-        for g, away in enumerate((0, 2, 1, 3)):
+        for away in range(groups):
             to = pl.multiple_of((qry ^ away) * each, each)
-            out[pl.ds(to, each), :] = result[g * each:(g + 1) * each]
+            out[pl.ds(to, each), :] = result[away * each:(away + 1) * each]
 
     inverse, miss = refine(series)
     store(inverse)
@@ -210,6 +211,7 @@
 
 def body_small(hidden, out_grad, proj_in, proj_out, lengths, queries):
     width = proj_in.shape[0] * proj_in.shape[0]
+    examples = lengths.shape[1] - 1
     per = lax.axis_size("qry")
     core, y = per, 2 * per
 
@@ -218,24 +220,26 @@
 
     q1 = swap(queries, "ex", 1)
     q2 = swap(queries, "ex", 2)
-    hidden, q1 = lax.optimization_barrier((hidden, q1))
     vectors = example_vectors(hidden, out_grad, proj_in, proj_out, lengths)
-    own = jnp.concatenate([vectors, cross(vectors, 2)], axis=0)
-    own, q1, q2 = lax.optimization_barrier((own, q1, q2))
-    here = (own, cross(own, core + 1), cross(own, core + y), cross(own, core + y + 1))
-    there = tuple(cross(piece, core) for piece in here)
+    first = core + 2
+    own = jnp.concatenate([vectors, cross(vectors, first)], axis=0)
+    own, q2 = lax.optimization_barrier((own, q2))
+    pieces = {0: own}
+    for bits in (core + y, core + 1, core + y + 1):
+        pieces[bits] = cross(own, bits)
+    for bits in tuple(pieces):
+        pieces[bits ^ core] = cross(pieces[bits], core)
     q3 = swap(q2, "ex", 1)
-    pieces = (here[0], there[1], here[1], there[0], *here[2:], *there[2:])
-    total = sum(piece.shape[0] for piece in pieces)
-    mine = total // lax.axis_size("ex")
+    rows = sorted((bits ^ (first * half), k, half) for k, bits in enumerate(pieces) for half in range(2))
+    mine = per * examples
     count = queries.shape[0]
     return pl.pallas_call(
-        lambda *refs: scores_kernel(*refs, width=width),
+        lambda *refs: scores_kernel(*refs, width=width, rows=rows),
         out_shape=jax.ShapeDtypeStruct((mine, count), F32),
         in_specs=[pl.BlockSpec(memory_space=pltpu.VMEM)] * (len(pieces) + 4),
         out_specs=pl.BlockSpec(memory_space=pltpu.VMEM),
         compiler_params=pltpu.CompilerParams(vmem_limit_bytes=24 * 2**20),
-    )(*pieces, queries, q1, q2, q3)
+    )(*pieces.values(), queries, q1, q2, q3)
 
 
 def body_large(hidden, out_grad, proj_in, proj_out, lengths, queries):

time: 26.2 us -> 25 us (0.954); the launches traced: 26.4 us -> 24.9 us
  waiting for transfers between devices: 6.17 us -> 5.31 us
  local copies, waits for them, and re-layouts: 0.66 us -> 0.01 us
    ppermute x11, waiting for transfers between devices: 6.17 us -> 5.31 us  [swap(): return lax.ppermute(x, axis, [(i, i ^ bit) for i in range(size)])]
    unnamed x4 -> x2, local copies, waits for them, and re-layouts: 0.66 us -> 0.01 us
  transfers between devices with their start and end apart: 11 -> 11, of which waited for: 5 -> 6; matrix products, arithmetic and copies ran while one was open for 0% -> 0% of each run, Pallas kernels for 21% -> 22%
where the time goes in v5:
time: 25 us; the launch traced here: 24.9 us
  starting transfers between devices  10.2 us (41%)
  Pallas kernels  9.32 us (37%)
  waiting for transfers between devices  5.31 us (21%)
    ppermute x11, starting transfers between devices, swap(): return lax.ppermute(x, axis, [(i, i ^ bit) for i in range(size)])  10.2 us
    pallas_call x1, Pallas kernels, example_vectors(): pl.pallas_call(vectors_kernel, in_specs=[pl.BlockSpec(memory_space=pltpu....  5.6 us
    ppermute x11, waiting for transfers between devices, swap(): return lax.ppermute(x, axis, [(i, i ^ bit) for i in range(size)])  5.31 us
    pallas_call x1, Pallas kernels, body_small(): pl.pallas_call(lambda *refs: scores_kernel(*refs, width=width, rows=rows)...  3.72 us
  transfers between devices with their start and end apart: 11, of which 6 were waited for; matrix products, arithmetic and copies ran while one was open for 0% of the time, Pallas kernels for 22%

profile of v5, /device:TPU:0, one launch (start us, length us, event | category | flops | bytes accessed | tf_op | source)
XLA Modules:
  0.0 24.9 jit_solution(1748979295808965782)
XLA Ops:
  0.0 0.0 copy-start
  0.0 3.0 %collective-permute-start.1 = (bf16[512,256]{1,0:T(8,128)(2,1)}, bf16[512,256]{1,0:T(8,128)(2,1)S(1)}, u32[]{:S(2)}, u32[]{:S(2)}) collective-permute-start(bf16[512,256]{1,0:T(8,128)(2,1)} %refs_8_.1), channel_id=1, source_target_pairs={{0,8},{4,12},{8,0},{12,4},{1,9},{5,13},{9,1},{13,5},{2,10},{6,14},... | collective-permute-start | bytes 786440 | tf_op jit(solution)/shard_map/ppermute | solution.py:209
  3.0 5.6 %shard_map.64 = f32[8,1024]{1,0:T(8,128)S(1)} custom-call(s32[1,9]{1,0:T(1,128)} %lengths.1, bf16[256,14336]{1,0:T(8,128)(2,1)} %hidden.1, bf16[256,4096]{1,0:T(8,128)(2,1)} %out_grad.1, bf16[32,14336]{1,0:T(8,128)(2,1)} %proj_in.1, bf16[32,4096]{1,0:T(8,128)(2,1)} %proj_out.1), custom_call_target="tpu_custom_call" | custom-call | flops 301989888 | bytes 10616832 | tf_op jit(solution)/shard_map/pallas_call | solution.py:94
  8.6 1.8 %collective-permute-start = (f32[8,1024]{1,0:T(8,128)S(1)}, f32[8,1024]{1,0:T(8,128)S(1)}, u32[]{:S(2)}, u32[]{:S(2)}) collective-permute-start(f32[8,1024]{1,0:T(8,128)S(1)} %shard_map.64), channel_id=1, source_target_pairs={{0,6},{1,7},{2,4},{3,5},{4,2},{5,3},{6,0},{7,1},{8,14},{9,15},{10,... | collective-permute-start | bytes 98312 | tf_op jit(solution)/shard_map/ppermute | solution.py:209
  10.4 0.0 copy-done
  10.4 1.0 %collective-permute-start.9 = (bf16[512,256]{1,0:T(8,128)(2,1)S(1)}, bf16[512,256]{1,0:T(8,128)(2,1)S(1)}, u32[]{:S(2)}, u32[]{:S(2)}) collective-permute-start(bf16[512,256]{1,0:T(8,128)(2,1)S(1)} %copy-done), channel_id=1, source_target_pairs={{0,4},{4,0},{8,12},{12,8},{1,5},{5,1},{9,13},{13,9},{2,6},{6,2},{1... | collective-permute-start | bytes 786440 | tf_op jit(solution)/shard_map/ppermute | solution.py:209
  11.4 1.6 %collective-permute-done = f32[8,1024]{1,0:T(8,128)S(1)} collective-permute-done((f32[8,1024]{1,0:T(8,128)S(1)}, f32[8,1024]{1,0:T(8,128)S(1)}, u32[]{:S(2)}, u32[]{:S(2)}) %collective-permute-start) | collective-permute-done | bytes 32800 | tf_op jit(solution)/shard_map/ppermute | solution.py:209
  13.0 0.0 collective-permute-done.1.refs_10_
  13.0 0.2 collective-permute-start.10
  13.2 1.5 %collective-permute-start.4 = (f32[16,1024]{1,0:T(8,128)S(1)}, f32[16,1024]{1,0:T(8,128)S(1)}, u32[]{:S(2)}, u32[]{:S(2)}) collective-permute-start(f32[16,1024]{1,0:T(8,128)S(1)} %pad_maximum_fusion.refs_0_), channel_id=1, source_target_pairs={{0,13},{1,12},{2,15},{3,14},{4,9},{5,8},{6,11},{7,10},{8,5},{9,4},... | collective-permute-start | bytes 196616 | tf_op jit(solution)/shard_map/ppermute | solution.py:209
  14.7 0.1 collective-permute-start.3
  14.8 1.6 %collective-permute-start.2 = (f32[16,1024]{1,0:T(8,128)S(1)}, f32[16,1024]{1,0:T(8,128)S(1)}, u32[]{:S(2)}, u32[]{:S(2)}) collective-permute-start(f32[16,1024]{1,0:T(8,128)S(1)} %pad_maximum_fusion.refs_0_), channel_id=1, source_target_pairs={{0,12},{1,13},{2,14},{3,15},{4,8},{5,9},{6,10},{7,11},{8,4},{9,5},... | collective-permute-start | bytes 196616 | tf_op jit(solution)/shard_map/ppermute | solution.py:209
  16.4 0.0 collective-permute-done.9.refs_9_
  16.4 0.2 collective-permute-start.5
  16.6 1.5 %collective-permute-done.4.refs_3_ = f32[16,1024]{1,0:T(8,128)S(1)} collective-permute-done((f32[16,1024]{1,0:T(8,128)S(1)}, f32[16,1024]{1,0:T(8,128)S(1)}, u32[]{:S(2)}, u32[]{:S(2)}) %collective-permute-start.4) | collective-permute-done | bytes 65568 | tf_op jit(solution)/shard_map/ppermute | solution.py:209
  18.1 0.4 %collective-permute-start.8 = (f32[16,1024]{1,0:T(8,128)S(1)}, f32[16,1024]{1,0:T(8,128)S(1)}, u32[]{:S(2)}, u32[]{:S(2)}) collective-permute-start(f32[16,1024]{1,0:T(8,128)S(1)} %collective-permute-done.4.refs_3_), channel_id=1, source_target_pairs={{0,4},{1,5},{2,6},{3,7},{4,0},{5,1},{6,2},{7,3},{8,12},{9,13},{10,... | collective-permute-start | bytes 196616 | tf_op jit(solution)/shard_map/ppermute | solution.py:209
  18.4 0.4 %collective-permute-done.3.refs_2_ = f32[16,1024]{1,0:T(8,128)S(1)} collective-permute-done((f32[16,1024]{1,0:T(8,128)S(1)}, f32[16,1024]{1,0:T(8,128)S(1)}, u32[]{:S(2)}, u32[]{:S(2)}) %collective-permute-start.3) | collective-permute-done | bytes 65568 | tf_op jit(solution)/shard_map/ppermute | solution.py:209
  18.8 0.4 %collective-permute-start.7 = (f32[16,1024]{1,0:T(8,128)S(1)}, f32[16,1024]{1,0:T(8,128)S(1)}, u32[]{:S(2)}, u32[]{:S(2)}) collective-permute-start(f32[16,1024]{1,0:T(8,128)S(1)} %collective-permute-done.3.refs_2_), channel_id=1, source_target_pairs={{0,4},{1,5},{2,6},{3,7},{4,0},{5,1},{6,2},{7,3},{8,12},{9,13},{10,... | collective-permute-start | bytes 196616 | tf_op jit(solution)/shard_map/ppermute | solution.py:209
  19.2 0.7 %collective-permute-done.2.refs_1_ = f32[16,1024]{1,0:T(8,128)S(1)} collective-permute-done((f32[16,1024]{1,0:T(8,128)S(1)}, f32[16,1024]{1,0:T(8,128)S(1)}, u32[]{:S(2)}, u32[]{:S(2)}) %collective-permute-start.2) | collective-permute-done | bytes 65568 | tf_op jit(solution)/shard_map/ppermute | solution.py:209
  19.9 0.1 collective-permute-start.6
  20.0 0.0 collective-permute-done.5.refs_4_
  20.0 0.0 collective-permute-done.8.refs_7_
  20.0 0.1 collective-permute-done.7.refs_6_
  20.1 1.0 %collective-permute-done.6.refs_5_ = f32[16,1024]{1,0:T(8,128)S(1)} collective-permute-done((f32[16,1024]{1,0:T(8,128)S(1)}, f32[16,1024]{1,0:T(8,128)S(1)}, u32[]{:S(2)}, u32[]{:S(2)}) %collective-permute-start.6) | collective-permute-done | bytes 65568 | tf_op jit(solution)/shard_map/ppermute | solution.py:209
  21.1 0.0 collective-permute-done.10.refs_11_
  21.1 3.7 %shard_map.65 = f32[32,512]{1,0:T(8,128)} custom-call(f32[16,1024]{1,0:T(8,128)S(1)} %pad_maximum_fusion.refs_0_, f32[16,1024]{1,0:T(8,128)S(1)} %collective-permute-done.2.refs_1_, f32[16,1024]{1,0:T(8,128)S(1)} %collective-permute-done.3.refs_2_, f32[16,1024]{1,0:T(8,128)S(1)} %collective-permute-done.4.refs_3_, ...), custom_call_target="tpu_custom_call" | custom-call | tf_op jit(solution)/shard_map/pallas_call | solution.py:236
  (1 shorter events, 0.0 us)
Async XLA Ops:
  0.0 10.4 %copy-start = (bf16[512,256]{1,0:T(8,128)(2,1)S(1)}, bf16[512,256]{1,0:T(8,128)(2,1)}, u32[]{:S(2)}) copy-start(bf16[512,256]{1,0:T(8,128)(2,1)} %refs_8_.1) | copy-start | bytes 786436
  0.0 13.0 %collective-permute-start.1 = (bf16[512,256]{1,0:T(8,128)(2,1)}, bf16[512,256]{1,0:T(8,128)(2,1)S(1)}, u32[]{:S(2)}, u32[]{:S(2)}) collective-permute-start(bf16[512,256]{1,0:T(8,128)(2,1)} %refs_8_.1), channel_id=1, source_target_pairs={{0,8},{4,12},{8,0},{12,4},{1,9},{5,13},{9,1},{13,5},{2,10},{6,14},... | collective-permute-start | bytes 786440 | tf_op jit(solution)/shard_map/ppermute | solution.py:209
  8.6 4.4 %collective-permute-start = (f32[8,1024]{1,0:T(8,128)S(1)}, f32[8,1024]{1,0:T(8,128)S(1)}, u32[]{:S(2)}, u32[]{:S(2)}) collective-permute-start(f32[8,1024]{1,0:T(8,128)S(1)} %shard_map.64), channel_id=1, source_target_pairs={{0,6},{1,7},{2,4},{3,5},{4,2},{5,3},{6,0},{7,1},{8,14},{9,15},{10,... | collective-permute-start | bytes 98312 | tf_op jit(solution)/shard_map/ppermute | solution.py:209
  10.4 6.0 %collective-permute-start.9 = (bf16[512,256]{1,0:T(8,128)(2,1)S(1)}, bf16[512,256]{1,0:T(8,128)(2,1)S(1)}, u32[]{:S(2)}, u32[]{:S(2)}) collective-permute-start(bf16[512,256]{1,0:T(8,128)(2,1)S(1)} %copy-done), channel_id=1, source_target_pairs={{0,4},{4,0},{8,12},{12,8},{1,5},{5,1},{9,13},{13,9},{2,6},{6,2},{1... | collective-permute-start | bytes 786440 | tf_op jit(solution)/shard_map/ppermute | solution.py:209
  13.0 8.1 %collective-permute-start.10 = (bf16[512,256]{1,0:T(8,128)(2,1)S(1)}, bf16[512,256]{1,0:T(8,128)(2,1)S(1)}, u32[]{:S(2)}, u32[]{:S(2)}) collective-permute-start(bf16[512,256]{1,0:T(8,128)(2,1)S(1)} %collective-permute-done.1.refs_10_), channel_id=1, source_target_pairs={{0,4},{4,0},{8,12},{12,8},{1,5},{5,1},{9,13},{13,9},{2,6},{6,2},{1... | collective-permute-start | bytes 786440 | tf_op jit(solution)/shard_map/ppermute | solution.py:209
  13.2 4.9 %collective-permute-start.4 = (f32[16,1024]{1,0:T(8,128)S(1)}, f32[16,1024]{1,0:T(8,128)S(1)}, u32[]{:S(2)}, u32[]{:S(2)}) collective-permute-start(f32[16,1024]{1,0:T(8,128)S(1)} %pad_maximum_fusion.refs_0_), channel_id=1, source_target_pairs={{0,13},{1,12},{2,15},{3,14},{4,9},{5,8},{6,11},{7,10},{8,5},{9,4},... | collective-permute-start | bytes 196616 | tf_op jit(solution)/shard_map/ppermute | solution.py:209
  14.7 4.1 %collective-permute-start.3 = (f32[16,1024]{1,0:T(8,128)S(1)}, f32[16,1024]{1,0:T(8,128)S(1)}, u32[]{:S(2)}, u32[]{:S(2)}) collective-permute-start(f32[16,1024]{1,0:T(8,128)S(1)} %pad_maximum_fusion.refs_0_), channel_id=1, source_target_pairs={{0,5},{1,4},{2,7},{3,6},{4,1},{5,0},{6,3},{7,2},{8,13},{9,12},{10,... | collective-permute-start | bytes 196616 | tf_op jit(solution)/shard_map/ppermute | solution.py:209
  14.8 5.1 %collective-permute-start.2 = (f32[16,1024]{1,0:T(8,128)S(1)}, f32[16,1024]{1,0:T(8,128)S(1)}, u32[]{:S(2)}, u32[]{:S(2)}) collective-permute-start(f32[16,1024]{1,0:T(8,128)S(1)} %pad_maximum_fusion.refs_0_), channel_id=1, source_target_pairs={{0,12},{1,13},{2,14},{3,15},{4,8},{5,9},{6,10},{7,11},{8,4},{9,5},... | collective-permute-start | bytes 196616 | tf_op jit(solution)/shard_map/ppermute | solution.py:209
  16.4 3.6 %collective-permute-start.5 = (f32[16,1024]{1,0:T(8,128)S(1)}, f32[16,1024]{1,0:T(8,128)S(1)}, u32[]{:S(2)}, u32[]{:S(2)}) collective-permute-start(f32[16,1024]{1,0:T(8,128)S(1)} %pad_maximum_fusion.refs_0_), channel_id=1, source_target_pairs={{0,4},{1,5},{2,6},{3,7},{4,0},{5,1},{6,2},{7,3},{8,12},{9,13},{10,... | collective-permute-start | bytes 196616 | tf_op jit(solution)/shard_map/ppermute | solution.py:209
  18.1 1.9 %collective-permute-start.8 = (f32[16,1024]{1,0:T(8,128)S(1)}, f32[16,1024]{1,0:T(8,128)S(1)}, u32[]{:S(2)}, u32[]{:S(2)}) collective-permute-start(f32[16,1024]{1,0:T(8,128)S(1)} %collective-permute-done.4.refs_3_), channel_id=1, source_target_pairs={{0,4},{1,5},{2,6},{3,7},{4,0},{5,1},{6,2},{7,3},{8,12},{9,13},{10,... | collective-permute-start | bytes 196616 | tf_op jit(solution)/shard_map/ppermute | solution.py:209
  18.8 1.3 %collective-permute-start.7 = (f32[16,1024]{1,0:T(8,128)S(1)}, f32[16,1024]{1,0:T(8,128)S(1)}, u32[]{:S(2)}, u32[]{:S(2)}) collective-permute-start(f32[16,1024]{1,0:T(8,128)S(1)} %collective-permute-done.3.refs_2_), channel_id=1, source_target_pairs={{0,4},{1,5},{2,6},{3,7},{4,0},{5,1},{6,2},{7,3},{8,12},{9,13},{10,... | collective-permute-start | bytes 196616 | tf_op jit(solution)/shard_map/ppermute | solution.py:209
  19.9 1.3 %collective-permute-start.6 = (f32[16,1024]{1,0:T(8,128)S(1)}, f32[16,1024]{1,0:T(8,128)S(1)}, u32[]{:S(2)}, u32[]{:S(2)}) collective-permute-start(f32[16,1024]{1,0:T(8,128)S(1)} %collective-permute-done.2.refs_1_), channel_id=1, source_target_pairs={{0,4},{1,5},{2,6},{3,7},{4,0},{5,1},{6,2},{7,3},{8,12},{9,13},{10,... | collective-permute-start | bytes 196616 | tf_op jit(solution)/shard_map/ppermute | solution.py:209

commit v6 on v5

--- a/solution.py
+++ b/solution.py
@@ -157,10 +157,9 @@
     row = lax.broadcasted_iota(jnp.int32, (n, n), 0)
     col = lax.broadcasted_iota(jnp.int32, (n, n), 1)
     eye = jnp.where(row == col, 1.0, 0.0).astype(F32)
-    diag = gram * eye
-    diag_row = jnp.sum(diag, axis=0, keepdims=True)
-    diag_col = jnp.sum(diag, axis=1, keepdims=True)
-    damp = 0.1 * jnp.sum(diag_row, axis=1, keepdims=True) / width + 1e-05
+    diag_col = jnp.sum(vec * vec, axis=1, keepdims=True) / n
+    diag_row = jnp.sum(eye * diag_col, axis=0, keepdims=True)
+    damp = 0.1 * jnp.sum(diag_col, axis=0, keepdims=True) / width + 1e-05
     root_row = lax.rsqrt(diag_row + damp)
     root_col = lax.rsqrt(diag_col + damp)
     system = (gram + damp * eye) * root_row * root_col

time: 25 us -> 24.3 us (0.972)
  Pallas kernels: 9.32 us -> 8.61 us
    pallas_call x1, Pallas kernels: 3.72 us -> 3.02 us  [body_small(): pl.pallas_call(lambda *refs: scores_kernel(*refs, width=width, rows=rows)...]
  transfers between devices with their start and end apart: 11 -> 11, of which waited for: 6 -> 6; matrix products, arithmetic and copies ran while one was open for 0% -> 0% of each run, Pallas kernels for 22% -> 23%
where the time goes in v6:
time: 24.3 us; the launch traced here: 24.2 us
  starting transfers between devices  10.2 us (42%)
  Pallas kernels  8.61 us (35%)
  waiting for transfers between devices  5.31 us (22%)
    ppermute x11, starting transfers between devices, swap(): return lax.ppermute(x, axis, [(i, i ^ bit) for i in range(size)])  10.2 us
    pallas_call x1, Pallas kernels, example_vectors(): pl.pallas_call(vectors_kernel, in_specs=[pl.BlockSpec(memory_space=pltpu....  5.6 us
    ppermute x11, waiting for transfers between devices, swap(): return lax.ppermute(x, axis, [(i, i ^ bit) for i in range(size)])  5.31 us
    pallas_call x1, Pallas kernels, body_small(): pl.pallas_call(lambda *refs: scores_kernel(*refs, width=width, rows=rows)...  3.02 us
  transfers between devices with their start and end apart: 11, of which 6 were waited for; matrix products, arithmetic and copies ran while one was open for 0% of the time, Pallas kernels for 23%

profile of v6, /device:TPU:0, one launch (start us, length us, event | category | flops | bytes accessed | tf_op | source)
XLA Modules:
  0.0 24.2 jit_solution(3400125740277703475)
XLA Ops:
  0.0 0.0 copy-start
  0.0 3.0 %collective-permute-start.1 = (bf16[512,256]{1,0:T(8,128)(2,1)}, bf16[512,256]{1,0:T(8,128)(2,1)S(1)}, u32[]{:S(2)}, u32[]{:S(2)}) collective-permute-start(bf16[512,256]{1,0:T(8,128)(2,1)} %refs_8_.1), channel_id=1, source_target_pairs={{0,8},{4,12},{8,0},{12,4},{1,9},{5,13},{9,1},{13,5},{2,10},{6,14},... | collective-permute-start | bytes 786440 | tf_op jit(solution)/shard_map/ppermute | solution.py:208
  3.0 5.6 %shard_map.64 = f32[8,1024]{1,0:T(8,128)S(1)} custom-call(s32[1,9]{1,0:T(1,128)} %lengths.1, bf16[256,14336]{1,0:T(8,128)(2,1)} %hidden.1, bf16[256,4096]{1,0:T(8,128)(2,1)} %out_grad.1, bf16[32,14336]{1,0:T(8,128)(2,1)} %proj_in.1, bf16[32,4096]{1,0:T(8,128)(2,1)} %proj_out.1), custom_call_target="tpu_custom_call" | custom-call | flops 301989888 | bytes 10616832 | tf_op jit(solution)/shard_map/pallas_call | solution.py:94
  8.6 1.8 %collective-permute-start = (f32[8,1024]{1,0:T(8,128)S(1)}, f32[8,1024]{1,0:T(8,128)S(1)}, u32[]{:S(2)}, u32[]{:S(2)}) collective-permute-start(f32[8,1024]{1,0:T(8,128)S(1)} %shard_map.64), channel_id=1, source_target_pairs={{0,6},{1,7},{2,4},{3,5},{4,2},{5,3},{6,0},{7,1},{8,14},{9,15},{10,... | collective-permute-start | bytes 98312 | tf_op jit(solution)/shard_map/ppermute | solution.py:208
  10.4 0.0 copy-done
  10.4 1.0 %collective-permute-start.9 = (bf16[512,256]{1,0:T(8,128)(2,1)S(1)}, bf16[512,256]{1,0:T(8,128)(2,1)S(1)}, u32[]{:S(2)}, u32[]{:S(2)}) collective-permute-start(bf16[512,256]{1,0:T(8,128)(2,1)S(1)} %copy-done), channel_id=1, source_target_pairs={{0,4},{4,0},{8,12},{12,8},{1,5},{5,1},{9,13},{13,9},{2,6},{6,2},{1... | collective-permute-start | bytes 786440 | tf_op jit(solution)/shard_map/ppermute | solution.py:208
  11.4 1.6 %collective-permute-done = f32[8,1024]{1,0:T(8,128)S(1)} collective-permute-done((f32[8,1024]{1,0:T(8,128)S(1)}, f32[8,1024]{1,0:T(8,128)S(1)}, u32[]{:S(2)}, u32[]{:S(2)}) %collective-permute-start) | collective-permute-done | bytes 32800 | tf_op jit(solution)/shard_map/ppermute | solution.py:208
  13.0 0.0 collective-permute-done.1.refs_10_
  13.0 0.2 collective-permute-start.10
  13.2 1.5 %collective-permute-start.4 = (f32[16,1024]{1,0:T(8,128)S(1)}, f32[16,1024]{1,0:T(8,128)S(1)}, u32[]{:S(2)}, u32[]{:S(2)}) collective-permute-start(f32[16,1024]{1,0:T(8,128)S(1)} %pad_maximum_fusion.refs_0_), channel_id=1, source_target_pairs={{0,13},{1,12},{2,15},{3,14},{4,9},{5,8},{6,11},{7,10},{8,5},{9,4},... | collective-permute-start | bytes 196616 | tf_op jit(solution)/shard_map/ppermute | solution.py:208
  14.7 0.1 collective-permute-start.3
  14.8 1.6 %collective-permute-start.2 = (f32[16,1024]{1,0:T(8,128)S(1)}, f32[16,1024]{1,0:T(8,128)S(1)}, u32[]{:S(2)}, u32[]{:S(2)}) collective-permute-start(f32[16,1024]{1,0:T(8,128)S(1)} %pad_maximum_fusion.refs_0_), channel_id=1, source_target_pairs={{0,12},{1,13},{2,14},{3,15},{4,8},{5,9},{6,10},{7,11},{8,4},{9,5},... | collective-permute-start | bytes 196616 | tf_op jit(solution)/shard_map/ppermute | solution.py:208
  16.4 0.0 collective-permute-done.9.refs_9_
  16.4 0.2 collective-permute-start.5
  16.6 1.5 %collective-permute-done.4.refs_3_ = f32[16,1024]{1,0:T(8,128)S(1)} collective-permute-done((f32[16,1024]{1,0:T(8,128)S(1)}, f32[16,1024]{1,0:T(8,128)S(1)}, u32[]{:S(2)}, u32[]{:S(2)}) %collective-permute-start.4) | collective-permute-done | bytes 65568 | tf_op jit(solution)/shard_map/ppermute | solution.py:208
  18.1 0.4 %collective-permute-start.8 = (f32[16,1024]{1,0:T(8,128)S(1)}, f32[16,1024]{1,0:T(8,128)S(1)}, u32[]{:S(2)}, u32[]{:S(2)}) collective-permute-start(f32[16,1024]{1,0:T(8,128)S(1)} %collective-permute-done.4.refs_3_), channel_id=1, source_target_pairs={{0,4},{1,5},{2,6},{3,7},{4,0},{5,1},{6,2},{7,3},{8,12},{9,13},{10,... | collective-permute-start | bytes 196616 | tf_op jit(solution)/shard_map/ppermute | solution.py:208
  18.4 0.4 %collective-permute-done.3.refs_2_ = f32[16,1024]{1,0:T(8,128)S(1)} collective-permute-done((f32[16,1024]{1,0:T(8,128)S(1)}, f32[16,1024]{1,0:T(8,128)S(1)}, u32[]{:S(2)}, u32[]{:S(2)}) %collective-permute-start.3) | collective-permute-done | bytes 65568 | tf_op jit(solution)/shard_map/ppermute | solution.py:208
  18.8 0.4 %collective-permute-start.7 = (f32[16,1024]{1,0:T(8,128)S(1)}, f32[16,1024]{1,0:T(8,128)S(1)}, u32[]{:S(2)}, u32[]{:S(2)}) collective-permute-start(f32[16,1024]{1,0:T(8,128)S(1)} %collective-permute-done.3.refs_2_), channel_id=1, source_target_pairs={{0,4},{1,5},{2,6},{3,7},{4,0},{5,1},{6,2},{7,3},{8,12},{9,13},{10,... | collective-permute-start | bytes 196616 | tf_op jit(solution)/shard_map/ppermute | solution.py:208
  19.2 0.7 %collective-permute-done.2.refs_1_ = f32[16,1024]{1,0:T(8,128)S(1)} collective-permute-done((f32[16,1024]{1,0:T(8,128)S(1)}, f32[16,1024]{1,0:T(8,128)S(1)}, u32[]{:S(2)}, u32[]{:S(2)}) %collective-permute-start.2) | collective-permute-done | bytes 65568 | tf_op jit(solution)/shard_map/ppermute | solution.py:208
  19.9 0.1 collective-permute-start.6
  20.0 0.0 collective-permute-done.5.refs_4_
  20.0 0.0 collective-permute-done.8.refs_7_
  20.0 0.1 collective-permute-done.7.refs_6_
  20.1 1.0 %collective-permute-done.6.refs_5_ = f32[16,1024]{1,0:T(8,128)S(1)} collective-permute-done((f32[16,1024]{1,0:T(8,128)S(1)}, f32[16,1024]{1,0:T(8,128)S(1)}, u32[]{:S(2)}, u32[]{:S(2)}) %collective-permute-start.6) | collective-permute-done | bytes 65568 | tf_op jit(solution)/shard_map/ppermute | solution.py:208
  21.1 0.0 collective-permute-done.10.refs_11_
  21.1 3.0 %shard_map.65 = f32[32,512]{1,0:T(8,128)} custom-call(f32[16,1024]{1,0:T(8,128)S(1)} %pad_maximum_fusion.refs_0_, f32[16,1024]{1,0:T(8,128)S(1)} %collective-permute-done.2.refs_1_, f32[16,1024]{1,0:T(8,128)S(1)} %collective-permute-done.3.refs_2_, f32[16,1024]{1,0:T(8,128)S(1)} %collective-permute-done.4.refs_3_, ...), custom_call_target="tpu_custom_call" | custom-call | tf_op jit(solution)/shard_map/pallas_call | solution.py:235
  (1 shorter events, 0.0 us)
Async XLA Ops:
  0.0 10.4 %copy-start = (bf16[512,256]{1,0:T(8,128)(2,1)S(1)}, bf16[512,256]{1,0:T(8,128)(2,1)}, u32[]{:S(2)}) copy-start(bf16[512,256]{1,0:T(8,128)(2,1)} %refs_8_.1) | copy-start | bytes 786436
  0.0 13.0 %collective-permute-start.1 = (bf16[512,256]{1,0:T(8,128)(2,1)}, bf16[512,256]{1,0:T(8,128)(2,1)S(1)}, u32[]{:S(2)}, u32[]{:S(2)}) collective-permute-start(bf16[512,256]{1,0:T(8,128)(2,1)} %refs_8_.1), channel_id=1, source_target_pairs={{0,8},{4,12},{8,0},{12,4},{1,9},{5,13},{9,1},{13,5},{2,10},{6,14},... | collective-permute-start | bytes 786440 | tf_op jit(solution)/shard_map/ppermute | solution.py:208
  8.6 4.4 %collective-permute-start = (f32[8,1024]{1,0:T(8,128)S(1)}, f32[8,1024]{1,0:T(8,128)S(1)}, u32[]{:S(2)}, u32[]{:S(2)}) collective-permute-start(f32[8,1024]{1,0:T(8,128)S(1)} %shard_map.64), channel_id=1, source_target_pairs={{0,6},{1,7},{2,4},{3,5},{4,2},{5,3},{6,0},{7,1},{8,14},{9,15},{10,... | collective-permute-start | bytes 98312 | tf_op jit(solution)/shard_map/ppermute | solution.py:208
  10.4 6.0 %collective-permute-start.9 = (bf16[512,256]{1,0:T(8,128)(2,1)S(1)}, bf16[512,256]{1,0:T(8,128)(2,1)S(1)}, u32[]{:S(2)}, u32[]{:S(2)}) collective-permute-start(bf16[512,256]{1,0:T(8,128)(2,1)S(1)} %copy-done), channel_id=1, source_target_pairs={{0,4},{4,0},{8,12},{12,8},{1,5},{5,1},{9,13},{13,9},{2,6},{6,2},{1... | collective-permute-start | bytes 786440 | tf_op jit(solution)/shard_map/ppermute | solution.py:208
  13.0 8.1 %collective-permute-start.10 = (bf16[512,256]{1,0:T(8,128)(2,1)S(1)}, bf16[512,256]{1,0:T(8,128)(2,1)S(1)}, u32[]{:S(2)}, u32[]{:S(2)}) collective-permute-start(bf16[512,256]{1,0:T(8,128)(2,1)S(1)} %collective-permute-done.1.refs_10_), channel_id=1, source_target_pairs={{0,4},{4,0},{8,12},{12,8},{1,5},{5,1},{9,13},{13,9},{2,6},{6,2},{1... | collective-permute-start | bytes 786440 | tf_op jit(solution)/shard_map/ppermute | solution.py:208
  13.2 4.9 %collective-permute-start.4 = (f32[16,1024]{1,0:T(8,128)S(1)}, f32[16,1024]{1,0:T(8,128)S(1)}, u32[]{:S(2)}, u32[]{:S(2)}) collective-permute-start(f32[16,1024]{1,0:T(8,128)S(1)} %pad_maximum_fusion.refs_0_), channel_id=1, source_target_pairs={{0,13},{1,12},{2,15},{3,14},{4,9},{5,8},{6,11},{7,10},{8,5},{9,4},... | collective-permute-start | bytes 196616 | tf_op jit(solution)/shard_map/ppermute | solution.py:208
  14.7 4.1 %collective-permute-start.3 = (f32[16,1024]{1,0:T(8,128)S(1)}, f32[16,1024]{1,0:T(8,128)S(1)}, u32[]{:S(2)}, u32[]{:S(2)}) collective-permute-start(f32[16,1024]{1,0:T(8,128)S(1)} %pad_maximum_fusion.refs_0_), channel_id=1, source_target_pairs={{0,5},{1,4},{2,7},{3,6},{4,1},{5,0},{6,3},{7,2},{8,13},{9,12},{10,... | collective-permute-start | bytes 196616 | tf_op jit(solution)/shard_map/ppermute | solution.py:208
  14.8 5.1 %collective-permute-start.2 = (f32[16,1024]{1,0:T(8,128)S(1)}, f32[16,1024]{1,0:T(8,128)S(1)}, u32[]{:S(2)}, u32[]{:S(2)}) collective-permute-start(f32[16,1024]{1,0:T(8,128)S(1)} %pad_maximum_fusion.refs_0_), channel_id=1, source_target_pairs={{0,12},{1,13},{2,14},{3,15},{4,8},{5,9},{6,10},{7,11},{8,4},{9,5},... | collective-permute-start | bytes 196616 | tf_op jit(solution)/shard_map/ppermute | solution.py:208
  16.4 3.6 %collective-permute-start.5 = (f32[16,1024]{1,0:T(8,128)S(1)}, f32[16,1024]{1,0:T(8,128)S(1)}, u32[]{:S(2)}, u32[]{:S(2)}) collective-permute-start(f32[16,1024]{1,0:T(8,128)S(1)} %pad_maximum_fusion.refs_0_), channel_id=1, source_target_pairs={{0,4},{1,5},{2,6},{3,7},{4,0},{5,1},{6,2},{7,3},{8,12},{9,13},{10,... | collective-permute-start | bytes 196616 | tf_op jit(solution)/shard_map/ppermute | solution.py:208
  18.1 1.9 %collective-permute-start.8 = (f32[16,1024]{1,0:T(8,128)S(1)}, f32[16,1024]{1,0:T(8,128)S(1)}, u32[]{:S(2)}, u32[]{:S(2)}) collective-permute-start(f32[16,1024]{1,0:T(8,128)S(1)} %collective-permute-done.4.refs_3_), channel_id=1, source_target_pairs={{0,4},{1,5},{2,6},{3,7},{4,0},{5,1},{6,2},{7,3},{8,12},{9,13},{10,... | collective-permute-start | bytes 196616 | tf_op jit(solution)/shard_map/ppermute | solution.py:208
  18.8 1.3 %collective-permute-start.7 = (f32[16,1024]{1,0:T(8,128)S(1)}, f32[16,1024]{1,0:T(8,128)S(1)}, u32[]{:S(2)}, u32[]{:S(2)}) collective-permute-start(f32[16,1024]{1,0:T(8,128)S(1)} %collective-permute-done.3.refs_2_), channel_id=1, source_target_pairs={{0,4},{1,5},{2,6},{3,7},{4,0},{5,1},{6,2},{7,3},{8,12},{9,13},{10,... | collective-permute-start | bytes 196616 | tf_op jit(solution)/shard_map/ppermute | solution.py:208
  19.9 1.3 %collective-permute-start.6 = (f32[16,1024]{1,0:T(8,128)S(1)}, f32[16,1024]{1,0:T(8,128)S(1)}, u32[]{:S(2)}, u32[]{:S(2)}) collective-permute-start(f32[16,1024]{1,0:T(8,128)S(1)} %collective-permute-done.2.refs_1_), channel_id=1, source_target_pairs={{0,4},{1,5},{2,6},{3,7},{4,0},{5,1},{6,2},{7,3},{8,12},{9,13},{10,... | collective-permute-start | bytes 196616 | tf_op jit(solution)/shard_map/ppermute | solution.py:208

commit v7 on v6

--- a/solution.py
+++ b/solution.py
@@ -165,11 +165,12 @@
     system = (gram + damp * eye) * root_row * root_col
     square = product(system, system)
     size = jnp.max(jnp.sum(jnp.abs(square), axis=0, keepdims=True), axis=1, keepdims=True)
-    scale = (1.0 / 0.51) * lax.rsqrt(size)
+    safe = (1.0 / 0.51) * lax.rsqrt(size)
+    scale = (1.0 / 0.42) * lax.rsqrt(size)
     scaled = system * scale
     power = (eye - 2.0 * scaled) + square * (scale * scale)
     series = 2.0 * eye - scaled
-    for _ in range(3):
+    for _ in range(2):
         both = product(jnp.concatenate([series, power], axis=0), power)
         series = series + both[:n]
         power = both[n:]
@@ -183,24 +184,32 @@
         error = eye - product6(system, x)
         return x + product(x, error), jnp.sum(error * error)
 
-    def store(x):
-        weights = x[:mine] * root_row * root_col[:mine]
-        result = dot(weights, cross, NN, HIGHEST)
+    def store(result):
         for away in range(groups):
             to = pl.multiple_of((qry ^ away) * each, each)
             out[pl.ds(to, each), :] = result[away * each:(away + 1) * each]
 
     inverse, miss = refine(series)
-    store(inverse)
-
-    @pl.when(miss > 1e-6)
+    store(dot(inverse[:mine] * root_row * root_col[:mine], cross, NN, HIGHEST))
+
+    @pl.when(jnp.logical_not(miss < 1e-4))
     def _():
         def again(state):
             x, _, turns = state
             x, left = refine(x)
             return x, left, turns + 1
 
-        store(lax.while_loop(lambda s: (s[1] > 1e-6) & (s[2] < 16), again, (inverse, miss, jnp.int32(0)))[0])
+        begin = jnp.where(miss < 0.25, inverse, eye * safe)
+        found, _, _ = lax.while_loop(
+            lambda s: (s[1] > 1e-4) & (s[2] < 24), again, (begin, miss + 1.0, jnp.int32(0))
+        )
+        right = cross * root_col
+
+        def correct(_, z):
+            return z + dot(found, right - dot(system, z, NN, HIGHEST), NN, HIGHEST)
+
+        solved = lax.fori_loop(0, 6, correct, jnp.zeros_like(right))
+        store(solved[:mine] * root_col[:mine])
 
 
 def swap(x, axis, bit):

time: 24.3 us -> 28.8 us (1.19)
  Pallas kernels: 8.61 us -> 13.1 us
    pallas_call x1, Pallas kernels: 3.02 us -> 7.51 us  [body_small(): pl.pallas_call(lambda *refs: scores_kernel(*refs, width=width, rows=rows)...]
  transfers between devices with their start and end apart: 11 -> 11, of which waited for: 6 -> 6; matrix products, arithmetic and copies ran while one was open for 0% -> 0% of each run, Pallas kernels for 23% -> 20%
where the time goes in v7:
time: 28.8 us; the launch traced here: 28.6 us
  Pallas kernels  13.1 us (45%)
  starting transfers between devices  10.2 us (35%)
  waiting for transfers between devices  5.31 us (18%)
    ppermute x11, starting transfers between devices, swap(): return lax.ppermute(x, axis, [(i, i ^ bit) for i in range(size)])  10.2 us
    pallas_call x1, Pallas kernels, body_small(): pl.pallas_call(lambda *refs: scores_kernel(*refs, width=width, rows=rows)...  7.51 us
    pallas_call x1, Pallas kernels, example_vectors(): pl.pallas_call(vectors_kernel, in_specs=[pl.BlockSpec(memory_space=pltpu....  5.6 us
    ppermute x11, waiting for transfers between devices, swap(): return lax.ppermute(x, axis, [(i, i ^ bit) for i in range(size)])  5.31 us
  transfers between devices with their start and end apart: 11, of which 6 were waited for; matrix products, arithmetic and copies ran while one was open for 0% of the time, Pallas kernels for 20%

profile of v7, /device:TPU:0, one launch (start us, length us, event | category | flops | bytes accessed | tf_op | source)
XLA Modules:
  0.0 28.6 jit_solution(11275546520437572121)
XLA Ops:
  0.0 0.0 copy-start
  0.0 3.0 %collective-permute-start.1 = (bf16[512,256]{1,0:T(8,128)(2,1)}, bf16[512,256]{1,0:T(8,128)(2,1)S(1)}, u32[]{:S(2)}, u32[]{:S(2)}) collective-permute-start(bf16[512,256]{1,0:T(8,128)(2,1)} %refs_8_.1), channel_id=1, source_target_pairs={{0,8},{4,12},{8,0},{12,4},{1,9},{5,13},{9,1},{13,5},{2,10},{6,14},... | collective-permute-start | bytes 786440 | tf_op jit(solution)/shard_map/ppermute | solution.py:217
  3.0 5.6 %shard_map.64 = f32[8,1024]{1,0:T(8,128)S(1)} custom-call(s32[1,9]{1,0:T(1,128)} %lengths.1, bf16[256,14336]{1,0:T(8,128)(2,1)} %hidden.1, bf16[256,4096]{1,0:T(8,128)(2,1)} %out_grad.1, bf16[32,14336]{1,0:T(8,128)(2,1)} %proj_in.1, bf16[32,4096]{1,0:T(8,128)(2,1)} %proj_out.1), custom_call_target="tpu_custom_call" | custom-call | flops 301989888 | bytes 10616832 | tf_op jit(solution)/shard_map/pallas_call | solution.py:94
  8.6 1.8 %collective-permute-start = (f32[8,1024]{1,0:T(8,128)S(1)}, f32[8,1024]{1,0:T(8,128)S(1)}, u32[]{:S(2)}, u32[]{:S(2)}) collective-permute-start(f32[8,1024]{1,0:T(8,128)S(1)} %shard_map.64), channel_id=1, source_target_pairs={{0,6},{1,7},{2,4},{3,5},{4,2},{5,3},{6,0},{7,1},{8,14},{9,15},{10,... | collective-permute-start | bytes 98312 | tf_op jit(solution)/shard_map/ppermute | solution.py:217
  10.4 0.0 copy-done
  10.4 1.0 %collective-permute-start.9 = (bf16[512,256]{1,0:T(8,128)(2,1)S(1)}, bf16[512,256]{1,0:T(8,128)(2,1)S(1)}, u32[]{:S(2)}, u32[]{:S(2)}) collective-permute-start(bf16[512,256]{1,0:T(8,128)(2,1)S(1)} %copy-done), channel_id=1, source_target_pairs={{0,4},{4,0},{8,12},{12,8},{1,5},{5,1},{9,13},{13,9},{2,6},{6,2},{1... | collective-permute-start | bytes 786440 | tf_op jit(solution)/shard_map/ppermute | solution.py:217
  11.4 1.6 %collective-permute-done = f32[8,1024]{1,0:T(8,128)S(1)} collective-permute-done((f32[8,1024]{1,0:T(8,128)S(1)}, f32[8,1024]{1,0:T(8,128)S(1)}, u32[]{:S(2)}, u32[]{:S(2)}) %collective-permute-start) | collective-permute-done | bytes 32800 | tf_op jit(solution)/shard_map/ppermute | solution.py:217
  13.0 0.0 collective-permute-done.1.refs_10_
  13.0 0.2 collective-permute-start.10
  13.2 1.5 %collective-permute-start.4 = (f32[16,1024]{1,0:T(8,128)S(1)}, f32[16,1024]{1,0:T(8,128)S(1)}, u32[]{:S(2)}, u32[]{:S(2)}) collective-permute-start(f32[16,1024]{1,0:T(8,128)S(1)} %pad_maximum_fusion.refs_0_), channel_id=1, source_target_pairs={{0,13},{1,12},{2,15},{3,14},{4,9},{5,8},{6,11},{7,10},{8,5},{9,4},... | collective-permute-start | bytes 196616 | tf_op jit(solution)/shard_map/ppermute | solution.py:217
  14.7 0.1 collective-permute-start.3
  14.8 1.6 %collective-permute-start.2 = (f32[16,1024]{1,0:T(8,128)S(1)}, f32[16,1024]{1,0:T(8,128)S(1)}, u32[]{:S(2)}, u32[]{:S(2)}) collective-permute-start(f32[16,1024]{1,0:T(8,128)S(1)} %pad_maximum_fusion.refs_0_), channel_id=1, source_target_pairs={{0,12},{1,13},{2,14},{3,15},{4,8},{5,9},{6,10},{7,11},{8,4},{9,5},... | collective-permute-start | bytes 196616 | tf_op jit(solution)/shard_map/ppermute | solution.py:217
  16.4 0.0 collective-permute-done.9.refs_9_
  16.4 0.2 collective-permute-start.5
  16.6 1.5 %collective-permute-done.4.refs_3_ = f32[16,1024]{1,0:T(8,128)S(1)} collective-permute-done((f32[16,1024]{1,0:T(8,128)S(1)}, f32[16,1024]{1,0:T(8,128)S(1)}, u32[]{:S(2)}, u32[]{:S(2)}) %collective-permute-start.4) | collective-permute-done | bytes 65568 | tf_op jit(solution)/shard_map/ppermute | solution.py:217
  18.1 0.4 %collective-permute-start.8 = (f32[16,1024]{1,0:T(8,128)S(1)}, f32[16,1024]{1,0:T(8,128)S(1)}, u32[]{:S(2)}, u32[]{:S(2)}) collective-permute-start(f32[16,1024]{1,0:T(8,128)S(1)} %collective-permute-done.4.refs_3_), channel_id=1, source_target_pairs={{0,4},{1,5},{2,6},{3,7},{4,0},{5,1},{6,2},{7,3},{8,12},{9,13},{10,... | collective-permute-start | bytes 196616 | tf_op jit(solution)/shard_map/ppermute | solution.py:217
  18.4 0.4 %collective-permute-done.3.refs_2_ = f32[16,1024]{1,0:T(8,128)S(1)} collective-permute-done((f32[16,1024]{1,0:T(8,128)S(1)}, f32[16,1024]{1,0:T(8,128)S(1)}, u32[]{:S(2)}, u32[]{:S(2)}) %collective-permute-start.3) | collective-permute-done | bytes 65568 | tf_op jit(solution)/shard_map/ppermute | solution.py:217
  18.8 0.4 %collective-permute-start.7 = (f32[16,1024]{1,0:T(8,128)S(1)}, f32[16,1024]{1,0:T(8,128)S(1)}, u32[]{:S(2)}, u32[]{:S(2)}) collective-permute-start(f32[16,1024]{1,0:T(8,128)S(1)} %collective-permute-done.3.refs_2_), channel_id=1, source_target_pairs={{0,4},{1,5},{2,6},{3,7},{4,0},{5,1},{6,2},{7,3},{8,12},{9,13},{10,... | collective-permute-start | bytes 196616 | tf_op jit(solution)/shard_map/ppermute | solution.py:217
  19.2 0.7 %collective-permute-done.2.refs_1_ = f32[16,1024]{1,0:T(8,128)S(1)} collective-permute-done((f32[16,1024]{1,0:T(8,128)S(1)}, f32[16,1024]{1,0:T(8,128)S(1)}, u32[]{:S(2)}, u32[]{:S(2)}) %collective-permute-start.2) | collective-permute-done | bytes 65568 | tf_op jit(solution)/shard_map/ppermute | solution.py:217
  19.9 0.1 collective-permute-start.6
  20.0 0.0 collective-permute-done.5.refs_4_
  20.0 0.0 collective-permute-done.8.refs_7_
  20.0 0.1 collective-permute-done.7.refs_6_
  20.1 1.0 %collective-permute-done.6.refs_5_ = f32[16,1024]{1,0:T(8,128)S(1)} collective-permute-done((f32[16,1024]{1,0:T(8,128)S(1)}, f32[16,1024]{1,0:T(8,128)S(1)}, u32[]{:S(2)}, u32[]{:S(2)}) %collective-permute-start.6) | collective-permute-done | bytes 65568 | tf_op jit(solution)/shard_map/ppermute | solution.py:217
  21.1 0.0 collective-permute-done.10.refs_11_
  21.1 7.5 %shard_map.65 = f32[32,512]{1,0:T(8,128)} custom-call(f32[16,1024]{1,0:T(8,128)S(1)} %pad_maximum_fusion.refs_0_, f32[16,1024]{1,0:T(8,128)S(1)} %collective-permute-done.2.refs_1_, f32[16,1024]{1,0:T(8,128)S(1)} %collective-permute-done.3.refs_2_, f32[16,1024]{1,0:T(8,128)S(1)} %collective-permute-done.4.refs_3_, ...), custom_call_target="tpu_custom_call" | custom-call | tf_op jit(solution)/shard_map/pallas_call | solution.py:244
  (1 shorter events, 0.0 us)
Async XLA Ops:
  0.0 10.4 %copy-start = (bf16[512,256]{1,0:T(8,128)(2,1)S(1)}, bf16[512,256]{1,0:T(8,128)(2,1)}, u32[]{:S(2)}) copy-start(bf16[512,256]{1,0:T(8,128)(2,1)} %refs_8_.1) | copy-start | bytes 786436
  0.0 13.0 %collective-permute-start.1 = (bf16[512,256]{1,0:T(8,128)(2,1)}, bf16[512,256]{1,0:T(8,128)(2,1)S(1)}, u32[]{:S(2)}, u32[]{:S(2)}) collective-permute-start(bf16[512,256]{1,0:T(8,128)(2,1)} %refs_8_.1), channel_id=1, source_target_pairs={{0,8},{4,12},{8,0},{12,4},{1,9},{5,13},{9,1},{13,5},{2,10},{6,14},... | collective-permute-start | bytes 786440 | tf_op jit(solution)/shard_map/ppermute | solution.py:217
  8.6 4.4 %collective-permute-start = (f32[8,1024]{1,0:T(8,128)S(1)}, f32[8,1024]{1,0:T(8,128)S(1)}, u32[]{:S(2)}, u32[]{:S(2)}) collective-permute-start(f32[8,1024]{1,0:T(8,128)S(1)} %shard_map.64), channel_id=1, source_target_pairs={{0,6},{1,7},{2,4},{3,5},{4,2},{5,3},{6,0},{7,1},{8,14},{9,15},{10,... | collective-permute-start | bytes 98312 | tf_op jit(solution)/shard_map/ppermute | solution.py:217
  10.4 6.0 %collective-permute-start.9 = (bf16[512,256]{1,0:T(8,128)(2,1)S(1)}, bf16[512,256]{1,0:T(8,128)(2,1)S(1)}, u32[]{:S(2)}, u32[]{:S(2)}) collective-permute-start(bf16[512,256]{1,0:T(8,128)(2,1)S(1)} %copy-done), channel_id=1, source_target_pairs={{0,4},{4,0},{8,12},{12,8},{1,5},{5,1},{9,13},{13,9},{2,6},{6,2},{1... | collective-permute-start | bytes 786440 | tf_op jit(solution)/shard_map/ppermute | solution.py:217
  13.0 8.1 %collective-permute-start.10 = (bf16[512,256]{1,0:T(8,128)(2,1)S(1)}, bf16[512,256]{1,0:T(8,128)(2,1)S(1)}, u32[]{:S(2)}, u32[]{:S(2)}) collective-permute-start(bf16[512,256]{1,0:T(8,128)(2,1)S(1)} %collective-permute-done.1.refs_10_), channel_id=1, source_target_pairs={{0,4},{4,0},{8,12},{12,8},{1,5},{5,1},{9,13},{13,9},{2,6},{6,2},{1... | collective-permute-start | bytes 786440 | tf_op jit(solution)/shard_map/ppermute | solution.py:217
  13.2 4.9 %collective-permute-start.4 = (f32[16,1024]{1,0:T(8,128)S(1)}, f32[16,1024]{1,0:T(8,128)S(1)}, u32[]{:S(2)}, u32[]{:S(2)}) collective-permute-start(f32[16,1024]{1,0:T(8,128)S(1)} %pad_maximum_fusion.refs_0_), channel_id=1, source_target_pairs={{0,13},{1,12},{2,15},{3,14},{4,9},{5,8},{6,11},{7,10},{8,5},{9,4},... | collective-permute-start | bytes 196616 | tf_op jit(solution)/shard_map/ppermute | solution.py:217
  14.7 4.1 %collective-permute-start.3 = (f32[16,1024]{1,0:T(8,128)S(1)}, f32[16,1024]{1,0:T(8,128)S(1)}, u32[]{:S(2)}, u32[]{:S(2)}) collective-permute-start(f32[16,1024]{1,0:T(8,128)S(1)} %pad_maximum_fusion.refs_0_), channel_id=1, source_target_pairs={{0,5},{1,4},{2,7},{3,6},{4,1},{5,0},{6,3},{7,2},{8,13},{9,12},{10,... | collective-permute-start | bytes 196616 | tf_op jit(solution)/shard_map/ppermute | solution.py:217
  14.8 5.1 %collective-permute-start.2 = (f32[16,1024]{1,0:T(8,128)S(1)}, f32[16,1024]{1,0:T(8,128)S(1)}, u32[]{:S(2)}, u32[]{:S(2)}) collective-permute-start(f32[16,1024]{1,0:T(8,128)S(1)} %pad_maximum_fusion.refs_0_), channel_id=1, source_target_pairs={{0,12},{1,13},{2,14},{3,15},{4,8},{5,9},{6,10},{7,11},{8,4},{9,5},... | collective-permute-start | bytes 196616 | tf_op jit(solution)/shard_map/ppermute | solution.py:217
  16.4 3.6 %collective-permute-start.5 = (f32[16,1024]{1,0:T(8,128)S(1)}, f32[16,1024]{1,0:T(8,128)S(1)}, u32[]{:S(2)}, u32[]{:S(2)}) collective-permute-start(f32[16,1024]{1,0:T(8,128)S(1)} %pad_maximum_fusion.refs_0_), channel_id=1, source_target_pairs={{0,4},{1,5},{2,6},{3,7},{4,0},{5,1},{6,2},{7,3},{8,12},{9,13},{10,... | collective-permute-start | bytes 196616 | tf_op jit(solution)/shard_map/ppermute | solution.py:217
  18.1 1.9 %collective-permute-start.8 = (f32[16,1024]{1,0:T(8,128)S(1)}, f32[16,1024]{1,0:T(8,128)S(1)}, u32[]{:S(2)}, u32[]{:S(2)}) collective-permute-start(f32[16,1024]{1,0:T(8,128)S(1)} %collective-permute-done.4.refs_3_), channel_id=1, source_target_pairs={{0,4},{1,5},{2,6},{3,7},{4,0},{5,1},{6,2},{7,3},{8,12},{9,13},{10,... | collective-permute-start | bytes 196616 | tf_op jit(solution)/shard_map/ppermute | solution.py:217
  18.8 1.3 %collective-permute-start.7 = (f32[16,1024]{1,0:T(8,128)S(1)}, f32[16,1024]{1,0:T(8,128)S(1)}, u32[]{:S(2)}, u32[]{:S(2)}) collective-permute-start(f32[16,1024]{1,0:T(8,128)S(1)} %collective-permute-done.3.refs_2_), channel_id=1, source_target_pairs={{0,4},{1,5},{2,6},{3,7},{4,0},{5,1},{6,2},{7,3},{8,12},{9,13},{10,... | collective-permute-start | bytes 196616 | tf_op jit(solution)/shard_map/ppermute | solution.py:217
  19.9 1.3 %collective-permute-start.6 = (f32[16,1024]{1,0:T(8,128)S(1)}, f32[16,1024]{1,0:T(8,128)S(1)}, u32[]{:S(2)}, u32[]{:S(2)}) collective-permute-start(f32[16,1024]{1,0:T(8,128)S(1)} %collective-permute-done.2.refs_1_), channel_id=1, source_target_pairs={{0,4},{1,5},{2,6},{3,7},{4,0},{5,1},{6,2},{7,3},{8,12},{9,13},{10,... | collective-permute-start | bytes 196616 | tf_op jit(solution)/shard_map/ppermute | solution.py:217

commit v8 on v7

--- a/solution.py
+++ b/solution.py
@@ -227,7 +227,7 @@
         return swap(x, ("ex", "qry"), bits)
 
     q1 = swap(queries, "ex", 1)
-    q2 = swap(queries, "ex", 2)
+    q2 = cross(queries, core + y)
     vectors = example_vectors(hidden, out_grad, proj_in, proj_out, lengths)
     first = core + 2
     own = jnp.concatenate([vectors, cross(vectors, first)], axis=0)
@@ -247,7 +247,7 @@
         in_specs=[pl.BlockSpec(memory_space=pltpu.VMEM)] * (len(pieces) + 4),
         out_specs=pl.BlockSpec(memory_space=pltpu.VMEM),
         compiler_params=pltpu.CompilerParams(vmem_limit_bytes=24 * 2**20),
-    )(*pieces.values(), queries, q1, q2, q3)
+    )(*pieces.values(), queries, q1, q3, q2)
 
 
 def body_large(hidden, out_grad, proj_in, proj_out, lengths, queries):

time: 28.8 us -> 28.6 us (level)
  transfers between devices with their start and end apart: 11 -> 11, of which waited for: 6 -> 4; matrix products, arithmetic and copies ran while one was open for 0% -> 0% of each run, Pallas kernels for 20% -> 20%
where the time goes in v8:
time: 28.6 us; the launch traced here: 28.5 us
  Pallas kernels  13.1 us (46%)
  starting transfers between devices  9.99 us (35%)
  waiting for transfers between devices  5.35 us (19%)
    ppermute x11, starting transfers between devices, swap(): return lax.ppermute(x, axis, [(i, i ^ bit) for i in range(size)])  9.99 us
    pallas_call x1, Pallas kernels, body_small(): pl.pallas_call(lambda *refs: scores_kernel(*refs, width=width, rows=rows)...  7.51 us
    pallas_call x1, Pallas kernels, example_vectors(): pl.pallas_call(vectors_kernel, in_specs=[pl.BlockSpec(memory_space=pltpu....  5.6 us
    ppermute x11, waiting for transfers between devices, swap(): return lax.ppermute(x, axis, [(i, i ^ bit) for i in range(size)])  5.35 us
  transfers between devices with their start and end apart: 11, of which 4 were waited for; matrix products, arithmetic and copies ran while one was open for 0% of the time, Pallas kernels for 20%

profile of v8, /device:TPU:0, one launch (start us, length us, event | category | flops | bytes accessed | tf_op | source)
XLA Modules:
  0.0 28.5 jit_solution(11710562087826664903)
XLA Ops:
  0.0 0.0 copy-start
  0.0 2.4 %collective-permute-start.1 = (bf16[512,256]{1,0:T(8,128)(2,1)}, bf16[512,256]{1,0:T(8,128)(2,1)S(1)}, u32[]{:S(2)}, u32[]{:S(2)}) collective-permute-start(bf16[512,256]{1,0:T(8,128)(2,1)} %refs_8_.1), channel_id=1, source_target_pairs={{0,12},{1,13},{2,14},{3,15},{4,8},{5,9},{6,10},{7,11},{8,4},{9,5},... | collective-permute-start | bytes 786440 | tf_op jit(solution)/shard_map/ppermute | solution.py:217
  2.4 5.6 %shard_map.64 = f32[8,1024]{1,0:T(8,128)S(1)} custom-call(s32[1,9]{1,0:T(1,128)} %lengths.1, bf16[256,14336]{1,0:T(8,128)(2,1)} %hidden.1, bf16[256,4096]{1,0:T(8,128)(2,1)} %out_grad.1, bf16[32,14336]{1,0:T(8,128)(2,1)} %proj_in.1, bf16[32,4096]{1,0:T(8,128)(2,1)} %proj_out.1), custom_call_target="tpu_custom_call" | custom-call | flops 301989888 | bytes 10616832 | tf_op jit(solution)/shard_map/pallas_call | solution.py:94
  8.0 2.9 %collective-permute-start = (f32[8,1024]{1,0:T(8,128)S(1)}, f32[8,1024]{1,0:T(8,128)S(1)}, u32[]{:S(2)}, u32[]{:S(2)}) collective-permute-start(f32[8,1024]{1,0:T(8,128)S(1)} %shard_map.64), channel_id=1, source_target_pairs={{0,6},{1,7},{2,4},{3,5},{4,2},{5,3},{6,0},{7,1},{8,14},{9,15},{10,... | collective-permute-start | bytes 98312 | tf_op jit(solution)/shard_map/ppermute | solution.py:217
  11.0 0.0 copy-done
  11.0 0.0 collective-permute-start.9
  11.0 1.6 %collective-permute-done = f32[8,1024]{1,0:T(8,128)S(1)} collective-permute-done((f32[8,1024]{1,0:T(8,128)S(1)}, f32[8,1024]{1,0:T(8,128)S(1)}, u32[]{:S(2)}, u32[]{:S(2)}) %collective-permute-start) | collective-permute-done | bytes 32800 | tf_op jit(solution)/shard_map/ppermute | solution.py:217
  12.6 0.0 collective-permute-done.1.refs_11_
  12.6 0.5 %collective-permute-start.10 = (bf16[512,256]{1,0:T(8,128)(2,1)S(1)}, bf16[512,256]{1,0:T(8,128)(2,1)S(1)}, u32[]{:S(2)}, u32[]{:S(2)}) collective-permute-start(bf16[512,256]{1,0:T(8,128)(2,1)S(1)} %collective-permute-done.1.refs_11_), channel_id=1, source_target_pairs={{0,4},{4,0},{8,12},{12,8},{1,5},{5,1},{9,13},{13,9},{2,6},{6,2},{1... | collective-permute-start | bytes 786440 | tf_op jit(solution)/shard_map/ppermute | solution.py:217
  13.1 1.3 %collective-permute-start.4 = (f32[16,1024]{1,0:T(8,128)S(1)}, f32[16,1024]{1,0:T(8,128)S(1)}, u32[]{:S(2)}, u32[]{:S(2)}) collective-permute-start(f32[16,1024]{1,0:T(8,128)S(1)} %pad_maximum_fusion.refs_0_), channel_id=1, source_target_pairs={{0,13},{1,12},{2,15},{3,14},{4,9},{5,8},{6,11},{7,10},{8,5},{9,4},... | collective-permute-start | bytes 196616 | tf_op jit(solution)/shard_map/ppermute | solution.py:217
  14.4 0.3 %collective-permute-start.3 = (f32[16,1024]{1,0:T(8,128)S(1)}, f32[16,1024]{1,0:T(8,128)S(1)}, u32[]{:S(2)}, u32[]{:S(2)}) collective-permute-start(f32[16,1024]{1,0:T(8,128)S(1)} %pad_maximum_fusion.refs_0_), channel_id=1, source_target_pairs={{0,5},{1,4},{2,7},{3,6},{4,1},{5,0},{6,3},{7,2},{8,13},{9,12},{10,... | collective-permute-start | bytes 196616 | tf_op jit(solution)/shard_map/ppermute | solution.py:217
  14.7 1.3 %collective-permute-start.2 = (f32[16,1024]{1,0:T(8,128)S(1)}, f32[16,1024]{1,0:T(8,128)S(1)}, u32[]{:S(2)}, u32[]{:S(2)}) collective-permute-start(f32[16,1024]{1,0:T(8,128)S(1)} %pad_maximum_fusion.refs_0_), channel_id=1, source_target_pairs={{0,12},{1,13},{2,14},{3,15},{4,8},{5,9},{6,10},{7,11},{8,4},{9,5},... | collective-permute-start | bytes 196616 | tf_op jit(solution)/shard_map/ppermute | solution.py:217
  16.0 0.0 collective-permute-done.9.refs_9_
  16.0 0.4 %collective-permute-start.5 = (f32[16,1024]{1,0:T(8,128)S(1)}, f32[16,1024]{1,0:T(8,128)S(1)}, u32[]{:S(2)}, u32[]{:S(2)}) collective-permute-start(f32[16,1024]{1,0:T(8,128)S(1)} %pad_maximum_fusion.refs_0_), channel_id=1, source_target_pairs={{0,4},{1,5},{2,6},{3,7},{4,0},{5,1},{6,2},{7,3},{8,12},{9,13},{10,... | collective-permute-start | bytes 196616 | tf_op jit(solution)/shard_map/ppermute | solution.py:217
  16.4 1.7 %collective-permute-done.4.refs_3_ = f32[16,1024]{1,0:T(8,128)S(1)} collective-permute-done((f32[16,1024]{1,0:T(8,128)S(1)}, f32[16,1024]{1,0:T(8,128)S(1)}, u32[]{:S(2)}, u32[]{:S(2)}) %collective-permute-start.4) | collective-permute-done | bytes 65568 | tf_op jit(solution)/shard_map/ppermute | solution.py:217
  18.1 0.1 collective-permute-start.8
  18.3 0.0 collective-permute-done.3.refs_2_
  18.3 0.6 %collective-permute-start.7 = (f32[16,1024]{1,0:T(8,128)S(1)}, f32[16,1024]{1,0:T(8,128)S(1)}, u32[]{:S(2)}, u32[]{:S(2)}) collective-permute-start(f32[16,1024]{1,0:T(8,128)S(1)} %collective-permute-done.3.refs_2_), channel_id=1, source_target_pairs={{0,4},{1,5},{2,6},{3,7},{4,0},{5,1},{6,2},{7,3},{8,12},{9,13},{10,... | collective-permute-start | bytes 196616 | tf_op jit(solution)/shard_map/ppermute | solution.py:217
  18.9 0.8 %collective-permute-done.2.refs_1_ = f32[16,1024]{1,0:T(8,128)S(1)} collective-permute-done((f32[16,1024]{1,0:T(8,128)S(1)}, f32[16,1024]{1,0:T(8,128)S(1)}, u32[]{:S(2)}, u32[]{:S(2)}) %collective-permute-start.2) | collective-permute-done | bytes 65568 | tf_op jit(solution)/shard_map/ppermute | solution.py:217
  19.7 0.1 collective-permute-start.6
  19.8 0.0 collective-permute-done.5.refs_4_
  19.8 0.0 collective-permute-done.8.refs_7_
  19.8 0.0 collective-permute-done.7.refs_6_
  19.9 1.1 %collective-permute-done.6.refs_5_ = f32[16,1024]{1,0:T(8,128)S(1)} collective-permute-done((f32[16,1024]{1,0:T(8,128)S(1)}, f32[16,1024]{1,0:T(8,128)S(1)}, u32[]{:S(2)}, u32[]{:S(2)}) %collective-permute-start.6) | collective-permute-done | bytes 65568 | tf_op jit(solution)/shard_map/ppermute | solution.py:217
  21.0 0.0 collective-permute-done.10.refs_10_
  21.0 7.5 %shard_map.65 = f32[32,512]{1,0:T(8,128)} custom-call(f32[16,1024]{1,0:T(8,128)S(1)} %pad_maximum_fusion.refs_0_, f32[16,1024]{1,0:T(8,128)S(1)} %collective-permute-done.2.refs_1_, f32[16,1024]{1,0:T(8,128)S(1)} %collective-permute-done.3.refs_2_, f32[16,1024]{1,0:T(8,128)S(1)} %collective-permute-done.4.refs_3_, ...), custom_call_target="tpu_custom_call" | custom-call | tf_op jit(solution)/shard_map/pallas_call | solution.py:244
  (1 shorter events, 0.0 us)
Async XLA Ops:
  0.0 11.0 %copy-start = (bf16[512,256]{1,0:T(8,128)(2,1)S(1)}, bf16[512,256]{1,0:T(8,128)(2,1)}, u32[]{:S(2)}) copy-start(bf16[512,256]{1,0:T(8,128)(2,1)} %refs_8_.1) | copy-start | bytes 786436
  0.0 12.6 %collective-permute-start.1 = (bf16[512,256]{1,0:T(8,128)(2,1)}, bf16[512,256]{1,0:T(8,128)(2,1)S(1)}, u32[]{:S(2)}, u32[]{:S(2)}) collective-permute-start(bf16[512,256]{1,0:T(8,128)(2,1)} %refs_8_.1), channel_id=1, source_target_pairs={{0,12},{1,13},{2,14},{3,15},{4,8},{5,9},{6,10},{7,11},{8,4},{9,5},... | collective-permute-start | bytes 786440 | tf_op jit(solution)/shard_map/ppermute | solution.py:217
  8.0 4.5 %collective-permute-start = (f32[8,1024]{1,0:T(8,128)S(1)}, f32[8,1024]{1,0:T(8,128)S(1)}, u32[]{:S(2)}, u32[]{:S(2)}) collective-permute-start(f32[8,1024]{1,0:T(8,128)S(1)} %shard_map.64), channel_id=1, source_target_pairs={{0,6},{1,7},{2,4},{3,5},{4,2},{5,3},{6,0},{7,1},{8,14},{9,15},{10,... | collective-permute-start | bytes 98312 | tf_op jit(solution)/shard_map/ppermute | solution.py:217
  11.0 5.0 %collective-permute-start.9 = (bf16[512,256]{1,0:T(8,128)(2,1)S(1)}, bf16[512,256]{1,0:T(8,128)(2,1)S(1)}, u32[]{:S(2)}, u32[]{:S(2)}) collective-permute-start(bf16[512,256]{1,0:T(8,128)(2,1)S(1)} %copy-done), channel_id=1, source_target_pairs={{0,4},{4,0},{8,12},{12,8},{1,5},{5,1},{9,13},{13,9},{2,6},{6,2},{1... | collective-permute-start | bytes 786440 | tf_op jit(solution)/shard_map/ppermute | solution.py:217
  12.6 8.4 %collective-permute-start.10 = (bf16[512,256]{1,0:T(8,128)(2,1)S(1)}, bf16[512,256]{1,0:T(8,128)(2,1)S(1)}, u32[]{:S(2)}, u32[]{:S(2)}) collective-permute-start(bf16[512,256]{1,0:T(8,128)(2,1)S(1)} %collective-permute-done.1.refs_11_), channel_id=1, source_target_pairs={{0,4},{4,0},{8,12},{12,8},{1,5},{5,1},{9,13},{13,9},{2,6},{6,2},{1... | collective-permute-start | bytes 786440 | tf_op jit(solution)/shard_map/ppermute | solution.py:217
  13.1 5.1 %collective-permute-start.4 = (f32[16,1024]{1,0:T(8,128)S(1)}, f32[16,1024]{1,0:T(8,128)S(1)}, u32[]{:S(2)}, u32[]{:S(2)}) collective-permute-start(f32[16,1024]{1,0:T(8,128)S(1)} %pad_maximum_fusion.refs_0_), channel_id=1, source_target_pairs={{0,13},{1,12},{2,15},{3,14},{4,9},{5,8},{6,11},{7,10},{8,5},{9,4},... | collective-permute-start | bytes 196616 | tf_op jit(solution)/shard_map/ppermute | solution.py:217
  14.4 3.9 %collective-permute-start.3 = (f32[16,1024]{1,0:T(8,128)S(1)}, f32[16,1024]{1,0:T(8,128)S(1)}, u32[]{:S(2)}, u32[]{:S(2)}) collective-permute-start(f32[16,1024]{1,0:T(8,128)S(1)} %pad_maximum_fusion.refs_0_), channel_id=1, source_target_pairs={{0,5},{1,4},{2,7},{3,6},{4,1},{5,0},{6,3},{7,2},{8,13},{9,12},{10,... | collective-permute-start | bytes 196616 | tf_op jit(solution)/shard_map/ppermute | solution.py:217
  14.7 5.0 %collective-permute-start.2 = (f32[16,1024]{1,0:T(8,128)S(1)}, f32[16,1024]{1,0:T(8,128)S(1)}, u32[]{:S(2)}, u32[]{:S(2)}) collective-permute-start(f32[16,1024]{1,0:T(8,128)S(1)} %pad_maximum_fusion.refs_0_), channel_id=1, source_target_pairs={{0,12},{1,13},{2,14},{3,15},{4,8},{5,9},{6,10},{7,11},{8,4},{9,5},... | collective-permute-start | bytes 196616 | tf_op jit(solution)/shard_map/ppermute | solution.py:217
  16.0 3.9 %collective-permute-start.5 = (f32[16,1024]{1,0:T(8,128)S(1)}, f32[16,1024]{1,0:T(8,128)S(1)}, u32[]{:S(2)}, u32[]{:S(2)}) collective-permute-start(f32[16,1024]{1,0:T(8,128)S(1)} %pad_maximum_fusion.refs_0_), channel_id=1, source_target_pairs={{0,4},{1,5},{2,6},{3,7},{4,0},{5,1},{6,2},{7,3},{8,12},{9,13},{10,... | collective-permute-start | bytes 196616 | tf_op jit(solution)/shard_map/ppermute | solution.py:217
  18.1 1.7 %collective-permute-start.8 = (f32[16,1024]{1,0:T(8,128)S(1)}, f32[16,1024]{1,0:T(8,128)S(1)}, u32[]{:S(2)}, u32[]{:S(2)}) collective-permute-start(f32[16,1024]{1,0:T(8,128)S(1)} %collective-permute-done.4.refs_3_), channel_id=1, source_target_pairs={{0,4},{1,5},{2,6},{3,7},{4,0},{5,1},{6,2},{7,3},{8,12},{9,13},{10,... | collective-permute-start | bytes 196616 | tf_op jit(solution)/shard_map/ppermute | solution.py:217
  18.3 1.5 %collective-permute-start.7 = (f32[16,1024]{1,0:T(8,128)S(1)}, f32[16,1024]{1,0:T(8,128)S(1)}, u32[]{:S(2)}, u32[]{:S(2)}) collective-permute-start(f32[16,1024]{1,0:T(8,128)S(1)} %collective-permute-done.3.refs_2_), channel_id=1, source_target_pairs={{0,4},{1,5},{2,6},{3,7},{4,0},{5,1},{6,2},{7,3},{8,12},{9,13},{10,... | collective-permute-start | bytes 196616 | tf_op jit(solution)/shard_map/ppermute | solution.py:217
  19.7 1.3 %collective-permute-start.6 = (f32[16,1024]{1,0:T(8,128)S(1)}, f32[16,1024]{1,0:T(8,128)S(1)}, u32[]{:S(2)}, u32[]{:S(2)}) collective-permute-start(f32[16,1024]{1,0:T(8,128)S(1)} %collective-permute-done.2.refs_1_), channel_id=1, source_target_pairs={{0,4},{1,5},{2,6},{3,7},{4,0},{5,1},{6,2},{7,3},{8,12},{9,13},{10,... | collective-permute-start | bytes 196616 | tf_op jit(solution)/shard_map/ppermute | solution.py:217

commit v9 on v8

--- a/solution.py
+++ b/solution.py
@@ -233,7 +233,7 @@
     own = jnp.concatenate([vectors, cross(vectors, first)], axis=0)
     own, q2 = lax.optimization_barrier((own, q2))
     pieces = {0: own}
-    for bits in (core + y, core + 1, core + y + 1):
+    for bits in (core + y, 1, core + y + 1):
         pieces[bits] = cross(own, bits)
     for bits in tuple(pieces):
         pieces[bits ^ core] = cross(pieces[bits], core)

time: 28.6 us -> 28.7 us (level)
  waiting for transfers between devices: 5.35 us -> 5.98 us
  starting transfers between devices: 9.99 us -> 9.42 us
    ppermute x11, waiting for transfers between devices: 5.35 us -> 5.98 us  [swap(): return lax.ppermute(x, axis, [(i, i ^ bit) for i in range(size)])]
    ppermute x11, starting transfers between devices: 9.99 us -> 9.42 us  [swap(): return lax.ppermute(x, axis, [(i, i ^ bit) for i in range(size)])]
  transfers between devices with their start and end apart: 11 -> 11, of which waited for: 4 -> 6; matrix products, arithmetic and copies ran while one was open for 0% -> 0% of each run, Pallas kernels for 20% -> 20%
where the time goes in v9:
time: 28.7 us; the launch traced here: 28.5 us
  Pallas kernels  13.1 us (46%)
  starting transfers between devices  9.42 us (33%)
  waiting for transfers between devices  5.98 us (21%)
    ppermute x11, starting transfers between devices, swap(): return lax.ppermute(x, axis, [(i, i ^ bit) for i in range(size)])  9.42 us
    pallas_call x1, Pallas kernels, body_small(): pl.pallas_call(lambda *refs: scores_kernel(*refs, width=width, rows=rows)...  7.51 us
    ppermute x11, waiting for transfers between devices, swap(): return lax.ppermute(x, axis, [(i, i ^ bit) for i in range(size)])  5.98 us
    pallas_call x1, Pallas kernels, example_vectors(): pl.pallas_call(vectors_kernel, in_specs=[pl.BlockSpec(memory_space=pltpu....  5.6 us
  transfers between devices with their start and end apart: 11, of which 6 were waited for; matrix products, arithmetic and copies ran while one was open for 0% of the time, Pallas kernels for 20%

profile of v9, /device:TPU:0, one launch (start us, length us, event | category | flops | bytes accessed | tf_op | source)
XLA Modules:
  0.0 28.5 jit_solution(12792166651687113269)
XLA Ops:
  0.0 0.0 copy-start
  0.0 2.4 %collective-permute-start.1 = (bf16[512,256]{1,0:T(8,128)(2,1)}, bf16[512,256]{1,0:T(8,128)(2,1)S(1)}, u32[]{:S(2)}, u32[]{:S(2)}) collective-permute-start(bf16[512,256]{1,0:T(8,128)(2,1)} %refs_8_.1), channel_id=1, source_target_pairs={{0,12},{1,13},{2,14},{3,15},{4,8},{5,9},{6,10},{7,11},{8,4},{9,5},... | collective-permute-start | bytes 786440 | tf_op jit(solution)/shard_map/ppermute | solution.py:217
  2.4 5.6 %shard_map.64 = f32[8,1024]{1,0:T(8,128)S(1)} custom-call(s32[1,9]{1,0:T(1,128)} %lengths.1, bf16[256,14336]{1,0:T(8,128)(2,1)} %hidden.1, bf16[256,4096]{1,0:T(8,128)(2,1)} %out_grad.1, bf16[32,14336]{1,0:T(8,128)(2,1)} %proj_in.1, bf16[32,4096]{1,0:T(8,128)(2,1)} %proj_out.1), custom_call_target="tpu_custom_call" | custom-call | flops 301989888 | bytes 10616832 | tf_op jit(solution)/shard_map/pallas_call | solution.py:94
  8.0 2.9 %collective-permute-start = (f32[8,1024]{1,0:T(8,128)S(1)}, f32[8,1024]{1,0:T(8,128)S(1)}, u32[]{:S(2)}, u32[]{:S(2)}) collective-permute-start(f32[8,1024]{1,0:T(8,128)S(1)} %shard_map.64), channel_id=1, source_target_pairs={{0,6},{1,7},{2,4},{3,5},{4,2},{5,3},{6,0},{7,1},{8,14},{9,15},{10,... | collective-permute-start | bytes 98312 | tf_op jit(solution)/shard_map/ppermute | solution.py:217
  11.0 0.0 copy-done
  11.0 0.0 collective-permute-start.9
  11.0 1.6 %collective-permute-done = f32[8,1024]{1,0:T(8,128)S(1)} collective-permute-done((f32[8,1024]{1,0:T(8,128)S(1)}, f32[8,1024]{1,0:T(8,128)S(1)}, u32[]{:S(2)}, u32[]{:S(2)}) %collective-permute-start) | collective-permute-done | bytes 32800 | tf_op jit(solution)/shard_map/ppermute | solution.py:217
  12.6 0.0 collective-permute-done.1.refs_11_
  12.6 0.5 %collective-permute-start.10 = (bf16[512,256]{1,0:T(8,128)(2,1)S(1)}, bf16[512,256]{1,0:T(8,128)(2,1)S(1)}, u32[]{:S(2)}, u32[]{:S(2)}) collective-permute-start(bf16[512,256]{1,0:T(8,128)(2,1)S(1)} %collective-permute-done.1.refs_11_), channel_id=1, source_target_pairs={{0,4},{4,0},{8,12},{12,8},{1,5},{5,1},{9,13},{13,9},{2,6},{6,2},{1... | collective-permute-start | bytes 786440 | tf_op jit(solution)/shard_map/ppermute | solution.py:217
  13.1 1.3 %collective-permute-start.4 = (f32[16,1024]{1,0:T(8,128)S(1)}, f32[16,1024]{1,0:T(8,128)S(1)}, u32[]{:S(2)}, u32[]{:S(2)}) collective-permute-start(f32[16,1024]{1,0:T(8,128)S(1)} %pad_maximum_fusion.refs_0_), channel_id=1, source_target_pairs={{0,13},{1,12},{2,15},{3,14},{4,9},{5,8},{6,11},{7,10},{8,5},{9,4},... | collective-permute-start | bytes 196616 | tf_op jit(solution)/shard_map/ppermute | solution.py:217
  14.4 0.6 %collective-permute-start.3 = (f32[16,1024]{1,0:T(8,128)S(1)}, f32[16,1024]{1,0:T(8,128)S(1)}, u32[]{:S(2)}, u32[]{:S(2)}) collective-permute-start(f32[16,1024]{1,0:T(8,128)S(1)} %pad_maximum_fusion.refs_0_), channel_id=1, source_target_pairs={{0,1},{1,0},{2,3},{3,2},{4,5},{5,4},{6,7},{7,6},{8,9},{9,8},{10,11... | collective-permute-start | bytes 196616 | tf_op jit(solution)/shard_map/ppermute | solution.py:217
  15.0 1.1 %collective-permute-start.2 = (f32[16,1024]{1,0:T(8,128)S(1)}, f32[16,1024]{1,0:T(8,128)S(1)}, u32[]{:S(2)}, u32[]{:S(2)}) collective-permute-start(f32[16,1024]{1,0:T(8,128)S(1)} %pad_maximum_fusion.refs_0_), channel_id=1, source_target_pairs={{0,12},{1,13},{2,14},{3,15},{4,8},{5,9},{6,10},{7,11},{8,4},{9,5},... | collective-permute-start | bytes 196616 | tf_op jit(solution)/shard_map/ppermute | solution.py:217
  16.0 0.0 collective-permute-done.9.refs_9_
  16.0 0.3 %collective-permute-start.5 = (f32[16,1024]{1,0:T(8,128)S(1)}, f32[16,1024]{1,0:T(8,128)S(1)}, u32[]{:S(2)}, u32[]{:S(2)}) collective-permute-start(f32[16,1024]{1,0:T(8,128)S(1)} %pad_maximum_fusion.refs_0_), channel_id=1, source_target_pairs={{0,4},{1,5},{2,6},{3,7},{4,0},{5,1},{6,2},{7,3},{8,12},{9,13},{10,... | collective-permute-start | bytes 196616 | tf_op jit(solution)/shard_map/ppermute | solution.py:217
  16.4 1.8 %collective-permute-done.4.refs_3_ = f32[16,1024]{1,0:T(8,128)S(1)} collective-permute-done((f32[16,1024]{1,0:T(8,128)S(1)}, f32[16,1024]{1,0:T(8,128)S(1)}, u32[]{:S(2)}, u32[]{:S(2)}) %collective-permute-start.4) | collective-permute-done | bytes 65568 | tf_op jit(solution)/shard_map/ppermute | solution.py:217
  18.1 0.2 collective-permute-start.8
  18.3 0.5 %collective-permute-done.3.refs_2_ = f32[16,1024]{1,0:T(8,128)S(1)} collective-permute-done((f32[16,1024]{1,0:T(8,128)S(1)}, f32[16,1024]{1,0:T(8,128)S(1)}, u32[]{:S(2)}, u32[]{:S(2)}) %collective-permute-start.3) | collective-permute-done | bytes 65568 | tf_op jit(solution)/shard_map/ppermute | solution.py:217
  18.8 0.0 collective-permute-start.7
  18.8 1.0 %collective-permute-done.2.refs_1_ = f32[16,1024]{1,0:T(8,128)S(1)} collective-permute-done((f32[16,1024]{1,0:T(8,128)S(1)}, f32[16,1024]{1,0:T(8,128)S(1)}, u32[]{:S(2)}, u32[]{:S(2)}) %collective-permute-start.2) | collective-permute-done | bytes 65568 | tf_op jit(solution)/shard_map/ppermute | solution.py:217
  19.8 0.1 collective-permute-start.6
  19.9 0.0 collective-permute-done.5.refs_4_
  19.9 0.0 collective-permute-done.8.refs_7_
  19.9 0.1 collective-permute-done.7.refs_6_
  20.0 1.0 %collective-permute-done.6.refs_5_ = f32[16,1024]{1,0:T(8,128)S(1)} collective-permute-done((f32[16,1024]{1,0:T(8,128)S(1)}, f32[16,1024]{1,0:T(8,128)S(1)}, u32[]{:S(2)}, u32[]{:S(2)}) %collective-permute-start.6) | collective-permute-done | bytes 65568 | tf_op jit(solution)/shard_map/ppermute | solution.py:217
  21.0 0.0 collective-permute-done.10.refs_10_
  21.0 7.5 %shard_map.65 = f32[32,512]{1,0:T(8,128)} custom-call(f32[16,1024]{1,0:T(8,128)S(1)} %pad_maximum_fusion.refs_0_, f32[16,1024]{1,0:T(8,128)S(1)} %collective-permute-done.2.refs_1_, f32[16,1024]{1,0:T(8,128)S(1)} %collective-permute-done.3.refs_2_, f32[16,1024]{1,0:T(8,128)S(1)} %collective-permute-done.4.refs_3_, ...), custom_call_target="tpu_custom_call" | custom-call | tf_op jit(solution)/shard_map/pallas_call | solution.py:244
  (1 shorter events, 0.0 us)
Async XLA Ops:
  0.0 11.0 %copy-start = (bf16[512,256]{1,0:T(8,128)(2,1)S(1)}, bf16[512,256]{1,0:T(8,128)(2,1)}, u32[]{:S(2)}) copy-start(bf16[512,256]{1,0:T(8,128)(2,1)} %refs_8_.1) | copy-start | bytes 786436
  0.0 12.6 %collective-permute-start.1 = (bf16[512,256]{1,0:T(8,128)(2,1)}, bf16[512,256]{1,0:T(8,128)(2,1)S(1)}, u32[]{:S(2)}, u32[]{:S(2)}) collective-permute-start(bf16[512,256]{1,0:T(8,128)(2,1)} %refs_8_.1), channel_id=1, source_target_pairs={{0,12},{1,13},{2,14},{3,15},{4,8},{5,9},{6,10},{7,11},{8,4},{9,5},... | collective-permute-start | bytes 786440 | tf_op jit(solution)/shard_map/ppermute | solution.py:217
  8.0 4.5 %collective-permute-start = (f32[8,1024]{1,0:T(8,128)S(1)}, f32[8,1024]{1,0:T(8,128)S(1)}, u32[]{:S(2)}, u32[]{:S(2)}) collective-permute-start(f32[8,1024]{1,0:T(8,128)S(1)} %shard_map.64), channel_id=1, source_target_pairs={{0,6},{1,7},{2,4},{3,5},{4,2},{5,3},{6,0},{7,1},{8,14},{9,15},{10,... | collective-permute-start | bytes 98312 | tf_op jit(solution)/shard_map/ppermute | solution.py:217
  11.0 5.1 %collective-permute-start.9 = (bf16[512,256]{1,0:T(8,128)(2,1)S(1)}, bf16[512,256]{1,0:T(8,128)(2,1)S(1)}, u32[]{:S(2)}, u32[]{:S(2)}) collective-permute-start(bf16[512,256]{1,0:T(8,128)(2,1)S(1)} %copy-done), channel_id=1, source_target_pairs={{0,4},{4,0},{8,12},{12,8},{1,5},{5,1},{9,13},{13,9},{2,6},{6,2},{1... | collective-permute-start | bytes 786440 | tf_op jit(solution)/shard_map/ppermute | solution.py:217
  12.6 8.5 %collective-permute-start.10 = (bf16[512,256]{1,0:T(8,128)(2,1)S(1)}, bf16[512,256]{1,0:T(8,128)(2,1)S(1)}, u32[]{:S(2)}, u32[]{:S(2)}) collective-permute-start(bf16[512,256]{1,0:T(8,128)(2,1)S(1)} %collective-permute-done.1.refs_11_), channel_id=1, source_target_pairs={{0,4},{4,0},{8,12},{12,8},{1,5},{5,1},{9,13},{13,9},{2,6},{6,2},{1... | collective-permute-start | bytes 786440 | tf_op jit(solution)/shard_map/ppermute | solution.py:217
  13.1 5.0 %collective-permute-start.4 = (f32[16,1024]{1,0:T(8,128)S(1)}, f32[16,1024]{1,0:T(8,128)S(1)}, u32[]{:S(2)}, u32[]{:S(2)}) collective-permute-start(f32[16,1024]{1,0:T(8,128)S(1)} %pad_maximum_fusion.refs_0_), channel_id=1, source_target_pairs={{0,13},{1,12},{2,15},{3,14},{4,9},{5,8},{6,11},{7,10},{8,5},{9,4},... | collective-permute-start | bytes 196616 | tf_op jit(solution)/shard_map/ppermute | solution.py:217
  14.4 4.4 %collective-permute-start.3 = (f32[16,1024]{1,0:T(8,128)S(1)}, f32[16,1024]{1,0:T(8,128)S(1)}, u32[]{:S(2)}, u32[]{:S(2)}) collective-permute-start(f32[16,1024]{1,0:T(8,128)S(1)} %pad_maximum_fusion.refs_0_), channel_id=1, source_target_pairs={{0,1},{1,0},{2,3},{3,2},{4,5},{5,4},{6,7},{7,6},{8,9},{9,8},{10,11... | collective-permute-start | bytes 196616 | tf_op jit(solution)/shard_map/ppermute | solution.py:217
  15.0 4.8 %collective-permute-start.2 = (f32[16,1024]{1,0:T(8,128)S(1)}, f32[16,1024]{1,0:T(8,128)S(1)}, u32[]{:S(2)}, u32[]{:S(2)}) collective-permute-start(f32[16,1024]{1,0:T(8,128)S(1)} %pad_maximum_fusion.refs_0_), channel_id=1, source_target_pairs={{0,12},{1,13},{2,14},{3,15},{4,8},{5,9},{6,10},{7,11},{8,4},{9,5},... | collective-permute-start | bytes 196616 | tf_op jit(solution)/shard_map/ppermute | solution.py:217
  16.0 3.9 %collective-permute-start.5 = (f32[16,1024]{1,0:T(8,128)S(1)}, f32[16,1024]{1,0:T(8,128)S(1)}, u32[]{:S(2)}, u32[]{:S(2)}) collective-permute-start(f32[16,1024]{1,0:T(8,128)S(1)} %pad_maximum_fusion.refs_0_), channel_id=1, source_target_pairs={{0,4},{1,5},{2,6},{3,7},{4,0},{5,1},{6,2},{7,3},{8,12},{9,13},{10,... | collective-permute-start | bytes 196616 | tf_op jit(solution)/shard_map/ppermute | solution.py:217
  18.1 1.8 %collective-permute-start.8 = (f32[16,1024]{1,0:T(8,128)S(1)}, f32[16,1024]{1,0:T(8,128)S(1)}, u32[]{:S(2)}, u32[]{:S(2)}) collective-permute-start(f32[16,1024]{1,0:T(8,128)S(1)} %collective-permute-done.4.refs_3_), channel_id=1, source_target_pairs={{0,4},{1,5},{2,6},{3,7},{4,0},{5,1},{6,2},{7,3},{8,12},{9,13},{10,... | collective-permute-start | bytes 196616 | tf_op jit(solution)/shard_map/ppermute | solution.py:217
  18.8 1.3 %collective-permute-start.7 = (f32[16,1024]{1,0:T(8,128)S(1)}, f32[16,1024]{1,0:T(8,128)S(1)}, u32[]{:S(2)}, u32[]{:S(2)}) collective-permute-start(f32[16,1024]{1,0:T(8,128)S(1)} %collective-permute-done.3.refs_2_), channel_id=1, source_target_pairs={{0,4},{1,5},{2,6},{3,7},{4,0},{5,1},{6,2},{7,3},{8,12},{9,13},{10,... | collective-permute-start | bytes 196616 | tf_op jit(solution)/shard_map/ppermute | solution.py:217
  19.8 1.3 %collective-permute-start.6 = (f32[16,1024]{1,0:T(8,128)S(1)}, f32[16,1024]{1,0:T(8,128)S(1)}, u32[]{:S(2)}, u32[]{:S(2)}) collective-permute-start(f32[16,1024]{1,0:T(8,128)S(1)} %collective-permute-done.2.refs_1_), channel_id=1, source_target_pairs={{0,4},{1,5},{2,6},{3,7},{4,0},{5,1},{6,2},{7,3},{8,12},{9,13},{10,... | collective-permute-start | bytes 196616 | tf_op jit(solution)/shard_map/ppermute | solution.py:217
